TPU v7x, 32 devices: a whole 2x2x4 slice. The times are simulated.
32 devices in a mesh: gx: 8 (over y, x, core), gy: 4 (over z).
Axes of the slice: x: 2, y: 2, z: 4, core: 2. Of those that a mesh axis runs over, the one named last changes fastest.
Arguments:
- node_values: bfloat16 [24, 12, 128, 256], P('gx', 'gy'), may hold values from -6 to 6
- fit_ops: bfloat16 [8, 4, 8, 320, 300], P('gx', 'gy'), may hold values from -0.0034179688 to 0.0034179688
- node_xyz: float32 [8, 4, 8, 3, 300], P('gx', 'gy'), may hold values from -6 to 6
- patch_nodes: int32 [8, 4, 8, 300], P('gx', 'gy'), may hold values from 0 to 3199, as said below
- patch_valid: int32 [8, 4, 8], P('gx', 'gy'), may hold values from 160 to 300
- patch_cell: int32 [8, 4, 8, 3], P('gx', 'gy'), may hold values from 0 to 11, as said below
- patch_radius: float32 [8, 4, 8], P('gx', 'gy'), may hold values from 3 to 6
- cell_scale: float32 [96, 48, 8], P('gx', 'gy'), may hold values from 0.5 to 2
Outputs:
- velocity: bfloat16 [96, 48, 8, 256], P('gx', 'gy')
Inputs may be any that keep to these rules, and one draw needn't show every extreme that they name: `patch_nodes`: an entry (a * 5 + b) * 128 + n names node n of subregion (a, b) among the 5 by 5 subregions around the patch's tile, whose own subregions are a, b = 1 to 3; a and b differ by at most one from the subregion 1 + (3 c0) // 12, 1 + (3 c1) // 12 that holds the patch's centre cell, and the subregion never lies outside the grid along the second horizontal dimension. `patch_cell`: the first entry is below 12, the second below 12, the third at most 4.
All inputs are finite; a program needn't handle non-finite values.
Results may differ from a plain program's by a relative error of at most 0.0085.
Values may be sent and summed in bfloat16 or wider, within the bound.
No kernel may reach another device: no remote copies, remote signals or barrier semaphores. Data moves between devices by JAX's collectives and lax.ppermute only.
A program may use at most 64 MiB of HBM per device.

v0:
```python
import jax
import jax.numpy as jnp
from jax import lax
from jax.experimental import pallas as pl
from jax.experimental.pallas import tpu as pltpu
from jax.sharding import PartitionSpec as P

REACH = 4
SPAN = 2 * REACH + 1
LAYERS = 4
NEAR = 3
EXPONENTS = (
    (0, 0, 0),
    (1, 0, 0),
    (0, 1, 0),
    (0, 0, 1),
    (2, 0, 0),
    (1, 1, 0),
    (1, 0, 1),
    (0, 2, 0),
    (0, 1, 1),
    (0, 0, 2),
    (3, 0, 0),
    (2, 1, 0),
    (2, 0, 1),
    (1, 2, 0),
    (1, 1, 1),
    (1, 0, 2),
    (0, 3, 0),
    (0, 2, 1),
    (0, 1, 2),
    (0, 0, 3),
)
DISTANCES = sorted({a * a + b * b for a in range(REACH + 1) for b in range(REACH + 1)})
VMEM = pl.BlockSpec(memory_space=pltpu.VMEM)
SMEM = pl.BlockSpec(memory_space=pltpu.SMEM)


def up(value, multiple):
    return -(-value // multiple) * multiple


def swap(size, first, wrap):
    pairs = []
    for i in range(first, size, 2):
        j = i + 1
        if j == size:
            if not wrap:
                continue
            j = 0
        pairs += [(i, j), (j, i)]
    return pairs


def design_kernel(nodes, unknowns, cells_ref, radius_ref, xyz_ref, scale_ref, design_ref, wide_ref, pos, ax, by, bc, bm, bl):
    patches = design_ref.shape[0]
    lanes = design_ref.shape[2]
    depth = bl.shape[1]
    tile = (depth, lanes)
    pos[:, :, 0:nodes] = xyz_ref[...]
    lane = lax.broadcasted_iota(jnp.int32, (1, lanes), 1)
    is_node = lane < nodes
    used = lane < unknowns
    power = []
    for axis in range(3):
        rows = []
        for degree in range(1, 4):
            hit = lane < 0
            for index, triple in enumerate(EXPONENTS):
                if triple[axis] == degree:
                    hit = hit | (lane == nodes + index)
            rows.append(hit)
        power.append(rows)

    def raised(value, axis):
        one, two, three = power[axis]
        square = value * value
        out = jnp.where(one, value, 1.0)
        out = jnp.where(two, square, out)
        return jnp.where(three, square * value, out)

    across = (lax.broadcasted_iota(jnp.int32, (16, lanes), 0) - REACH).astype(jnp.float32)
    layer = lax.broadcasted_iota(jnp.int32, tile, 0)

    def patch(p, carry):
        inverse = 1.0 / jnp.full((1, lanes), radius_ref[0, p], jnp.float32)
        deep = (layer - cells_ref[p, 2]).astype(jnp.float32) - 1.5
        x = jnp.where(is_node, pos[0, pl.ds(p, 1), :], 0.0)
        y = jnp.where(is_node, pos[1, pl.ds(p, 1), :], 0.0)
        z = jnp.where(is_node, pos[2, pl.ds(p, 1), :], 0.0)
        dx = (across - x) * inverse
        dy = (across - y) * inverse
        dz = (deep - z) * inverse
        ax[...] = jnp.where(is_node, dx * dx, raised(dx, 0))
        by[...] = jnp.where(is_node, dy * dy, raised(dy, 1))
        cz = jnp.where(is_node, dz * dz, raised(dz, 2))
        for ey in range(SPAN):
            row = by[ey : ey + 1, :]
            bc[ey] = row + cz
            bm[ey] = (row * cz)[:, lanes - 128 :]
        inside = jnp.abs(deep[:, :128]) < 2.0
        near = inverse[:, :128]
        for index, flat in enumerate(DISTANCES):
            rho = jnp.sqrt(float(flat) + deep[:, :128] * deep[:, :128]) * near
            left = jnp.maximum(1.0 - rho, 0.0)
            left = left * left
            bl[index] = jnp.where(inside, left * left * (4.0 * rho + 1.0), 0.0)
        repeats = lanes // 128

        def one(spot):
            ex, ey = divmod(spot, SPAN)
            row = ax[ex : ex + 1, :]
            part = row + bc[ey]
            part = part * part * lax.rsqrt(jnp.maximum(part, 1e-30))
            last = row[:, lanes - 128 :] * bm[ey]
            low = (ex - REACH) ** 2 + (ey - REACH) ** 2
            blend = bl[DISTANCES.index(low)]
            pieces = [part[:, c * 128 : c * 128 + 128] for c in range(repeats)]
            pieces[-1] = jnp.where(is_node[:, lanes - 128 :], pieces[-1], last)
            pieces = [piece * blend for piece in pieces]
            pieces[-1] = jnp.where(used[:, lanes - 128 :], pieces[-1], 0.0)
            return jnp.concatenate(pieces, 1)

        for spot in range(0, SPAN * SPAN, 2):
            first = one(spot)
            second = one(spot + 1) if spot + 1 < SPAN * SPAN else jnp.zeros_like(first)
            pair = jnp.concatenate([first, second], 0).astype(jnp.bfloat16)
            design_ref[p, spot * depth : (spot + 2) * depth, :] = pair
        return carry

    lax.fori_loop(0, patches, patch, 0)
    for i in range(scale_ref.shape[0]):
        columns = scale_ref[i]
        for j in range(scale_ref.shape[2]):
            wide_ref[i, j] = jnp.broadcast_to(columns[:, j : j + 1], wide_ref.shape[2:])


def select_kernel(sides, subregion, tile, cells_ref, valid_ref, nodes_ref, fit_ref, out_ref, hot):
    patches, slots = nodes_ref.shape
    lane = lax.broadcasted_iota(jnp.int32, (1, slots), 1)
    node = lax.broadcasted_iota(jnp.int32, (subregion, slots), 0)
    for p in range(patches):
        index = nodes_ref[p : p + 1, :]
        where = lax.div(index, jnp.int32(subregion))
        inner = index - where * subregion
        a = jnp.zeros_like(where)
        for t in range(1, sides[0] + 2):
            a = a + jnp.where(where >= t * (sides[1] + 2), 1, 0)
        b = where - a * (sides[1] + 2)
        home_x = (cells_ref[p, 0] * sides[0]) // tile[0]
        home_y = (cells_ref[p, 1] * sides[1]) // tile[1]
        local = (a - home_x) * NEAR + (b - home_y)
        local = jnp.where(lane < valid_ref[0, p], local, -1)
        for s in range(NEAR * NEAR):
            row = jnp.where(local == s, inner, -1)
            hot[s * subregion : (s + 1) * subregion, :] = jnp.where(node == row, 1.0, 0.0).astype(jnp.bfloat16)
        out_ref[p] = lax.dot_general(
            fit_ref[p], hot[...], (((1,), (1,)), ((), ())), preferred_element_type=jnp.float32
        ).astype(jnp.bfloat16)


def blend_kernel(
    tile, cells_ref, turn_ref, own_ref, a_ref, b_ref, c_ref, d_ref, e_ref, f_ref, select_ref, design_ref,
    inner_ref, xa_ref, xb_ref, ca_ref, cb_ref, za_ref, zb_ref, near, acc,
):
    sx, sy, subregion, fields = own_ref.shape
    patches, unknowns, _ = select_ref.shape
    cx, cy = tile
    depth = acc.shape[2]
    rows = SPAN * SPAN * depth
    odd_x, odd_y = turn_ref[0], turn_ref[1]
    xa = (1 - odd_x) * (sx + 1)
    xb = odd_x * (sx + 1)
    ya = (1 - odd_y) * (sy + 1)
    yb = odd_y * (sy + 1)
    near[1 : sx + 1, 1 : sy + 1] = own_ref[...]
    near[xa, 1 : sy + 1] = a_ref[...]
    near[xb, 1 : sy + 1] = b_ref[...]
    near[1 : sx + 1, ya] = c_ref[...]
    near[1 : sx + 1, yb] = d_ref[...]
    near[xa, ya] = e_ref[0]
    near[xa, yb] = e_ref[1]
    near[xb, ya] = f_ref[0]
    near[xb, yb] = f_ref[1]
    acc[...] = jnp.zeros_like(acc)
    for p in range(patches):
        first, second = cells_ref[p, 0], cells_ref[p, 1]
        home_x = (first * sx) // cx
        home_y = (second * sy) // cy
        window = jnp.concatenate(
            [near[home_x + r, pl.ds(home_y, NEAR)].reshape(NEAR * subregion, fields) for r in range(NEAR)], 0
        )
        coeffs = jnp.dot(select_ref[p], window, preferred_element_type=jnp.float32).astype(jnp.bfloat16)
        values = jnp.dot(design_ref[p, :rows, :unknowns], coeffs, preferred_element_type=jnp.float32)
        values = values.reshape(SPAN, SPAN, depth, fields)
        for ex in range(SPAN):
            spot = (first + ex, pl.ds(second, SPAN))
            acc[spot] = acc[spot] + values[ex]
    ra = (1 - odd_x) * (cx + REACH)
    rb = odd_x * (cx + REACH)
    sa = (1 - odd_y) * (cy + REACH)
    sb = odd_y * (cy + REACH)
    rim, in_x, in_y = REACH, pl.ds(REACH, cx), pl.ds(REACH, cy)
    for ref, r in ((ca_ref, ra), (cb_ref, rb)):
        for index, s in ((0, sa), (1, sb)):
            ref[index] = acc[pl.ds(r, rim), pl.ds(s, rim)].astype(ref.dtype)
    for ref, r in ((xa_ref, ra), (xb_ref, rb)):
        ref[...] = acc[pl.ds(r, rim), in_y].astype(ref.dtype)
    for ref, s in ((za_ref, sa), (zb_ref, sb)):
        ref[...] = acc[in_x, pl.ds(s, rim)]
    inner_ref[...] = acc[in_x, in_y]


def relay_kernel(turn_ref, za_ref, zb_ref, ca_ref, cb_ref, outa_ref, outb_ref):
    odd = turn_ref[0]
    last = za_ref.shape[0] - REACH
    at = ((1 - odd) * last, odd * last)
    for index, (z_ref, out_ref) in enumerate(((za_ref, outa_ref), (zb_ref, outb_ref))):
        out_ref[...] = z_ref[...].astype(out_ref.dtype)
        for c_ref, r in ((ca_ref, at[0]), (cb_ref, at[1])):
            rows = pl.ds(r, REACH)
            out_ref[rows] = (z_ref[rows] + c_ref[index].astype(jnp.float32)).astype(out_ref.dtype)


def finish_kernel(turn_ref, inner_ref, wide_ref, xa_ref, xb_ref, za_ref, zb_ref, out_ref, acc):
    cx, cy, depth, fields = inner_ref.shape
    odd_x, odd_y = turn_ref[0], turn_ref[1]
    acc[...] = inner_ref[...]
    for ref, r in ((xa_ref, (1 - odd_x) * (cx - REACH)), (xb_ref, odd_x * (cx - REACH))):
        rows = pl.ds(r, REACH)
        acc[rows] = acc[rows] + ref[...].astype(jnp.float32)
    for ref, s in ((za_ref, (1 - odd_y) * (cy - REACH)), (zb_ref, odd_y * (cy - REACH))):
        rows = pl.ds(s, REACH)
        acc[:, rows] = acc[:, rows] + ref[...].astype(jnp.float32)
    for f in range(0, fields, 128):
        out_ref[:, :, :, f : f + 128] = (acc[:, :, :, f : f + 128] * wide_ref[...]).astype(out_ref.dtype)


def params(megabytes):
    return pltpu.CompilerParams(vmem_limit_bytes=megabytes * 2**20)


def local(node_values, fit_ops, node_xyz, patch_nodes, patch_valid, patch_cell, patch_radius, cell_scale):
    sx, sy, subregion, fields = node_values.shape
    patches, unknowns, slots = fit_ops.shape[2:]
    cx, cy, depth = cell_scale.shape
    across, along = lax.axis_size("gx"), lax.axis_size("gy")
    kind = node_values.dtype
    full = jnp.float32
    shape = jax.ShapeDtypeStruct
    lanes = up(unknowns, 128)
    rows = up(SPAN * SPAN, 2) * depth

    def send(block, axis, first):
        size = across if axis == "gx" else along
        return lax.ppermute(block, axis, swap(size, first, axis == "gx"))

    odd_x = lax.axis_index("gx") % 2
    odd_y = lax.axis_index("gy") % 2
    turn = jnp.stack([odd_x, odd_y]).astype(jnp.int32)
    cells = patch_cell[0, 0]

    far_x, far_y = (1 - odd_x) * (sx - 1), (1 - odd_y) * (sy - 1)
    back_x, back_y = odd_x * (sx - 1), odd_y * (sy - 1)
    column = lambda j: lax.dynamic_index_in_dim(node_values, j, 1, keepdims=False)
    line = lambda i: lax.dynamic_index_in_dim(node_values, i, 0, keepdims=False)
    from_ya = send(column(far_y), "gy", 0)
    from_yb = send(column(back_y), "gy", 1)
    from_xb = send(line(back_x), "gx", 1)
    from_xa = send(line(far_x), "gx", 0)
    pick = lambda block, i: lax.dynamic_index_in_dim(block, i, 0, keepdims=False)
    corner_b = send(jnp.stack([pick(from_ya, back_x), pick(from_yb, back_x)]), "gx", 1)
    corner_a = send(jnp.stack([pick(from_ya, far_x), pick(from_yb, far_x)]), "gx", 0)

    design, wide = pl.pallas_call(
        lambda *refs: design_kernel(slots, unknowns, *refs),
        out_shape=(shape((patches, rows, lanes), kind), shape((cx, cy, depth, 128), full)),
        in_specs=[SMEM, SMEM, VMEM, VMEM],
        out_specs=(VMEM, VMEM),
        scratch_shapes=[
            pltpu.VMEM((3, patches, lanes), full),
            pltpu.VMEM((16, lanes), full),
            pltpu.VMEM((16, lanes), full),
            pltpu.VMEM((SPAN, depth, lanes), full),
            pltpu.VMEM((SPAN, depth, 128), full),
            pltpu.VMEM((len(DISTANCES), depth, 128), full),
        ],
        compiler_params=params(16),
        cost_estimate=pl.CostEstimate(flops=40_000_000, bytes_accessed=6_000_000, transcendentals=2_000_000),
        name="design",
    )(cells, patch_radius[0], node_xyz[0, 0].transpose(1, 0, 2), cell_scale.transpose(0, 2, 1))

    select = pl.pallas_call(
        lambda *refs: select_kernel((sx, sy), subregion, (cx, cy), *refs),
        out_shape=shape((patches, unknowns, NEAR * NEAR * subregion), kind),
        in_specs=[SMEM, SMEM, VMEM, VMEM],
        out_specs=VMEM,
        scratch_shapes=[pltpu.VMEM((NEAR * NEAR * subregion, slots), kind)],
        compiler_params=params(20),
        cost_estimate=pl.CostEstimate(flops=1_800_000_000, bytes_accessed=8_000_000, transcendentals=0),
        name="select",
    )(cells, patch_valid[0], patch_nodes[0, 0], fit_ops[0, 0])

    block = lambda *dims, kind=kind: shape(dims + (depth, fields), kind)
    inner, xa, xb, ca, cb, za, zb = pl.pallas_call(
        lambda *refs: blend_kernel((cx, cy), *refs),
        out_shape=(
            block(cx, cy, kind=full),
            block(REACH, cy),
            block(REACH, cy),
            block(2, REACH, REACH),
            block(2, REACH, REACH),
            block(cx, REACH, kind=full),
            block(cx, REACH, kind=full),
        ),
        in_specs=[SMEM, SMEM] + [VMEM] * 9,
        out_specs=(VMEM,) * 7,
        scratch_shapes=[
            pltpu.VMEM((sx + 2, sy + 2, subregion, fields), kind),
            pltpu.VMEM((cx + 2 * REACH, cy + 2 * REACH, depth, fields), full),
        ],
        compiler_params=params(32),
        cost_estimate=pl.CostEstimate(flops=2_500_000_000, bytes_accessed=20_000_000, transcendentals=0),
        name="blend",
    )(cells, turn, node_values, from_xa, from_xb, from_ya, from_yb, corner_a, corner_b, select, design)

    got_cb = send(cb, "gx", 1)
    got_ca = send(ca, "gx", 0)
    got_xb = send(xb, "gx", 1)
    got_xa = send(xa, "gx", 0)
    za, zb = pl.pallas_call(
        relay_kernel,
        out_shape=(block(cx, REACH), block(cx, REACH)),
        in_specs=[SMEM] + [VMEM] * 4,
        out_specs=(VMEM, VMEM),
        compiler_params=params(8),
        cost_estimate=pl.CostEstimate(flops=400_000, bytes_accessed=1_500_000, transcendentals=0),
        name="relay",
    )(turn, za, zb, got_ca, got_cb)
    got_za = send(za, "gy", 0)
    got_zb = send(zb, "gy", 1)
    return pl.pallas_call(
        finish_kernel,
        out_shape=block(cx, cy),
        in_specs=[SMEM] + [VMEM] * 6,
        out_specs=VMEM,
        scratch_shapes=[pltpu.VMEM((cx, cy, depth, fields), full)],
        compiler_params=params(12),
        cost_estimate=pl.CostEstimate(flops=2_000_000, bytes_accessed=4_000_000, transcendentals=0),
        name="finish",
    )(turn, inner, wide, got_xa, got_xb, got_za, got_zb)


def solution(mesh):
    placed = (
        P("gx", "gy", None, None),
        P("gx", "gy", None, None, None),
        P("gx", "gy", None, None, None),
        P("gx", "gy", None, None),
        P("gx", "gy", None),
        P("gx", "gy", None, None),
        P("gx", "gy", None),
        P("gx", "gy", None),
    )
    return jax.shard_map(
        local, mesh=mesh, in_specs=placed, out_specs=P("gx", "gy", None, None), check_vma=False
    )
```

profile of v0, /device:TPU:8, one launch (start us, length us, event | category | flops | bytes accessed | tf_op | source)
XLA Modules:
  0.0 48.9 jit_solution(7176869956999934166)
XLA Ops:
  0.0 1.0 %dynamic-slice_bitcast_fusion = (bf16[3,128,256]{2,1,0:T(8,128)(2,1)S(1)}, bf16[3,128,256]{2,1,0:T(8,128)(2,1)S(1)}) fusion(bf16[3,3,128,256]{3,2,1,0:T(8,128)(2,1)} %refs_2_.1, s32[]{:T(128)S(6)} %select_n.35, s32[]{:T(128)S(6)} %select_n.34), kind=kLoop, calls=%fused_computation | loop fusion | bytes 786440 | tf_op jit(solution)/shard_map/jit(dynamic_index_in_dim)/squeeze | solution.py:265
  1.1 3.5 %collective-permute-start.3 = (bf16[3,128,256]{2,1,0:T(8,128)(2,1)S(1)}, bf16[3,128,256]{2,1,0:T(8,128)(2,1)S(1)}, u32[]{:S(2)}, u32[]{:S(2)}) collective-permute-start(bf16[3,128,256]{2,1,0:T(8,128)(2,1)S(1)} %get-tuple-element.27), channel_id=1, source_target_pairs={{1,2},{2,1},{5,6},{6,5},{9,10},{10,9},{13,14},{14,13},{17,18},{18,... | collective-permute-start | bytes 589832 | tf_op jit(solution)/shard_map/ppermute | solution.py:256
  4.5 0.1 collective-permute-start.2
  4.6 1.7 %dynamic-slice_bitcast_fusion.2 = (bf16[3,128,256]{2,1,0:T(8,128)(2,1)}, bf16[3,128,256]{2,1,0:T(8,128)(2,1)S(1)}) fusion(bf16[3,3,128,256]{3,2,1,0:T(8,128)(2,1)} %refs_2_.1, s32[]{:T(128)S(6)} %select_n.33, s32[]{:T(128)S(6)} %select_n.32), kind=kLoop, calls=%fused_computation.2 | loop fusion | bytes 786440 | tf_op jit(solution)/shard_map/jit(dynamic_index_in_dim)/squeeze | solution.py:266
  6.4 1.6 %collective-permute-start.1 = (bf16[3,128,256]{2,1,0:T(8,128)(2,1)}, bf16[3,128,256]{2,1,0:T(8,128)(2,1)S(1)}, u32[]{:S(2)}, u32[]{:S(2)}) collective-permute-start(bf16[3,128,256]{2,1,0:T(8,128)(2,1)} %get-tuple-element.29), channel_id=1, source_target_pairs={{4,8},{8,4},{12,16},{16,12},{20,24},{24,20},{28,0},{0,28},{5,9},{9... | collective-permute-start | bytes 589832 | tf_op jit(solution)/shard_map/ppermute | solution.py:256
  8.0 0.8 %copy.13 = s32[1,1,8,3]{3,2,1,0:T(8,128)S(1)} copy(s32[1,1,8,3]{2,1,3,0:T(1,128)} %param.13) | data formatting | bytes 192 | tf_op jit(solution)/shard_map/squeeze | solution.py:261
  8.7 3.1 %copy.9 = bf16[1,1,8,320,300]{4,3,2,1,0:T(8,128)(2,1)S(1)} copy(bf16[1,1,8,320,300]{3,2,4,1,0:T(8,128)(2,1)} %param.9) | data formatting | bytes 3072000 | tf_op args[1]
  12.0 0.6 %collective-permute-start.4 = (bf16[2,128,256]{2,1,0:T(8,128)(2,1)S(1)}, bf16[2,128,256]{2,1,0:T(8,128)(2,1)S(1)}, u32[]{:S(2)}, u32[]{:S(2)}) collective-permute-start(bf16[2,128,256]{2,1,0:T(8,128)(2,1)S(1)} %pad_maximum_fusion), channel_id=1, source_target_pairs={{0,4},{4,0},{8,12},{12,8},{16,20},{20,16},{24,28},{28,24},{1,5},{5... | collective-permute-start | bytes 393224 | tf_op jit(solution)/shard_map/ppermute | solution.py:256
  12.6 1.2 %collective-permute-start.5 = (bf16[2,128,256]{2,1,0:T(8,128)(2,1)S(1)}, bf16[2,128,256]{2,1,0:T(8,128)(2,1)S(1)}, u32[]{:S(2)}, u32[]{:S(2)}) collective-permute-start(bf16[2,128,256]{2,1,0:T(8,128)(2,1)S(1)} %pad_maximum_fusion.1), channel_id=1, source_target_pairs={{4,8},{8,4},{12,16},{16,12},{20,24},{24,20},{28,0},{0,28},{5,9},{9... | collective-permute-start | bytes 393224 | tf_op jit(solution)/shard_map/ppermute | solution.py:256
  13.7 0.0 copy-start.5
  13.7 4.4 %select.5.refs_9_ = bf16[8,320,1152]{2,1,0:T(8,128)(2,1)S(1)} custom-call(s32[8,3]{1,0:T(8,128)S(1)} %bitcast.20, s32[1,8]{1,0:T(1,128)S(1)} %bitcast.24, s32[8,300]{1,0:T(8,128)S(1)} %bitcast.23, bf16[8,320,300]{2,1,0:T(8,128)(2,1)S(1)} %bitcast.19), custom_call_target="tpu_custom_call" | custom-call | flops 1800000000 | bytes 8000000 | tf_op jit(solution)/shard_map/select/pallas_call | solution.py:293
  18.2 3.5 %design.1 = (bf16[8,656,384]{2,1,0:T(8,128)(2,1)S(1)}, f32[12,12,8,128]{3,2,1,0:T(8,128)S(1)}) custom-call(s32[8,3]{1,0:T(8,128)S(1)} %bitcast.21, f32[1,8]{1,0:T(1,128)S(1)} %bitcast.27, f32[3,8,300]{2,1,0:T(8,128)S(1)} %bitcast.26, f32[12,8,12]{2,1,0:T(8,128)S(1)} %bitcast.25), custom_call_target="tpu_custom_call" | custom-call | flops 40000000 | bytes 6000000 | tf_op jit(solution)/shard_map/design/pallas_call | solution.py:275
  21.7 0.1 pad_add_fusion.refs_1_.turn_ref
  21.8 8.1 %blend.1 = (f32[12,12,8,256]{3,2,1,0:T(8,128)S(1)}, bf16[4,12,8,256]{3,2,1,0:T(8,128)(2,1)S(1)}, bf16[4,12,8,256]{3,2,1,0:T(8,128)(2,1)S(1)}, bf16[2,4,4,8,256]{...) custom-call(s32[8,3]{1,0:T(8,128)S(1)} %bitcast.22, ...), custom_call_target="tpu_custom_call" | custom-call | flops 2500000000 | bytes 20000000 | tf_op jit(solution)/shard_map/blend/pallas_call | solution.py:305
  29.9 0.1 collective-permute-start.8
  29.9 1.6 %collective-permute-start.9 = (bf16[2,4,4,8,256]{4,3,2,1,0:T(8,128)(2,1)S(1)}, bf16[2,4,4,8,256]{4,3,2,1,0:T(8,128)(2,1)S(1)}, u32[]{:S(2)}, u32[]{:S(2)}) collective-permute-start(bf16[2,4,4,8,256]{4,3,2,1,0:T(8,128)(2,1)S(1)} %get-tuple-element.24), channel_id=1, source_target_pairs={{4,8},{8,4},{12,16},{16,12},{20,24},{24,20},{28,0},{0,28},{5,9},{9... | collective-permute-start | bytes 393224 | tf_op jit(solution)/shard_map/ppermute | solution.py:256
  31.5 1.5 %collective-permute-start.7 = (bf16[4,12,8,256]{3,2,1,0:T(8,128)(2,1)S(1)}, bf16[4,12,8,256]{3,2,1,0:T(8,128)(2,1)S(1)}, u32[]{:S(2)}, u32[]{:S(2)}) collective-permute-start(bf16[4,12,8,256]{3,2,1,0:T(8,128)(2,1)S(1)} %get-tuple-element.20), channel_id=1, source_target_pairs={{4,8},{8,4},{12,16},{16,12},{20,24},{24,20},{28,0},{0,28},{5,9},{9... | collective-permute-start | bytes 589832 | tf_op jit(solution)/shard_map/ppermute | solution.py:256
  33.1 3.1 %collective-permute-done.9.cb_ref = bf16[2,4,4,8,256]{4,3,2,1,0:T(8,128)(2,1)S(1)} collective-permute-done((bf16[2,4,4,8,256]{4,3,2,1,0:T(8,128)(2,1)S(1)}, bf16[2,4,4,8,256]{4,3,2,1,0:T(8,128)(2,1)S(1)}, u32[]{:S(2)}, u32[]{:S(2)}) %collective-permute-start.9) | collective-permute-done | bytes 131104 | tf_op jit(solution)/shard_map/ppermute | solution.py:256
  36.1 0.6 %relay.1 = (bf16[12,4,8,256]{3,2,1,0:T(8,128)(2,1)S(1)}, bf16[12,4,8,256]{3,2,1,0:T(8,128)(2,1)S(1)}) custom-call(s32[2]{0:T(128)S(1)} %pad_add_fusion.refs_1_.turn_ref, f32[12,4,8,256]{3,2,1,0:T(8,128)S(1)} %get-tuple-element.21.za_ref, f32[12,4,8,256]{3,2,1,0:T(8,128)S(1)} %get-tuple-element.22.zb_ref, ...), custom_call_target="tpu_custom_call" | custom-call | flops 400000 | bytes 1500000 | tf_op jit(solution)/shard_map/relay/pallas_call | solution.py:331
  36.8 1.9 %collective-permute-start.10 = (bf16[12,4,8,256]{3,2,1,0:T(8,128)(2,1)S(1)}, bf16[12,4,8,256]{3,2,1,0:T(8,128)(2,1)S(1)}, u32[]{:S(2)}, u32[]{:S(2)}) collective-permute-start(bf16[12,4,8,256]{3,2,1,0:T(8,128)(2,1)S(1)} %get-tuple-element.25), channel_id=1, source_target_pairs={{0,1},{1,0},{2,3},{3,2},{4,5},{5,4},{6,7},{7,6},{8,9},{9,8},{10,11... | collective-permute-start | bytes 589832 | tf_op jit(solution)/shard_map/ppermute | solution.py:256
  38.7 2.4 %collective-permute-start.11 = (bf16[12,4,8,256]{3,2,1,0:T(8,128)(2,1)S(1)}, bf16[12,4,8,256]{3,2,1,0:T(8,128)(2,1)S(1)}, u32[]{:S(2)}, u32[]{:S(2)}) collective-permute-start(bf16[12,4,8,256]{3,2,1,0:T(8,128)(2,1)S(1)} %get-tuple-element.26), channel_id=1, source_target_pairs={{1,2},{2,1},{5,6},{6,5},{9,10},{10,9},{13,14},{14,13},{17,18},{18,... | collective-permute-start | bytes 589832 | tf_op jit(solution)/shard_map/ppermute | solution.py:256
  41.1 2.8 %collective-permute-done.10.za_ref = bf16[12,4,8,256]{3,2,1,0:T(8,128)(2,1)S(1)} collective-permute-done((bf16[12,4,8,256]{3,2,1,0:T(8,128)(2,1)S(1)}, bf16[12,4,8,256]{3,2,1,0:T(8,128)(2,1)S(1)}, u32[]{:S(2)}, u32[]{:S(2)}) %collective-permute-start.10) | collective-permute-done | bytes 196640 | tf_op jit(solution)/shard_map/ppermute | solution.py:256
  43.9 3.3 %collective-permute-done.11.zb_ref = bf16[12,4,8,256]{3,2,1,0:T(8,128)(2,1)S(1)} collective-permute-done((bf16[12,4,8,256]{3,2,1,0:T(8,128)(2,1)S(1)}, bf16[12,4,8,256]{3,2,1,0:T(8,128)(2,1)S(1)}, u32[]{:S(2)}, u32[]{:S(2)}) %collective-permute-start.11) | collective-permute-done | bytes 196640 | tf_op jit(solution)/shard_map/ppermute | solution.py:256
  47.2 1.7 %finish.1 = bf16[12,12,8,256]{3,2,1,0:T(8,128)(2,1)} custom-call(s32[2]{0:T(128)S(1)} %pad_add_fusion.refs_1_.turn_ref, f32[12,12,8,256]{3,2,1,0:T(8,128)S(1)} %get-tuple-element.17.inner_ref, f32[12,12,8,128]{3,2,1,0:T(8,128)S(1)} %get-tuple-element.18.wide_ref, bf16[4,12,8,256]{3,2,1,0:T(8,128)(2,1)S(1)} %collective-permute-done.6.xa_ref, ...), custom_call_target="tpu_custom_call" | custom-call | flops 2000000 | bytes 4000000 | tf_op jit(solution)/shard_map/finish/pallas_call | solution.py:342
  (26 shorter events, 0.1 us)
Async XLA Ops:
  1.1 10.8 %collective-permute-start.3 = (bf16[3,128,256]{2,1,0:T(8,128)(2,1)S(1)}, bf16[3,128,256]{2,1,0:T(8,128)(2,1)S(1)}, u32[]{:S(2)}, u32[]{:S(2)}) collective-permute-start(bf16[3,128,256]{2,1,0:T(8,128)(2,1)S(1)} %get-tuple-element.27), channel_id=1, source_target_pairs={{1,2},{2,1},{5,6},{6,5},{9,10},{10,9},{13,14},{14,13},{17,18},{18,... | collective-permute-start | bytes 589832 | tf_op jit(solution)/shard_map/ppermute | solution.py:256
  4.5 7.4 %collective-permute-start.2 = (bf16[3,128,256]{2,1,0:T(8,128)(2,1)S(1)}, bf16[3,128,256]{2,1,0:T(8,128)(2,1)S(1)}, u32[]{:S(2)}, u32[]{:S(2)}) collective-permute-start(bf16[3,128,256]{2,1,0:T(8,128)(2,1)S(1)} %get-tuple-element.28), channel_id=1, source_target_pairs={{0,1},{1,0},{2,3},{3,2},{4,5},{5,4},{6,7},{7,6},{8,9},{9,8},{10,11... | collective-permute-start | bytes 589832 | tf_op jit(solution)/shard_map/ppermute | solution.py:256
  6.4 15.4 %collective-permute-start.1 = (bf16[3,128,256]{2,1,0:T(8,128)(2,1)}, bf16[3,128,256]{2,1,0:T(8,128)(2,1)S(1)}, u32[]{:S(2)}, u32[]{:S(2)}) collective-permute-start(bf16[3,128,256]{2,1,0:T(8,128)(2,1)} %get-tuple-element.29), channel_id=1, source_target_pairs={{4,8},{8,4},{12,16},{16,12},{20,24},{24,20},{28,0},{0,28},{5,9},{9... | collective-permute-start | bytes 589832 | tf_op jit(solution)/shard_map/ppermute | solution.py:256
  8.0 13.8 %collective-permute-start = (bf16[3,128,256]{2,1,0:T(8,128)(2,1)S(1)}, bf16[3,128,256]{2,1,0:T(8,128)(2,1)S(1)}, u32[]{:S(2)}, u32[]{:S(2)}) collective-permute-start(bf16[3,128,256]{2,1,0:T(8,128)(2,1)S(1)} %get-tuple-element.30), channel_id=1, source_target_pairs={{0,4},{4,0},{8,12},{12,8},{16,20},{20,16},{24,28},{28,24},{1,5},{5... | collective-permute-start | bytes 589832 | tf_op jit(solution)/shard_map/ppermute | solution.py:256
  8.7 5.0 %copy-start.1 = (s32[1,1,8,300]{3,2,1,0:T(8,128)S(1)}, s32[1,1,8,300]{3,2,1,0:T(8,128)}, u32[]{:S(2)}) copy-start(s32[1,1,8,300]{3,2,1,0:T(8,128)} %param.11) | copy-start | bytes 28804
  8.7 5.0 %copy-start.2 = (s32[1,1,8]{2,1,0:T(1,128)S(1)}, s32[1,1,8]{2,1,0:T(1,128)}, u32[]{:S(2)}) copy-start(s32[1,1,8]{2,1,0:T(1,128)} %param.12) | copy-start | bytes 100
  12.0 9.8 %collective-permute-start.4 = (bf16[2,128,256]{2,1,0:T(8,128)(2,1)S(1)}, bf16[2,128,256]{2,1,0:T(8,128)(2,1)S(1)}, u32[]{:S(2)}, u32[]{:S(2)}) collective-permute-start(bf16[2,128,256]{2,1,0:T(8,128)(2,1)S(1)} %pad_maximum_fusion), channel_id=1, source_target_pairs={{0,4},{4,0},{8,12},{12,8},{16,20},{20,16},{24,28},{28,24},{1,5},{5... | collective-permute-start | bytes 393224 | tf_op jit(solution)/shard_map/ppermute | solution.py:256
  12.6 9.2 %collective-permute-start.5 = (bf16[2,128,256]{2,1,0:T(8,128)(2,1)S(1)}, bf16[2,128,256]{2,1,0:T(8,128)(2,1)S(1)}, u32[]{:S(2)}, u32[]{:S(2)}) collective-permute-start(bf16[2,128,256]{2,1,0:T(8,128)(2,1)S(1)} %pad_maximum_fusion.1), channel_id=1, source_target_pairs={{4,8},{8,4},{12,16},{16,12},{20,24},{24,20},{28,0},{0,28},{5,9},{9... | collective-permute-start | bytes 393224 | tf_op jit(solution)/shard_map/ppermute | solution.py:256
  13.7 4.5 %copy-start.3 = (f32[12,12,8]{1,2,0:T(8,128)S(1)}, f32[12,12,8]{1,2,0:T(8,128)}, u32[]{:S(2)}) copy-start(f32[12,12,8]{1,2,0:T(8,128)} %param.15) | copy-start | bytes 13828
  13.7 4.5 %copy-start.4 = (f32[1,1,8,3,300]{4,2,3,1,0:T(8,128)S(1)}, f32[1,1,8,3,300]{4,2,3,1,0:T(8,128)}, u32[]{:S(2)}) copy-start(f32[1,1,8,3,300]{4,2,3,1,0:T(8,128)} %param.10) | copy-start | bytes 86404
  13.7 4.5 %copy-start.5 = (f32[1,1,8]{2,1,0:T(1,128)S(1)}, f32[1,1,8]{2,1,0:T(1,128)}, u32[]{:S(2)}) copy-start(f32[1,1,8]{2,1,0:T(1,128)} %param.14) | copy-start | bytes 100
  18.2 3.6 %copy-start = (bf16[3,3,128,256]{3,2,1,0:T(8,128)(2,1)S(1)}, bf16[3,3,128,256]{3,2,1,0:T(8,128)(2,1)}, u32[]{:S(2)}) copy-start(bf16[3,3,128,256]{3,2,1,0:T(8,128)(2,1)} %refs_2_.1) | copy-start | bytes 1769476
  29.9 3.2 %collective-permute-start.8 = (bf16[2,4,4,8,256]{4,3,2,1,0:T(8,128)(2,1)S(1)}, bf16[2,4,4,8,256]{4,3,2,1,0:T(8,128)(2,1)S(1)}, u32[]{:S(2)}, u32[]{:S(2)}) collective-permute-start(bf16[2,4,4,8,256]{4,3,2,1,0:T(8,128)(2,1)S(1)} %get-tuple-element.23), channel_id=1, source_target_pairs={{0,4},{4,0},{8,12},{12,8},{16,20},{20,16},{24,28},{28,24},{1,5},{5... | collective-permute-start | bytes 393224 | tf_op jit(solution)/shard_map/ppermute | solution.py:256
  29.9 6.2 %collective-permute-start.9 = (bf16[2,4,4,8,256]{4,3,2,1,0:T(8,128)(2,1)S(1)}, bf16[2,4,4,8,256]{4,3,2,1,0:T(8,128)(2,1)S(1)}, u32[]{:S(2)}, u32[]{:S(2)}) collective-permute-start(bf16[2,4,4,8,256]{4,3,2,1,0:T(8,128)(2,1)S(1)} %get-tuple-element.24), channel_id=1, source_target_pairs={{4,8},{8,4},{12,16},{16,12},{20,24},{24,20},{28,0},{0,28},{5,9},{9... | collective-permute-start | bytes 393224 | tf_op jit(solution)/shard_map/ppermute | solution.py:256
  31.5 9.5 %collective-permute-start.6 = (bf16[4,12,8,256]{3,2,1,0:T(8,128)(2,1)S(1)}, bf16[4,12,8,256]{3,2,1,0:T(8,128)(2,1)S(1)}, u32[]{:S(2)}, u32[]{:S(2)}) collective-permute-start(bf16[4,12,8,256]{3,2,1,0:T(8,128)(2,1)S(1)} %get-tuple-element.19), channel_id=1, source_target_pairs={{0,4},{4,0},{8,12},{12,8},{16,20},{20,16},{24,28},{28,24},{1,5},{5... | collective-permute-start | bytes 589832 | tf_op jit(solution)/shard_map/ppermute | solution.py:256
  31.5 9.5 %collective-permute-start.7 = (bf16[4,12,8,256]{3,2,1,0:T(8,128)(2,1)S(1)}, bf16[4,12,8,256]{3,2,1,0:T(8,128)(2,1)S(1)}, u32[]{:S(2)}, u32[]{:S(2)}) collective-permute-start(bf16[4,12,8,256]{3,2,1,0:T(8,128)(2,1)S(1)} %get-tuple-element.20), channel_id=1, source_target_pairs={{4,8},{8,4},{12,16},{16,12},{20,24},{24,20},{28,0},{0,28},{5,9},{9... | collective-permute-start | bytes 589832 | tf_op jit(solution)/shard_map/ppermute | solution.py:256
  36.8 7.1 %collective-permute-start.10 = (bf16[12,4,8,256]{3,2,1,0:T(8,128)(2,1)S(1)}, bf16[12,4,8,256]{3,2,1,0:T(8,128)(2,1)S(1)}, u32[]{:S(2)}, u32[]{:S(2)}) collective-permute-start(bf16[12,4,8,256]{3,2,1,0:T(8,128)(2,1)S(1)} %get-tuple-element.25), channel_id=1, source_target_pairs={{0,1},{1,0},{2,3},{3,2},{4,5},{5,4},{6,7},{7,6},{8,9},{9,8},{10,11... | collective-permute-start | bytes 589832 | tf_op jit(solution)/shard_map/ppermute | solution.py:256
  38.7 8.5 %collective-permute-start.11 = (bf16[12,4,8,256]{3,2,1,0:T(8,128)(2,1)S(1)}, bf16[12,4,8,256]{3,2,1,0:T(8,128)(2,1)S(1)}, u32[]{:S(2)}, u32[]{:S(2)}) collective-permute-start(bf16[12,4,8,256]{3,2,1,0:T(8,128)(2,1)S(1)} %get-tuple-element.26), channel_id=1, source_target_pairs={{1,2},{2,1},{5,6},{6,5},{9,10},{10,9},{13,14},{14,13},{17,18},{18,... | collective-permute-start | bytes 589832 | tf_op jit(solution)/shard_map/ppermute | solution.py:256
where the time goes:
time: 49.5 us; the launch traced here: 48.9 us
  Pallas kernels  18.3 us (37%)
  starting transfers between devices  14.4 us (29%)
  waiting for transfers between devices  9.2 us (19%)
  local copies, waits for them, and re-layouts  6.71 us (14%)
    ppermute x12, starting transfers between devices, send(): return lax.ppermute(block, axis, swap(size, first, axis == 'gx'))  14.4 us
    ppermute x12, waiting for transfers between devices, send(): return lax.ppermute(block, axis, swap(size, first, axis == 'gx'))  9.2 us
    pallas_call x1, Pallas kernels, local(): pl.pallas_call(lambda *refs: blend_kernel((cx, cy), *refs), out_shape=(bl...  8.06 us
    pallas_call x1, Pallas kernels, local(): pl.pallas_call(lambda *refs: select_kernel((sx, sy), subregion, (cx, cy),...  4.42 us
    pallas_call x1, Pallas kernels, local(): pl.pallas_call(lambda *refs: design_kernel(slots, unknowns, *refs), out_s...  3.45 us
    unnamed x13, local copies, waits for them, and re-layouts  3.14 us
    squeeze x1, local copies, waits for them, and re-layouts, local(): line = lambda i: lax.dynamic_index_in_dim(node_values, i, 0, keepdims=False)  1.73 us
    pallas_call x1, Pallas kernels, local(): pl.pallas_call(finish_kernel, out_shape=block(cx, cy), in_specs=[SMEM] +...  1.73 us
  transfers between devices with their start and end apart: 12, of which 3 were waited for; matrix products, arithmetic and copies ran while one was open for 12% of the time, Pallas kernels for 17%

commit v1 on v0

v1 whole, which is shorter than its diff:
```python
import jax
import jax.numpy as jnp
from jax import lax
from jax.experimental import pallas as pl
from jax.experimental.pallas import tpu as pltpu
from jax.sharding import PartitionSpec as P

REACH = 4
SPAN = 2 * REACH + 1
LAYERS = 4
NEAR = 3
EXPONENTS = (
    (0, 0, 0),
    (1, 0, 0),
    (0, 1, 0),
    (0, 0, 1),
    (2, 0, 0),
    (1, 1, 0),
    (1, 0, 1),
    (0, 2, 0),
    (0, 1, 1),
    (0, 0, 2),
    (3, 0, 0),
    (2, 1, 0),
    (2, 0, 1),
    (1, 2, 0),
    (1, 1, 1),
    (1, 0, 2),
    (0, 3, 0),
    (0, 2, 1),
    (0, 1, 2),
    (0, 0, 3),
)
DISTANCES = sorted({a * a + b * b for a in range(REACH + 1) for b in range(REACH + 1)})
SPOTS = [(ex, ey) for ex in range(SPAN) for ey in range(SPAN - 1)] + [(ex, SPAN - 1) for ex in range(SPAN)]
VMEM = pl.BlockSpec(memory_space=pltpu.VMEM)
SMEM = pl.BlockSpec(memory_space=pltpu.SMEM)


SMALL = pl.CostEstimate(flops=1000, bytes_accessed=1000, transcendentals=0)
LARGE = pl.CostEstimate(flops=4_000_000_000, bytes_accessed=40_000_000, transcendentals=0)


def up(value, multiple):
    return -(-value // multiple) * multiple


def parity():
    return lax.rem(lax.axis_index("gx"), 2), lax.rem(lax.axis_index("gy"), 2)


def swap(size, first, wrap):
    pairs = []
    for i in range(first, size, 2):
        j = i + 1
        if j == size:
            if not wrap:
                continue
            j = 0
        pairs += [(i, j), (j, i)]
    return pairs


def pack_kernel(count, nodes_ref, *refs):
    plain, sent, copied, sems = refs[:count], refs[count : count + 6], refs[count + 6 : -1], refs[-1]
    ya_ref, yb_ref, xa_ref, xb_ref, da_ref, db_ref = sent
    sx, sy = nodes_ref.shape[:2]
    odd_x, odd_y = parity()
    far_x, back_x = (1 - odd_x) * (sx - 1), odd_x * (sx - 1)
    far_y, back_y = (1 - odd_y) * (sy - 1), odd_y * (sy - 1)
    pairs = (
        (nodes_ref.at[back_x, back_y], db_ref),
        (nodes_ref.at[back_x, far_y], da_ref),
        (nodes_ref.at[:, far_y], ya_ref),
        (nodes_ref.at[:, back_y], yb_ref),
        (nodes_ref.at[back_x], xb_ref),
        (nodes_ref.at[far_x], xa_ref),
        *zip(plain, copied),
    )
    copies = [pltpu.make_async_copy(source, target, sems.at[index]) for index, (source, target) in enumerate(pairs)]
    for copy in copies:
        copy.start()
    for copy in copies:
        copy.wait()


def extend_kernel(ya_ref, yb_ref, own_ref, out_ref):
    odd_x, odd_y = parity()
    far_x = (1 - odd_x) * (ya_ref.shape[0] - 1)
    last = out_ref.shape[0] - 1
    out_ref[1:last] = own_ref[...]
    out_ref[(1 - odd_y) * last] = ya_ref[far_x]
    out_ref[odd_y * last] = yb_ref[far_x]


def prepare_kernel(
    sides, subregion, tile, radius_ref, xyz_ref, scale_ref, cells_ref, valid_ref, nodes_ref, far_ref,
    design_ref, wide_ref, hot_ref, fit_ref, near_ref, split, places, sem, *scratch,
):
    copy = pltpu.make_async_copy(far_ref, near_ref, sem)
    copy.start()
    design_kernel(nodes_ref.shape[1], near_ref.shape[2], radius_ref, xyz_ref, scale_ref, design_ref, wide_ref, *scratch)
    copy.wait()
    choose(sides, subregion, tile, cells_ref, valid_ref, nodes_ref, near_ref, hot_ref, fit_ref, split, places)


def design_kernel(nodes, unknowns, radius_ref, xyz_ref, scale_ref, design_ref, wide_ref, pos, ax, by, ax2, bc, bm, bl):
    patches = design_ref.shape[0]
    lanes = design_ref.shape[2]
    tile = (2 * LAYERS, lanes)
    pos[:, :, 0:nodes] = xyz_ref[...]
    lane = lax.broadcasted_iota(jnp.int32, (1, lanes), 1)
    is_node = lane < nodes
    used = lane < unknowns
    power = []
    for axis in range(3):
        rows = []
        for degree in range(1, 4):
            hit = lane < 0
            for index, triple in enumerate(EXPONENTS):
                if triple[axis] == degree:
                    hit = hit | (lane == nodes + index)
            rows.append(hit)
        power.append(rows)

    def raised(value, axis):
        one, two, three = power[axis]
        square = value * value
        out = jnp.where(one, value, jnp.where(used, 1.0, 0.0))
        out = jnp.where(two, square, out)
        return jnp.where(three, square * value, out)

    across = (lax.broadcasted_iota(jnp.int32, (16, lanes), 0) - REACH).astype(jnp.float32)
    layer = lax.broadcasted_iota(jnp.int32, tile, 0)
    upper = layer < LAYERS
    deep = jnp.where(upper, layer, layer - LAYERS).astype(jnp.float32) - 0.5 * (LAYERS - 1)
    tail = slice(lanes - 128, lanes)
    half = SPAN // 2

    def patch(p, carry):
        inverse = 1.0 / jnp.full((1, lanes), radius_ref[0, p], jnp.float32)
        x = jnp.where(is_node, pos[0, pl.ds(p, 1), :], 0.0)
        y = jnp.where(is_node, pos[1, pl.ds(p, 1), :], 0.0)
        z = jnp.where(is_node, pos[2, pl.ds(p, 1), :], 0.0)
        dx = (across - x) * inverse
        dy = (across - y) * inverse
        dz = (deep - z) * inverse
        ax[...] = jnp.where(is_node, dx * dx, raised(dx, 0))
        by[...] = jnp.where(is_node, dy * dy, raised(dy, 1))
        cz = jnp.where(is_node, dz * dz + 1e-30, raised(dz, 2))
        for i in range(half + 1):
            low, high = 2 * i, min(2 * i + 1, SPAN - 1)
            row = jnp.where(upper, by[low : low + 1, :], by[high : high + 1, :])
            bc[i] = row + cz
            bm[i] = row[:, tail] * cz[:, tail]
            ax2[i] = jnp.where(upper, ax[low : low + 1, :], ax[high : high + 1, :])
        for index, flat in enumerate(DISTANCES):
            rho = jnp.sqrt(float(flat) + deep[:, :128] * deep[:, :128]) * inverse[:, :128]
            left = jnp.maximum(1.0 - rho, 0.0)
            left = left * left
            bl[index] = left * left * (4.0 * rho + 1.0)

        def pair(spots):
            (ex, ey), (fx, fy) = spots[0], spots[-1]
            row = ax[ex : ex + 1, :] if ex == fx else ax2[ex // 2]
            part = row + bc[ey // 2]
            part = part * part * lax.rsqrt(part)
            last = row[:, tail] * bm[ey // 2]
            blend = [bl[DISTANCES.index((i - REACH) ** 2 + (j - REACH) ** 2)] for i, j in ((ex, ey), (fx, fy))]
            blend = blend[0] if (ex, ey) == (fx, fy) else jnp.where(upper[:, :128], blend[0], blend[1])
            if len(spots) == 1:
                blend = jnp.where(upper[:, :128], blend, 0.0)
            pieces = [part[:, c : c + 128] for c in range(0, lanes, 128)]
            pieces[-1] = jnp.where(is_node[:, tail], pieces[-1], last)
            return jnp.concatenate([piece * blend for piece in pieces], 1)

        for spot in range(0, len(SPOTS), 4):
            rows = [pair(SPOTS[q : q + 2]) if q < len(SPOTS) else jnp.zeros(tile, jnp.float32) for q in (spot, spot + 2)]
            design_ref[p, spot * LAYERS : (spot + 4) * LAYERS, :] = jnp.concatenate(rows, 0).astype(jnp.bfloat16)
        return carry

    lax.fori_loop(0, patches, patch, 0)
    for i in range(scale_ref.shape[0]):
        columns = scale_ref[i]
        for j in range(scale_ref.shape[2]):
            wide_ref[i, j] = jnp.broadcast_to(columns[:, j : j + 1], wide_ref.shape[2:])


def choose(sides, subregion, tile, cells_ref, valid_ref, nodes_ref, fit_ref, hot, fit, wide, places):
    patches, slots = nodes_ref.shape
    unknowns = fit.shape[1]
    padded = hot.shape[1]
    kind = fit.dtype
    lane = lax.broadcasted_iota(jnp.int32, (1, slots), 1)
    places[...] = jnp.full(places.shape, -1.0, jnp.float32)
    for c in range(0, unknowns, 128):
        width = min(128, unknowns - c)
        wide[c // 128, :, :width] = fit_ref[:, :, c : c + width].astype(jnp.float32).reshape(slots * patches, width)
    for p in range(patches):
        index = nodes_ref[p : p + 1, :]
        where = lax.div(index, jnp.int32(subregion))
        a = jnp.zeros_like(where)
        for t in range(1, sides[0] + 2):
            a = a + jnp.where(where >= t * (sides[1] + 2), 1, 0)
        b = where - a * (sides[1] + 2)
        home_x, home_y = home(sides, tile, cells_ref, p)
        local = (a - home_x) * NEAR + (b - home_y)
        local = jnp.where(lane < valid_ref[0, p], local, -1)
        places[0, p : p + 1, 0:slots] = (index - where * subregion).astype(jnp.float32)
        places[1, p : p + 1, 0:slots] = local.astype(jnp.float32)
    inner, local = places[0].T, places[1].T
    node = lax.broadcasted_iota(jnp.int32, (padded, subregion), 1).astype(jnp.float32).astype(kind)
    one, zero = jnp.ones((), kind), jnp.zeros((), kind)
    fit[:, :, slots:] = jnp.zeros((patches, unknowns, padded - slots), kind)
    for p in range(patches):
        column = jnp.broadcast_to(inner[:padded, p : p + 1], (padded, subregion)).astype(kind)
        one_hot = jnp.where(node == column, one, zero)
        column = jnp.broadcast_to(local[:padded, p : p + 1], (padded, subregion)).astype(kind)
        for s in range(NEAR * NEAR):
            hot[p, :, s * subregion : (s + 1) * subregion] = jnp.where(column == jnp.full((), s, kind), one_hot, zero)
        for c in range(0, unknowns, 128):
            width = min(128, unknowns - c)
            piece = wide[c // 128, pl.ds(p, slots, stride=patches), :]
            fit[p, c : c + width, 0:slots] = piece.T[:width].astype(kind)


def home(sides, tile, cells_ref, p):
    return (cells_ref[0, 0, p] * sides[0]) // tile[0], (cells_ref[1, 0, p] * sides[1]) // tile[1]


def sample_kernel(
    tile, cells_ref, own_ref, b_ref, c_ref, d_ref, e_ref, f_ref, hot_ref, out_ref, near,
):
    sx, sy, subregion, fields = own_ref.shape
    odd_x, odd_y = parity()
    xa = (1 - odd_x) * (sx + 1)
    xb = odd_x * (sx + 1)
    ya = (1 - odd_y) * (sy + 1)
    yb = odd_y * (sy + 1)
    near[1 : sx + 1, 1 : sy + 1] = own_ref[...]
    near[xb, 1 : sy + 1] = b_ref[...]
    near[1 : sx + 1, ya] = c_ref[...]
    near[1 : sx + 1, yb] = d_ref[...]
    near[xb, ya] = e_ref[...]
    near[xb, yb] = f_ref[...]
    near[xa] = jnp.zeros(near.shape[1:], near.dtype)
    for p in range(hot_ref.shape[0]):
        home_x, home_y = home((sx, sy), tile, cells_ref, p)
        window = jnp.concatenate(
            [near[home_x + r, pl.ds(home_y, NEAR)].reshape(NEAR * subregion, fields) for r in range(NEAR)], 0
        )
        out_ref[p] = jnp.dot(hot_ref[p], window, preferred_element_type=jnp.float32)


def blend_kernel(
    sides, tile, cells_ref, side_ref, sample_ref, hot_ref, fit_ref, design_ref,
    inner_ref, xa_ref, xb_ref, da_ref, db_ref, za_ref, zb_ref, chosen, coeffs, values, acc,
):
    sx, sy = sides
    subregion, fields = side_ref.shape[1:]
    patches, unknowns, _ = fit_ref.shape
    cx, cy = tile
    rows = len(SPOTS) * LAYERS
    odd_x, odd_y = parity()
    xa = (1 - odd_x) * (sx + 1)
    acc[...] = jnp.zeros_like(acc)
    for p in range(patches):
        home_x, home_y = home(sides, tile, cells_ref, p)
        row = xa - home_x
        here = (row >= 0) & (row < NEAR)
        spot = pl.multiple_of(jnp.where(here, row, 0) * (NEAR * subregion), NEAR * subregion)
        side = side_ref[pl.ds(home_y, NEAR)].reshape(NEAR * subregion, fields)
        side = side * jnp.where(here, 1.0, 0.0).astype(side.dtype)
        extra = jnp.dot(hot_ref[p, :, pl.ds(spot, NEAR * subregion)], side, preferred_element_type=jnp.float32)
        chosen[p] = (sample_ref[p] + extra).astype(chosen.dtype)
    for p in range(patches):
        coeffs[p] = jnp.dot(fit_ref[p], chosen[p], preferred_element_type=jnp.float32).astype(coeffs.dtype)

    def place(p):
        first, second, third = cells_ref[0, 0, p], cells_ref[1, 0, p], cells_ref[2, 0, p]
        for s, (ex, ey) in enumerate(SPOTS):
            for l in range(acc.shape[0]):
                spot = (l, first + ex, second + ey, pl.ds(third, LAYERS))
                acc[spot] = acc[spot] + values[p, s * LAYERS : (s + 1) * LAYERS, l * 128 : (l + 1) * 128]

    for p in range(patches):
        values[p] = jnp.dot(design_ref[p, :rows, :unknowns], coeffs[p], preferred_element_type=jnp.float32)
        if p:
            place(p - 1)
    place(patches - 1)

    ra = (1 - odd_x) * (cx + REACH)
    rb = odd_x * (cx + REACH)
    sa = (1 - odd_y) * (cy + REACH)
    sb = odd_y * (cy + REACH)
    rim, in_x, in_y = REACH, pl.ds(REACH, cx), pl.ds(REACH, cy)
    for l in range(acc.shape[0]):
        f = pl.ds(l * 128, 128)
        xa_ref[:, :, :, f] = acc[l, pl.ds(ra, rim)].astype(xa_ref.dtype)
        xb_ref[:, :, :, f] = acc[l, pl.ds(rb, rim), in_y].astype(xb_ref.dtype)
        for ref, s in ((da_ref, sa), (db_ref, sb)):
            ref[:, :, :, f] = acc[l, pl.ds(rb, rim), pl.ds(s, rim)].astype(ref.dtype)
        for ref, s in ((za_ref, sa), (zb_ref, sb)):
            ref[:, :, :, f] = acc[l, in_x, pl.ds(s, rim)]
        inner_ref[:, :, :, f] = acc[l, in_x, in_y]


def relay_kernel(za_ref, zb_ref, xa_ref, outa_ref, outb_ref):
    odd_x, odd_y = parity()
    cx = za_ref.shape[0]
    rows = pl.ds((1 - odd_x) * (cx - REACH), REACH)
    last = xa_ref.shape[1] - REACH
    for z_ref, out_ref, s in ((za_ref, outa_ref, (1 - odd_y) * last), (zb_ref, outb_ref, odd_y * last)):
        out_ref[...] = z_ref[...].astype(out_ref.dtype)
        got = xa_ref[:, pl.ds(s, REACH)].astype(jnp.float32)
        out_ref[rows] = (z_ref[rows] + got).astype(out_ref.dtype)


def gather_kernel(inner_ref, wide_ref, xa_ref, xb_ref, za_ref, zb_ref, out_ref):
    cx, cy, depth, fields = inner_ref.shape
    odd_x, odd_y = parity()
    far, back = pl.ds((1 - odd_x) * (cx - REACH), REACH), pl.ds(odd_x * (cx - REACH), REACH)
    for f in range(0, fields, 128):
        part = slice(f, f + 128)
        out_ref[:, :, :, part] = inner_ref[:, :, :, part] * wide_ref[...]
        got = xa_ref[:, REACH : REACH + cy, :, part].astype(jnp.float32)
        out_ref[far, :, :, part] = out_ref[far, :, :, part] + got * wide_ref[far]
        got = xb_ref[:, :, :, part].astype(jnp.float32)
        out_ref[back, :, :, part] = out_ref[back, :, :, part] + got * wide_ref[back]
        for z_ref, s in ((za_ref, (1 - odd_y) * (cy - REACH)), (zb_ref, odd_y * (cy - REACH))):
            spot = (slice(None), pl.ds(s, REACH))
            got = z_ref[:, :, :, part].astype(jnp.float32)
            out_ref[spot + (slice(None), part)] = out_ref[spot + (slice(None), part)] + got * wide_ref[spot]


def finish_kernel(base_ref, wide_ref, da_ref, db_ref, out_ref):
    cx, cy, depth, fields = base_ref.shape
    odd_x, odd_y = parity()
    back = pl.ds(odd_x * (cx - REACH), REACH)
    for f in range(0, fields, 128):
        part = slice(f, f + 128)
        out_ref[:, :, :, part] = base_ref[:, :, :, part].astype(out_ref.dtype)
        for d_ref, s in ((da_ref, (1 - odd_y) * (cy - REACH)), (db_ref, odd_y * (cy - REACH))):
            spot = (back, pl.ds(s, REACH))
            got = d_ref[:, :, :, part].astype(jnp.float32) * wide_ref[spot]
            out_ref[spot + (slice(None), part)] = (base_ref[spot + (slice(None), part)] + got).astype(out_ref.dtype)


def params(megabytes):
    return pltpu.CompilerParams(vmem_limit_bytes=megabytes * 2**20)


def local(node_values, fit_ops, node_xyz, patch_nodes, patch_valid, patch_cell, patch_radius, cell_scale):
    sx, sy, subregion, fields = node_values.shape
    patches, unknowns, slots = fit_ops.shape[2:]
    cx, cy, depth = cell_scale.shape
    across, along = lax.axis_size("gx"), lax.axis_size("gy")
    kind = node_values.dtype
    full = jnp.float32
    shape = jax.ShapeDtypeStruct
    lanes = up(unknowns, 128)
    rows = up(len(SPOTS), 4) * LAYERS
    halves = fields // 128

    pairs_x = [swap(across, first, True) for first in (0, 1)]
    pairs_y = [swap(along, first, False) for first in (0, 1)]

    def send_x(block, turn):
        return lax.ppermute(block, "gx", pairs_x[turn])

    def send_y(block, turn):
        return lax.ppermute(block, "gy", pairs_y[turn])

    def send_across(block, turn):
        both = [(a * along + c, b * along + d) for a, b in pairs_x[1] for c, d in pairs_y[turn]]
        return lax.ppermute(block, ("gx", "gy"), both)

    line = lambda *sides: shape(sides + (subregion, fields), kind)
    plain = (
        patch_cell.transpose(0, 3, 1, 2)[0],
        patch_valid[0],
        patch_nodes[0, 0],
        patch_radius[0],
        node_xyz[0, 0].transpose(1, 0, 2),
        cell_scale.transpose(0, 2, 1),
    )
    packed = pl.pallas_call(
        lambda *refs: pack_kernel(len(plain), *refs),
        out_shape=(line(sx), line(sx), line(sy), line(sy), line(), line()) + tuple(shape(x.shape, x.dtype) for x in plain),
        in_specs=[pl.BlockSpec(memory_space=pl.ANY)] * (1 + len(plain)),
        out_specs=(VMEM,) * (6 + len(plain)),
        scratch_shapes=[pltpu.SemaphoreType.DMA((6 + len(plain),))],
        compiler_params=params(4),
        cost_estimate=SMALL,
        name="pack",
    )(*[pltpu.with_memory_space_constraint(x, pltpu.HBM) for x in (node_values, *plain)])
    to_ya, to_yb, to_xa, to_xb, to_da, to_db, cells, valid, indices, radius, xyz, scale = packed
    from_ya = send_y(to_ya, 0)
    from_yb = send_y(to_yb, 1)
    from_xb = send_x(to_xb, 1)
    from_da = send_across(to_da, 0)
    from_db = send_across(to_db, 1)
    window = NEAR * NEAR * subregion
    padded = up(slots, 16)
    far = pltpu.with_memory_space_constraint(fit_ops[0, 0].transpose(2, 0, 1), pltpu.HBM)
    design, wide, hot, fit = pl.pallas_call(
        lambda *refs: prepare_kernel((sx, sy), subregion, (cx, cy), *refs),
        out_shape=(
            shape((patches, rows, lanes), kind),
            shape((cx, cy, depth, 128), full),
            shape((patches, padded, window), kind),
            shape((patches, unknowns, padded), kind),
        ),
        in_specs=[SMEM, VMEM, VMEM, SMEM, SMEM, VMEM, pl.BlockSpec(memory_space=pl.ANY)],
        out_specs=(VMEM,) * 4,
        scratch_shapes=[
            pltpu.VMEM(far.shape, kind),
            pltpu.VMEM((lanes // 128, slots * patches, 128), full),
            pltpu.VMEM((2, patches, up(padded, 128)), full),
            pltpu.SemaphoreType.DMA,
            pltpu.VMEM((3, patches, lanes), full),
            pltpu.VMEM((16, lanes), full),
            pltpu.VMEM((16, lanes), full),
            pltpu.VMEM((SPAN // 2 + 1, 2 * LAYERS, lanes), full),
            pltpu.VMEM((SPAN // 2 + 1, 2 * LAYERS, lanes), full),
            pltpu.VMEM((SPAN // 2 + 1, 2 * LAYERS, 128), full),
            pltpu.VMEM((len(DISTANCES), 2 * LAYERS, 128), full),
        ],
        compiler_params=params(24),
        cost_estimate=SMALL,
        name="prepare",
    )(radius, xyz, scale, cells, valid, indices, far)
    from_yb, from_ya, from_xb, from_db, from_da, hot = lax.optimization_barrier(
        (from_yb, from_ya, from_xb, from_db, from_da, hot)
    )
    to_xa = pl.pallas_call(
        extend_kernel,
        out_shape=line(sy + 2),
        in_specs=[VMEM] * 3,
        out_specs=VMEM,
        compiler_params=params(4),
        cost_estimate=SMALL,
        name="extend",
    )(from_ya, from_yb, to_xa)
    from_xa = send_x(to_xa, 0)
    samples = pl.pallas_call(
        lambda *refs: sample_kernel((cx, cy), *refs),
        out_shape=shape((patches, padded, fields), full),
        in_specs=[SMEM] + [VMEM] * 7,
        out_specs=VMEM,
        scratch_shapes=[pltpu.VMEM((sx + 2, sy + 2, subregion, fields), kind)],
        compiler_params=params(16),
        cost_estimate=LARGE,
        name="sample",
    )(cells, node_values, from_xb, from_ya, from_yb, from_da, from_db, hot)

    block = lambda *dims, kind=kind: shape(dims + (depth, fields), kind)
    inner, xa, xb, da, db, za, zb = pl.pallas_call(
        lambda *refs: blend_kernel((sx, sy), (cx, cy), *refs),
        out_shape=(
            block(cx, cy, kind=full),
            block(REACH, cy + 2 * REACH),
            block(REACH, cy),
            block(REACH, REACH),
            block(REACH, REACH),
            block(cx, REACH, kind=full),
            block(cx, REACH, kind=full),
        ),
        in_specs=[SMEM] + [VMEM] * 5,
        out_specs=(VMEM,) * 7,
        scratch_shapes=[
            pltpu.VMEM((patches, padded, fields), kind),
            pltpu.VMEM((patches, unknowns, fields), kind),
            pltpu.VMEM((patches, len(SPOTS) * LAYERS, fields), full),
            pltpu.VMEM((halves, cx + 2 * REACH, cy + 2 * REACH, depth, 128), full),
        ],
        compiler_params=params(32),
        cost_estimate=SMALL,
        name="blend",
    )(cells, from_xa, samples, hot, fit, design)

    got_xa = send_x(xa, 0)
    got_xb = send_x(xb, 1)
    got_db = send_across(db, 1)
    got_da = send_across(da, 0)
    za, zb = pl.pallas_call(
        relay_kernel,
        out_shape=(block(cx, REACH), block(cx, REACH)),
        in_specs=[VMEM] * 3,
        out_specs=(VMEM, VMEM),
        compiler_params=params(8),
        cost_estimate=SMALL,
        name="relay",
    )(za, zb, got_xa)
    got_za = send_y(za, 0)
    got_zb = send_y(zb, 1)
    base = pl.pallas_call(
        gather_kernel,
        out_shape=block(cx, cy, kind=full),
        in_specs=[VMEM] * 6,
        out_specs=VMEM,
        compiler_params=params(12),
        cost_estimate=LARGE,
        name="gather",
    )(inner, wide, got_xa, got_xb, got_za, got_zb)
    return pl.pallas_call(
        finish_kernel,
        out_shape=block(cx, cy),
        in_specs=[VMEM] * 4,
        out_specs=VMEM,
        compiler_params=params(12),
        cost_estimate=SMALL,
        name="finish",
    )(base, wide, got_da, got_db)


def solution(mesh):
    placed = (
        P("gx", "gy", None, None),
        P("gx", "gy", None, None, None),
        P("gx", "gy", None, None, None),
        P("gx", "gy", None, None),
        P("gx", "gy", None),
        P("gx", "gy", None, None),
        P("gx", "gy", None),
        P("gx", "gy", None),
    )
    return jax.shard_map(
        local, mesh=mesh, in_specs=placed, out_specs=P("gx", "gy", None, None), check_vma=False
    )
```

time: 49.5 us -> 38 us (0.77)
  local copies, waits for them, and re-layouts: 6.71 us -> 0.01 us
  Pallas kernels: 18.3 us -> 13.9 us
  starting transfers between devices: 14.4 us -> 17.1 us
  waiting for transfers between devices: 9.2 us -> 6.65 us
    pallas_call x4 -> x7, Pallas kernels: 17.7 us -> 13.8 us  [the longest x1 4.67 us: local(): pl.pallas_call(lambda *refs: prepare_kernel((sx, sy), subregion, (cx, cy)...]
    squeeze x3 -> x0, local copies, waits for them, and re-layouts: 3.53 us -> none  [the longest x1 1.73 us: local(): line = lambda i: lax.dynamic_index_in_dim(node_values, i, 0, keepdims=False)]
    unnamed x13 -> x2, local copies, waits for them, and re-layouts: 3.14 us -> 0.01 us
    ppermute x12, starting transfers between devices: 14.4 us -> 17.1 us  [the longest x4 8.29 us: send_y(): return lax.ppermute(block, 'gy', pairs_y[turn])]
    ppermute x12, waiting for transfers between devices: 9.2 us -> 6.65 us  [the longest x4 3.51 us: send_across(): return lax.ppermute(block, ('gx', 'gy'), both)]
    pallas_call x1, Pallas kernels: 0.62 us -> 0.07 us  [local(): pl.pallas_call(relay_kernel, out_shape=(block(cx, REACH), block(cx, REACH...]
  transfers between devices with their start and end apart: 12 -> 12, of which waited for: 3 -> 5; matrix products, arithmetic and copies ran while one was open for 12% -> 0% of each run, Pallas kernels for 17% -> 20%
where the time goes in v1:
time: 38 us; the launch traced here: 37.8 us
  starting transfers between devices  17.1 us (45%)
  Pallas kernels  13.9 us (37%)
  waiting for transfers between devices  6.65 us (18%)
    ppermute x4, starting transfers between devices, send_y(): return lax.ppermute(block, 'gy', pairs_y[turn])  8.29 us
    ppermute x4, starting transfers between devices, send_across(): return lax.ppermute(block, ('gx', 'gy'), both)  5.83 us
    pallas_call x1, Pallas kernels, local(): pl.pallas_call(lambda *refs: prepare_kernel((sx, sy), subregion, (cx, cy)...  4.67 us
    pallas_call x1, Pallas kernels, local(): pl.pallas_call(lambda *refs: blend_kernel((sx, sy), (cx, cy), *refs), out...  3.92 us
    ppermute x4, waiting for transfers between devices, send_across(): return lax.ppermute(block, ('gx', 'gy'), both)  3.51 us
    ppermute x4, starting transfers between devices, send_x(): return lax.ppermute(block, 'gx', pairs_x[turn])  2.98 us
    ppermute x4, waiting for transfers between devices, send_y(): return lax.ppermute(block, 'gy', pairs_y[turn])  2.57 us
    pallas_call x1, Pallas kernels, local(): pl.pallas_call(lambda *refs: sample_kernel((cx, cy), *refs), out_shape=sh...  2.46 us
  transfers between devices with their start and end apart: 12, of which 5 were waited for; matrix products, arithmetic and copies ran while one was open for 0% of the time, Pallas kernels for 20%

profile of v1, /device:TPU:8, one launch (start us, length us, event | category | flops | bytes accessed | tf_op | source)
XLA Modules:
  0.0 37.8 jit_solution(3609430131190710893)
XLA Ops:
  0.0 1.4 %pack.1 = (bf16[3,128,256]{2,1,0:T(8,128)(2,1)S(1)}, bf16[3,128,256]{2,1,0:T(8,128)(2,1)S(1)}, bf16[3,128,256]{2,1,0:T(8,128)(2,1)S(1)}, bf16[3,128,256]{2,1,0:T...) custom-call(bf16[3,3,128,256]{3,2,1,0:T(8,128)(2,1)} %refs_1_.1, ...), custom_call_target="tpu_custom_call" | custom-call | flops 1000 | bytes 1000 | tf_op jit(solution)/shard_map/pack/pallas_call | solution.py:387
  1.4 3.5 %collective-permute-start = (bf16[3,128,256]{2,1,0:T(8,128)(2,1)S(1)}, bf16[3,128,256]{2,1,0:T(8,128)(2,1)S(1)}, u32[]{:S(2)}, u32[]{:S(2)}) collective-permute-start(bf16[3,128,256]{2,1,0:T(8,128)(2,1)S(1)} %get-tuple-element.37), channel_id=1, source_target_pairs={{1,2},{2,1},{5,6},{6,5},{9,10},{10,9},{13,14},{14,13},{17,18},{18,... | collective-permute-start | bytes 589832 | tf_op jit(solution)/shard_map/ppermute | solution.py:372
  4.9 0.1 collective-permute-start.1
  5.0 1.7 %collective-permute-start.2 = (bf16[3,128,256]{2,1,0:T(8,128)(2,1)S(1)}, bf16[3,128,256]{2,1,0:T(8,128)(2,1)S(1)}, u32[]{:S(2)}, u32[]{:S(2)}) collective-permute-start(bf16[3,128,256]{2,1,0:T(8,128)(2,1)S(1)} %get-tuple-element.39), channel_id=1, source_target_pairs={{4,8},{8,4},{12,16},{16,12},{20,24},{24,20},{28,0},{0,28},{5,9},{9... | collective-permute-start | bytes 589832 | tf_op jit(solution)/shard_map/ppermute | solution.py:369
  6.7 2.8 %collective-permute-start.3 = (bf16[128,256]{1,0:T(8,128)(2,1)S(1)}, bf16[128,256]{1,0:T(8,128)(2,1)S(1)}, u32[]{:S(2)}, u32[]{:S(2)}) collective-permute-start(bf16[128,256]{1,0:T(8,128)(2,1)S(1)} %get-tuple-element.40), channel_id=1, source_target_pairs={{5,10},{6,9},{9,6},{10,5},{13,18},{14,17},{17,14},{18,13},{21,26},... | collective-permute-start | bytes 196616 | tf_op jit(solution)/shard_map/ppermute | solution.py:376
  9.5 0.3 collective-permute-start.4
  9.8 4.7 %prepare.1 = (bf16[8,336,384]{2,1,0:T(8,128)(2,1)S(1)}, f32[12,12,8,128]{3,2,1,0:T(8,128)S(1)}, bf16[8,304,1152]{2,1,0:T(8,128)(2,1)S(1)}, bf16[8,320,304]{2,1,0:T(8,128)(2,1)S(1)}) custom-call(f32[1,8]{1,0:T(1,128)S(1)} %get-tuple-element.42.refs_0_, f32[3,8,300]{2,1,0:T(8,128)S(1)} %get-tuple-element.43.refs_1_, ...), custom_call_target="tpu_custom_call" | custom-call | flops 1000 | bytes 1000 | tf_op jit(solution)/shard_map/prepare/pallas_call | solution.py:406
  14.5 0.8 %collective-permute-done.3.refs_6_ = bf16[128,256]{1,0:T(8,128)(2,1)S(1)} collective-permute-done((bf16[128,256]{1,0:T(8,128)(2,1)S(1)}, bf16[128,256]{1,0:T(8,128)(2,1)S(1)}, u32[]{:S(2)}, u32[]{:S(2)}) %collective-permute-start.3) | collective-permute-done | bytes 65568 | tf_op jit(solution)/shard_map/ppermute | solution.py:376
  15.3 0.8 %collective-permute-done.4.refs_5_ = bf16[128,256]{1,0:T(8,128)(2,1)S(1)} collective-permute-done((bf16[128,256]{1,0:T(8,128)(2,1)S(1)}, bf16[128,256]{1,0:T(8,128)(2,1)S(1)}, u32[]{:S(2)}, u32[]{:S(2)}) %collective-permute-start.4) | collective-permute-done | bytes 65568 | tf_op jit(solution)/shard_map/ppermute | solution.py:376
  16.2 0.1 collective-permute-start.5
  16.3 2.5 %sample.1.refs_2_ = f32[8,304,256]{2,1,0:T(8,128)S(1)} custom-call(s32[3,1,8]{2,1,0:T(1,128)S(1)} %get-tuple-element.36.refs_3_.refs_0_, bf16[3,3,128,256]{3,2,1,0:T(8,128)(2,1)S(1)} %copy-done, bf16[3,128,256]{2,1,0:T(8,128)(2,1)S(1)} %collective-permute-done.2.refs_2_, bf16[3,128,256]{2,1,0:T(8,128)(2,1)S(1)} %collective-permute-done.1.ya_ref.refs_3_, ...), custom_call_target="tpu_custom_call" | custom-call | flops 4000000000 | bytes 40000000 | tf_op jit(solution)/shard_map/sample/pallas_call | solution.py:446
  18.8 3.9 %blend.1 = (f32[12,12,8,256]{3,2,1,0:T(8,128)S(1)}, bf16[4,20,8,256]{3,2,1,0:T(8,128)(2,1)S(1)}, bf16[4,12,8,256]{3,2,1,0:T(8,128)(2,1)S(1)}, bf16[4,4,8,256]{3,...) custom-call(s32[3,1,8]{2,1,0:T(1,128)S(1)} %get-tuple-element.36.ref, ...), custom_call_target="tpu_custom_call" | custom-call | flops 1000 | bytes 1000 | tf_op jit(solution)/shard_map/blend/pallas_call | solution.py:458
  22.7 0.5 %collective-permute-start.6 = (bf16[4,20,8,256]{3,2,1,0:T(8,128)(2,1)S(1)}, bf16[4,20,8,256]{3,2,1,0:T(8,128)(2,1)S(1)}, u32[]{:S(2)}, u32[]{:S(2)}) collective-permute-start(bf16[4,20,8,256]{3,2,1,0:T(8,128)(2,1)S(1)} %get-tuple-element.59), channel_id=1, source_target_pairs={{0,4},{4,0},{8,12},{12,8},{16,20},{20,16},{24,28},{28,24},{1,5},{5... | collective-permute-start | bytes 983048 | tf_op jit(solution)/shard_map/ppermute | solution.py:369
  23.2 0.7 %collective-permute-start.7 = (bf16[4,12,8,256]{3,2,1,0:T(8,128)(2,1)S(1)}, bf16[4,12,8,256]{3,2,1,0:T(8,128)(2,1)S(1)}, u32[]{:S(2)}, u32[]{:S(2)}) collective-permute-start(bf16[4,12,8,256]{3,2,1,0:T(8,128)(2,1)S(1)} %get-tuple-element.60), channel_id=1, source_target_pairs={{4,8},{8,4},{12,16},{16,12},{20,24},{24,20},{28,0},{0,28},{5,9},{9... | collective-permute-start | bytes 589832 | tf_op jit(solution)/shard_map/ppermute | solution.py:369
  23.9 0.6 %collective-permute-done.6.xa_ref = bf16[4,20,8,256]{3,2,1,0:T(8,128)(2,1)S(1)} collective-permute-done((bf16[4,20,8,256]{3,2,1,0:T(8,128)(2,1)S(1)}, bf16[4,20,8,256]{3,2,1,0:T(8,128)(2,1)S(1)}, u32[]{:S(2)}, u32[]{:S(2)}) %collective-permute-start.6) | collective-permute-done | bytes 327712 | tf_op jit(solution)/shard_map/ppermute | solution.py:369
  24.5 0.1 relay.1
  24.5 1.3 %collective-permute-start.8 = (bf16[12,4,8,256]{3,2,1,0:T(8,128)(2,1)S(1)}, bf16[12,4,8,256]{3,2,1,0:T(8,128)(2,1)S(1)}, u32[]{:S(2)}, u32[]{:S(2)}) collective-permute-start(bf16[12,4,8,256]{3,2,1,0:T(8,128)(2,1)S(1)} %get-tuple-element.63), channel_id=1, source_target_pairs={{0,1},{1,0},{2,3},{3,2},{4,5},{5,4},{6,7},{7,6},{8,9},{9,8},{10,11... | collective-permute-start | bytes 589832 | tf_op jit(solution)/shard_map/ppermute | solution.py:372
  25.8 3.5 %collective-permute-start.9 = (bf16[12,4,8,256]{3,2,1,0:T(8,128)(2,1)S(1)}, bf16[12,4,8,256]{3,2,1,0:T(8,128)(2,1)S(1)}, u32[]{:S(2)}, u32[]{:S(2)}) collective-permute-start(bf16[12,4,8,256]{3,2,1,0:T(8,128)(2,1)S(1)} %get-tuple-element.64), channel_id=1, source_target_pairs={{1,2},{2,1},{5,6},{6,5},{9,10},{10,9},{13,14},{14,13},{17,18},{18,... | collective-permute-start | bytes 589832 | tf_op jit(solution)/shard_map/ppermute | solution.py:372
  29.3 0.1 collective-permute-start.10
  29.4 2.6 %collective-permute-start.11 = (bf16[4,4,8,256]{3,2,1,0:T(8,128)(2,1)S(1)}, bf16[4,4,8,256]{3,2,1,0:T(8,128)(2,1)S(1)}, u32[]{:S(2)}, u32[]{:S(2)}) collective-permute-start(bf16[4,4,8,256]{3,2,1,0:T(8,128)(2,1)S(1)} %get-tuple-element.66), channel_id=1, source_target_pairs={{5,10},{6,9},{9,6},{10,5},{13,18},{14,17},{17,14},{18,13},{21,26},... | collective-permute-start | bytes 196616 | tf_op jit(solution)/shard_map/ppermute | solution.py:376
  32.0 2.6 %collective-permute-done.9.zb_ref = bf16[12,4,8,256]{3,2,1,0:T(8,128)(2,1)S(1)} collective-permute-done((bf16[12,4,8,256]{3,2,1,0:T(8,128)(2,1)S(1)}, bf16[12,4,8,256]{3,2,1,0:T(8,128)(2,1)S(1)}, u32[]{:S(2)}, u32[]{:S(2)}) %collective-permute-start.9) | collective-permute-done | bytes 196640 | tf_op jit(solution)/shard_map/ppermute | solution.py:372
  34.6 0.4 %gather.1.base_ref = f32[12,12,8,256]{3,2,1,0:T(8,128)S(1)} custom-call(f32[12,12,8,256]{3,2,1,0:T(8,128)S(1)} %get-tuple-element.57.inner_ref, f32[12,12,8,128]{3,2,1,0:T(8,128)S(1)} %get-tuple-element.58.wide_ref, bf16[4,20,8,256]{3,2,1,0:T(8,128)(2,1)S(1)} %collective-permute-done.6.xa_ref, bf16[4,12,8,256]{3,2,1,0:T(8,128)(2,1)S(1)} %collective-permute-done.7.xb_ref, ...), custom_call_target="tpu_custom_call" | custom-call | flops 4000000000 | bytes 40000000 | tf_op jit(solution)/shard_map/gather/pallas_call | solution.py:497
  35.0 1.9 %collective-permute-done.11.db_ref = bf16[4,4,8,256]{3,2,1,0:T(8,128)(2,1)S(1)} collective-permute-done((bf16[4,4,8,256]{3,2,1,0:T(8,128)(2,1)S(1)}, bf16[4,4,8,256]{3,2,1,0:T(8,128)(2,1)S(1)}, u32[]{:S(2)}, u32[]{:S(2)}) %collective-permute-start.11) | collective-permute-done | bytes 65568 | tf_op jit(solution)/shard_map/ppermute | solution.py:376
  36.8 0.9 %finish.1 = bf16[12,12,8,256]{3,2,1,0:T(8,128)(2,1)} custom-call(f32[12,12,8,256]{3,2,1,0:T(8,128)S(1)} %gather.1.base_ref, f32[12,12,8,128]{3,2,1,0:T(8,128)S(1)} %get-tuple-element.58.wide_ref, bf16[4,4,8,256]{3,2,1,0:T(8,128)(2,1)S(1)} %collective-permute-done.10.da_ref, bf16[4,4,8,256]{3,2,1,0:T(8,128)(2,1)S(1)} %collective-permute-done.11.db_ref), custom_call_target="tpu_custom_call" | custom-call | flops 1000 | bytes 1000 | tf_op jit(solution)/shard_map/finish/pallas_call | solution.py:506
  (10 shorter events, 0.0 us)
Async XLA Ops:
  0.0 16.3 %copy-start = (bf16[3,3,128,256]{3,2,1,0:T(8,128)(2,1)S(1)}, bf16[3,3,128,256]{3,2,1,0:T(8,128)(2,1)}, u32[]{:S(2)}) copy-start(bf16[3,3,128,256]{3,2,1,0:T(8,128)(2,1)} %refs_1_.1) | copy-start | bytes 1769476
  1.4 14.7 %collective-permute-start = (bf16[3,128,256]{2,1,0:T(8,128)(2,1)S(1)}, bf16[3,128,256]{2,1,0:T(8,128)(2,1)S(1)}, u32[]{:S(2)}, u32[]{:S(2)}) collective-permute-start(bf16[3,128,256]{2,1,0:T(8,128)(2,1)S(1)} %get-tuple-element.37), channel_id=1, source_target_pairs={{1,2},{2,1},{5,6},{6,5},{9,10},{10,9},{13,14},{14,13},{17,18},{18,... | collective-permute-start | bytes 589832 | tf_op jit(solution)/shard_map/ppermute | solution.py:372
  4.9 11.2 %collective-permute-start.1 = (bf16[3,128,256]{2,1,0:T(8,128)(2,1)S(1)}, bf16[3,128,256]{2,1,0:T(8,128)(2,1)S(1)}, u32[]{:S(2)}, u32[]{:S(2)}) collective-permute-start(bf16[3,128,256]{2,1,0:T(8,128)(2,1)S(1)} %get-tuple-element.38), channel_id=1, source_target_pairs={{0,1},{1,0},{2,3},{3,2},{4,5},{5,4},{6,7},{7,6},{8,9},{9,8},{10,11... | collective-permute-start | bytes 589832 | tf_op jit(solution)/shard_map/ppermute | solution.py:372
  5.0 11.2 %collective-permute-start.2 = (bf16[3,128,256]{2,1,0:T(8,128)(2,1)S(1)}, bf16[3,128,256]{2,1,0:T(8,128)(2,1)S(1)}, u32[]{:S(2)}, u32[]{:S(2)}) collective-permute-start(bf16[3,128,256]{2,1,0:T(8,128)(2,1)S(1)} %get-tuple-element.39), channel_id=1, source_target_pairs={{4,8},{8,4},{12,16},{16,12},{20,24},{24,20},{28,0},{0,28},{5,9},{9... | collective-permute-start | bytes 589832 | tf_op jit(solution)/shard_map/ppermute | solution.py:369
  6.7 8.7 %collective-permute-start.3 = (bf16[128,256]{1,0:T(8,128)(2,1)S(1)}, bf16[128,256]{1,0:T(8,128)(2,1)S(1)}, u32[]{:S(2)}, u32[]{:S(2)}) collective-permute-start(bf16[128,256]{1,0:T(8,128)(2,1)S(1)} %get-tuple-element.40), channel_id=1, source_target_pairs={{5,10},{6,9},{9,6},{10,5},{13,18},{14,17},{17,14},{18,13},{21,26},... | collective-permute-start | bytes 196616 | tf_op jit(solution)/shard_map/ppermute | solution.py:376
  9.5 6.6 %collective-permute-start.4 = (bf16[128,256]{1,0:T(8,128)(2,1)S(1)}, bf16[128,256]{1,0:T(8,128)(2,1)S(1)}, u32[]{:S(2)}, u32[]{:S(2)}) collective-permute-start(bf16[128,256]{1,0:T(8,128)(2,1)S(1)} %get-tuple-element.41), channel_id=1, source_target_pairs={{4,9},{5,8},{6,11},{7,10},{8,5},{9,4},{10,7},{11,6},{12,17},{13,16... | collective-permute-start | bytes 196616 | tf_op jit(solution)/shard_map/ppermute | solution.py:376
  16.2 2.6 %collective-permute-start.5 = (bf16[5,128,256]{2,1,0:T(8,128)(2,1)S(1)}, bf16[5,128,256]{2,1,0:T(8,128)(2,1)S(1)}, u32[]{:S(2)}, u32[]{:S(2)}) collective-permute-start(bf16[5,128,256]{2,1,0:T(8,128)(2,1)S(1)} %extend.1), channel_id=1, source_target_pairs={{0,4},{4,0},{8,12},{12,8},{16,20},{20,16},{24,28},{28,24},{1,5},{5... | collective-permute-start | bytes 983048 | tf_op jit(solution)/shard_map/ppermute | solution.py:369
  22.7 1.8 %collective-permute-start.6 = (bf16[4,20,8,256]{3,2,1,0:T(8,128)(2,1)S(1)}, bf16[4,20,8,256]{3,2,1,0:T(8,128)(2,1)S(1)}, u32[]{:S(2)}, u32[]{:S(2)}) collective-permute-start(bf16[4,20,8,256]{3,2,1,0:T(8,128)(2,1)S(1)} %get-tuple-element.59), channel_id=1, source_target_pairs={{0,4},{4,0},{8,12},{12,8},{16,20},{20,16},{24,28},{28,24},{1,5},{5... | collective-permute-start | bytes 983048 | tf_op jit(solution)/shard_map/ppermute | solution.py:369
  23.2 8.8 %collective-permute-start.7 = (bf16[4,12,8,256]{3,2,1,0:T(8,128)(2,1)S(1)}, bf16[4,12,8,256]{3,2,1,0:T(8,128)(2,1)S(1)}, u32[]{:S(2)}, u32[]{:S(2)}) collective-permute-start(bf16[4,12,8,256]{3,2,1,0:T(8,128)(2,1)S(1)} %get-tuple-element.60), channel_id=1, source_target_pairs={{4,8},{8,4},{12,16},{16,12},{20,24},{24,20},{28,0},{0,28},{5,9},{9... | collective-permute-start | bytes 589832 | tf_op jit(solution)/shard_map/ppermute | solution.py:369
  24.5 7.5 %collective-permute-start.8 = (bf16[12,4,8,256]{3,2,1,0:T(8,128)(2,1)S(1)}, bf16[12,4,8,256]{3,2,1,0:T(8,128)(2,1)S(1)}, u32[]{:S(2)}, u32[]{:S(2)}) collective-permute-start(bf16[12,4,8,256]{3,2,1,0:T(8,128)(2,1)S(1)} %get-tuple-element.63), channel_id=1, source_target_pairs={{0,1},{1,0},{2,3},{3,2},{4,5},{5,4},{6,7},{7,6},{8,9},{9,8},{10,11... | collective-permute-start | bytes 589832 | tf_op jit(solution)/shard_map/ppermute | solution.py:372
  25.8 8.8 %collective-permute-start.9 = (bf16[12,4,8,256]{3,2,1,0:T(8,128)(2,1)S(1)}, bf16[12,4,8,256]{3,2,1,0:T(8,128)(2,1)S(1)}, u32[]{:S(2)}, u32[]{:S(2)}) collective-permute-start(bf16[12,4,8,256]{3,2,1,0:T(8,128)(2,1)S(1)} %get-tuple-element.64), channel_id=1, source_target_pairs={{1,2},{2,1},{5,6},{6,5},{9,10},{10,9},{13,14},{14,13},{17,18},{18,... | collective-permute-start | bytes 589832 | tf_op jit(solution)/shard_map/ppermute | solution.py:372
  29.3 5.7 %collective-permute-start.10 = (bf16[4,4,8,256]{3,2,1,0:T(8,128)(2,1)S(1)}, bf16[4,4,8,256]{3,2,1,0:T(8,128)(2,1)S(1)}, u32[]{:S(2)}, u32[]{:S(2)}) collective-permute-start(bf16[4,4,8,256]{3,2,1,0:T(8,128)(2,1)S(1)} %get-tuple-element.65), channel_id=1, source_target_pairs={{4,9},{5,8},{6,11},{7,10},{8,5},{9,4},{10,7},{11,6},{12,17},{13,16... | collective-permute-start | bytes 196616 | tf_op jit(solution)/shard_map/ppermute | solution.py:376
  29.4 7.5 %collective-permute-start.11 = (bf16[4,4,8,256]{3,2,1,0:T(8,128)(2,1)S(1)}, bf16[4,4,8,256]{3,2,1,0:T(8,128)(2,1)S(1)}, u32[]{:S(2)}, u32[]{:S(2)}) collective-permute-start(bf16[4,4,8,256]{3,2,1,0:T(8,128)(2,1)S(1)} %get-tuple-element.66), channel_id=1, source_target_pairs={{5,10},{6,9},{9,6},{10,5},{13,18},{14,17},{17,14},{18,13},{21,26},... | collective-permute-start | bytes 196616 | tf_op jit(solution)/shard_map/ppermute | solution.py:376

commit v2 on v1

--- a/solution.py
+++ b/solution.py
@@ -9,6 +9,7 @@
 SPAN = 2 * REACH + 1
 LAYERS = 4
 NEAR = 3
+LOOKS = 2
 EXPONENTS = (
     (0, 0, 0),
     (1, 0, 0),
@@ -49,16 +50,27 @@
     return lax.rem(lax.axis_index("gx"), 2), lax.rem(lax.axis_index("gy"), 2)
 
 
-def swap(size, first, wrap):
+def partner(i, size, turn, wrap):
+    j = i + 1 if i % 2 == turn else i - 1
+    return j % size if wrap or 0 <= j < size else None
+
+
+def routes(across, along, turn_x, turn_y):
     pairs = []
-    for i in range(first, size, 2):
-        j = i + 1
-        if j == size:
-            if not wrap:
-                continue
-            j = 0
-        pairs += [(i, j), (j, i)]
+    for i in range(across):
+        for j in range(along):
+            to = i if turn_x is None else partner(i, across, turn_x, True)
+            up_to = j if turn_y is None else partner(j, along, turn_y, False)
+            if up_to is None:
+                to, up_to = partner(i, across, 0, True), j
+            pairs.append((i * along + j, to * along + up_to))
     return pairs
+
+
+def paired(turn):
+    j, odd = lax.axis_index("gy"), parity()[1]
+    to = jnp.where(odd == turn, j + 1, j - 1)
+    return jnp.where((to >= 0) & (to < lax.axis_size("gy")), 1.0, 0.0).astype(jnp.float32)
 
 
 def pack_kernel(count, nodes_ref, *refs):
@@ -94,17 +106,21 @@
 
 
 def prepare_kernel(
-    sides, subregion, tile, radius_ref, xyz_ref, scale_ref, cells_ref, valid_ref, nodes_ref, far_ref,
-    design_ref, wide_ref, hot_ref, fit_ref, near_ref, split, places, sem, *scratch,
+    sides, subregion, tile, radius_ref, xyz_ref, cells_ref, valid_ref, nodes_ref, far_ref,
+    design_ref, hot_ref, fit_ref, near_ref, split, places, sem, *scratch,
 ):
+    slots, patches, unknowns = far_ref.shape
     copy = pltpu.make_async_copy(far_ref, near_ref, sem)
     copy.start()
-    design_kernel(nodes_ref.shape[1], near_ref.shape[2], radius_ref, xyz_ref, scale_ref, design_ref, wide_ref, *scratch)
+    choose(sides, subregion, tile, cells_ref, valid_ref, nodes_ref, hot_ref, places)
+    design_kernel(slots, unknowns, radius_ref, xyz_ref, design_ref, *scratch)
     copy.wait()
-    choose(sides, subregion, tile, cells_ref, valid_ref, nodes_ref, near_ref, hot_ref, fit_ref, split, places)
-
-
-def design_kernel(nodes, unknowns, radius_ref, xyz_ref, scale_ref, design_ref, wide_ref, pos, ax, by, ax2, bc, bm, bl):
+    spread(near_ref, split)
+    for p in range(patches):
+        turn(p, split, fit_ref, slots)
+
+
+def design_kernel(nodes, unknowns, radius_ref, xyz_ref, design_ref, pos, ax, by, ax2, bc, bm, bl, far):
     patches = design_ref.shape[0]
     lanes = design_ref.shape[2]
     tile = (2 * LAYERS, lanes)
@@ -137,7 +153,10 @@
     tail = slice(lanes - 128, lanes)
     half = SPAN // 2
 
-    def patch(p, carry):
+    for index, flat in enumerate(DISTANCES):
+        far[index] = jnp.sqrt(float(flat) + deep[:, :128] * deep[:, :128])
+
+    def patch(p, q):
         inverse = 1.0 / jnp.full((1, lanes), radius_ref[0, p], jnp.float32)
         x = jnp.where(is_node, pos[0, pl.ds(p, 1), :], 0.0)
         y = jnp.where(is_node, pos[1, pl.ds(p, 1), :], 0.0)
@@ -145,28 +164,28 @@
         dx = (across - x) * inverse
         dy = (across - y) * inverse
         dz = (deep - z) * inverse
-        ax[...] = jnp.where(is_node, dx * dx, raised(dx, 0))
-        by[...] = jnp.where(is_node, dy * dy, raised(dy, 1))
+        ax[q] = jnp.where(is_node, dx * dx, raised(dx, 0))
+        by[q] = jnp.where(is_node, dy * dy, raised(dy, 1))
         cz = jnp.where(is_node, dz * dz + 1e-30, raised(dz, 2))
         for i in range(half + 1):
             low, high = 2 * i, min(2 * i + 1, SPAN - 1)
-            row = jnp.where(upper, by[low : low + 1, :], by[high : high + 1, :])
-            bc[i] = row + cz
-            bm[i] = row[:, tail] * cz[:, tail]
-            ax2[i] = jnp.where(upper, ax[low : low + 1, :], ax[high : high + 1, :])
+            row = jnp.where(upper, by[q, low : low + 1, :], by[q, high : high + 1, :])
+            bc[q, i] = row + cz
+            bm[q, i] = row[:, tail] * cz[:, tail]
+            ax2[q, i] = jnp.where(upper, ax[q, low : low + 1, :], ax[q, high : high + 1, :])
         for index, flat in enumerate(DISTANCES):
-            rho = jnp.sqrt(float(flat) + deep[:, :128] * deep[:, :128]) * inverse[:, :128]
+            rho = far[index] * inverse[:, :128]
             left = jnp.maximum(1.0 - rho, 0.0)
             left = left * left
-            bl[index] = left * left * (4.0 * rho + 1.0)
+            bl[q, index] = left * left * (4.0 * rho + 1.0)
 
         def pair(spots):
             (ex, ey), (fx, fy) = spots[0], spots[-1]
-            row = ax[ex : ex + 1, :] if ex == fx else ax2[ex // 2]
-            part = row + bc[ey // 2]
+            row = ax[q, ex : ex + 1, :] if ex == fx else ax2[q, ex // 2]
+            part = row + bc[q, ey // 2]
             part = part * part * lax.rsqrt(part)
-            last = row[:, tail] * bm[ey // 2]
-            blend = [bl[DISTANCES.index((i - REACH) ** 2 + (j - REACH) ** 2)] for i, j in ((ex, ey), (fx, fy))]
+            last = row[:, tail] * bm[q, ey // 2]
+            blend = [bl[q, DISTANCES.index((i - REACH) ** 2 + (j - REACH) ** 2)] for i, j in ((ex, ey), (fx, fy))]
             blend = blend[0] if (ex, ey) == (fx, fy) else jnp.where(upper[:, :128], blend[0], blend[1])
             if len(spots) == 1:
                 blend = jnp.where(upper[:, :128], blend, 0.0)
@@ -175,27 +194,35 @@
             return jnp.concatenate([piece * blend for piece in pieces], 1)
 
         for spot in range(0, len(SPOTS), 4):
-            rows = [pair(SPOTS[q : q + 2]) if q < len(SPOTS) else jnp.zeros(tile, jnp.float32) for q in (spot, spot + 2)]
+            rows = [pair(SPOTS[r : r + 2]) if r < len(SPOTS) else jnp.zeros(tile, jnp.float32) for r in (spot, spot + 2)]
             design_ref[p, spot * LAYERS : (spot + 4) * LAYERS, :] = jnp.concatenate(rows, 0).astype(jnp.bfloat16)
-        return carry
-
-    lax.fori_loop(0, patches, patch, 0)
-    for i in range(scale_ref.shape[0]):
-        columns = scale_ref[i]
-        for j in range(scale_ref.shape[2]):
-            wide_ref[i, j] = jnp.broadcast_to(columns[:, j : j + 1], wide_ref.shape[2:])
-
-
-def choose(sides, subregion, tile, cells_ref, valid_ref, nodes_ref, fit_ref, hot, fit, wide, places):
-    patches, slots = nodes_ref.shape
-    unknowns = fit.shape[1]
-    padded = hot.shape[1]
-    kind = fit.dtype
-    lane = lax.broadcasted_iota(jnp.int32, (1, slots), 1)
-    places[...] = jnp.full(places.shape, -1.0, jnp.float32)
+
+    for p in range(patches):
+        patch(p, p % LOOKS)
+
+
+def spread(fit_ref, wide):
+    slots, patches, unknowns = fit_ref.shape
     for c in range(0, unknowns, 128):
         width = min(128, unknowns - c)
         wide[c // 128, :, :width] = fit_ref[:, :, c : c + width].astype(jnp.float32).reshape(slots * patches, width)
+
+
+def turn(p, wide, fit, slots):
+    patches, unknowns, padded = fit.shape
+    for c in range(0, unknowns, 128):
+        width = min(128, unknowns - c)
+        piece = wide[c // 128, pl.ds(p, slots, stride=patches), :].astype(fit.dtype)
+        fit[p, c : c + width, 0:slots] = piece.T[:width]
+        fit[p, c : c + width, slots:padded] = jnp.zeros((width, padded - slots), fit.dtype)
+
+
+def choose(sides, subregion, tile, cells_ref, valid_ref, nodes_ref, hot, places):
+    patches, slots = nodes_ref.shape
+    padded = hot.shape[1]
+    kind = hot.dtype
+    lane = lax.broadcasted_iota(jnp.int32, (1, slots), 1)
+    places[...] = jnp.full(places.shape, -1.0, jnp.float32)
     for p in range(patches):
         index = nodes_ref[p : p + 1, :]
         where = lax.div(index, jnp.int32(subregion))
@@ -211,17 +238,12 @@
     inner, local = places[0].T, places[1].T
     node = lax.broadcasted_iota(jnp.int32, (padded, subregion), 1).astype(jnp.float32).astype(kind)
     one, zero = jnp.ones((), kind), jnp.zeros((), kind)
-    fit[:, :, slots:] = jnp.zeros((patches, unknowns, padded - slots), kind)
     for p in range(patches):
         column = jnp.broadcast_to(inner[:padded, p : p + 1], (padded, subregion)).astype(kind)
         one_hot = jnp.where(node == column, one, zero)
         column = jnp.broadcast_to(local[:padded, p : p + 1], (padded, subregion)).astype(kind)
         for s in range(NEAR * NEAR):
             hot[p, :, s * subregion : (s + 1) * subregion] = jnp.where(column == jnp.full((), s, kind), one_hot, zero)
-        for c in range(0, unknowns, 128):
-            width = min(128, unknowns - c)
-            piece = wide[c // 128, pl.ds(p, slots, stride=patches), :]
-            fit[p, c : c + width, 0:slots] = piece.T[:width].astype(kind)
 
 
 def home(sides, tile, cells_ref, p):
@@ -229,7 +251,7 @@
 
 
 def sample_kernel(
-    tile, cells_ref, own_ref, b_ref, c_ref, d_ref, e_ref, f_ref, hot_ref, out_ref, near,
+    tile, cells_ref, own_ref, b_ref, c_ref, d_ref, hot_ref, out_ref, near,
 ):
     sx, sy, subregion, fields = own_ref.shape
     odd_x, odd_y = parity()
@@ -241,20 +263,20 @@
     near[xb, 1 : sy + 1] = b_ref[...]
     near[1 : sx + 1, ya] = c_ref[...]
     near[1 : sx + 1, yb] = d_ref[...]
-    near[xb, ya] = e_ref[...]
-    near[xb, yb] = f_ref[...]
+    near[xb, ya] = jnp.zeros(near.shape[2:], near.dtype)
+    near[xb, yb] = jnp.zeros(near.shape[2:], near.dtype)
     near[xa] = jnp.zeros(near.shape[1:], near.dtype)
     for p in range(hot_ref.shape[0]):
         home_x, home_y = home((sx, sy), tile, cells_ref, p)
         window = jnp.concatenate(
             [near[home_x + r, pl.ds(home_y, NEAR)].reshape(NEAR * subregion, fields) for r in range(NEAR)], 0
         )
-        out_ref[p] = jnp.dot(hot_ref[p], window, preferred_element_type=jnp.float32)
+        out_ref[p] = jnp.dot(hot_ref[p], window, preferred_element_type=jnp.float32).astype(out_ref.dtype)
 
 
 def blend_kernel(
-    sides, tile, cells_ref, side_ref, sample_ref, hot_ref, fit_ref, design_ref,
-    inner_ref, xa_ref, xb_ref, da_ref, db_ref, za_ref, zb_ref, chosen, coeffs, values, acc,
+    sides, tile, cells_ref, side_ref, ea_ref, eb_ref, sample_ref, hot_ref, fit_ref, design_ref,
+    inner_ref, xa_ref, xb_ref, da_ref, db_ref, za_ref, zb_ref, edges, chosen, coeffs, values, acc,
 ):
     sx, sy = sides
     subregion, fields = side_ref.shape[1:]
@@ -262,17 +284,22 @@
     cx, cy = tile
     rows = len(SPOTS) * LAYERS
     odd_x, odd_y = parity()
-    xa = (1 - odd_x) * (sx + 1)
+    xa, xb = (1 - odd_x) * (sx + 1), odd_x * (sx + 1)
     acc[...] = jnp.zeros_like(acc)
+    edges[0] = side_ref[...]
+    edges[1, 1 : sy + 1] = jnp.zeros((sy, subregion, fields), edges.dtype)
+    edges[1, (1 - odd_y) * (sy + 1)] = ea_ref[...]
+    edges[1, odd_y * (sy + 1)] = eb_ref[...]
     for p in range(patches):
         home_x, home_y = home(sides, tile, cells_ref, p)
-        row = xa - home_x
+        turn = jnp.where(jnp.abs(xa - home_x - 1) <= 1, 0, 1)
+        row = jnp.where(turn == 0, xa, xb) - home_x
         here = (row >= 0) & (row < NEAR)
         spot = pl.multiple_of(jnp.where(here, row, 0) * (NEAR * subregion), NEAR * subregion)
-        side = side_ref[pl.ds(home_y, NEAR)].reshape(NEAR * subregion, fields)
-        side = side * jnp.where(here, 1.0, 0.0).astype(side.dtype)
-        extra = jnp.dot(hot_ref[p, :, pl.ds(spot, NEAR * subregion)], side, preferred_element_type=jnp.float32)
-        chosen[p] = (sample_ref[p] + extra).astype(chosen.dtype)
+        edge = edges[turn, pl.ds(home_y, NEAR)].reshape(NEAR * subregion, fields)
+        edge = edge * jnp.where(here, 1.0, 0.0).astype(edge.dtype)
+        extra = jnp.dot(hot_ref[p, :, pl.ds(spot, NEAR * subregion)], edge, preferred_element_type=jnp.float32)
+        chosen[p] = sample_ref[p] + extra.astype(chosen.dtype)
     for p in range(patches):
         coeffs[p] = jnp.dot(fit_ref[p], chosen[p], preferred_element_type=jnp.float32).astype(coeffs.dtype)
 
@@ -298,8 +325,8 @@
         f = pl.ds(l * 128, 128)
         xa_ref[:, :, :, f] = acc[l, pl.ds(ra, rim)].astype(xa_ref.dtype)
         xb_ref[:, :, :, f] = acc[l, pl.ds(rb, rim), in_y].astype(xb_ref.dtype)
-        for ref, s in ((da_ref, sa), (db_ref, sb)):
-            ref[:, :, :, f] = acc[l, pl.ds(rb, rim), pl.ds(s, rim)].astype(ref.dtype)
+        for ref, s, turn in ((da_ref, sa, 0), (db_ref, sb, 1)):
+            ref[:, :, :, f] = (acc[l, pl.ds(rb, rim), pl.ds(s, rim)] * paired(turn)).astype(ref.dtype)
         for ref, s in ((za_ref, sa), (zb_ref, sb)):
             ref[:, :, :, f] = acc[l, in_x, pl.ds(s, rim)]
         inner_ref[:, :, :, f] = acc[l, in_x, in_y]
@@ -310,14 +337,19 @@
     cx = za_ref.shape[0]
     rows = pl.ds((1 - odd_x) * (cx - REACH), REACH)
     last = xa_ref.shape[1] - REACH
-    for z_ref, out_ref, s in ((za_ref, outa_ref, (1 - odd_y) * last), (zb_ref, outb_ref, odd_y * last)):
-        out_ref[...] = z_ref[...].astype(out_ref.dtype)
+    for z_ref, out_ref, s, turn in ((za_ref, outa_ref, (1 - odd_y) * last, 0), (zb_ref, outb_ref, odd_y * last, 1)):
+        keep = paired(turn)
+        out_ref[...] = (z_ref[...] * keep).astype(out_ref.dtype)
         got = xa_ref[:, pl.ds(s, REACH)].astype(jnp.float32)
-        out_ref[rows] = (z_ref[rows] + got).astype(out_ref.dtype)
-
-
-def gather_kernel(inner_ref, wide_ref, xa_ref, xb_ref, za_ref, zb_ref, out_ref):
+        out_ref[rows] = ((z_ref[rows] + got) * keep).astype(out_ref.dtype)
+
+
+def gather_kernel(inner_ref, scale_ref, xa_ref, xb_ref, za_ref, zb_ref, out_ref, wide_ref):
     cx, cy, depth, fields = inner_ref.shape
+    for i in range(cx):
+        columns = scale_ref[i]
+        for j in range(cy):
+            wide_ref[i, j] = jnp.broadcast_to(columns[:, j : j + 1], wide_ref.shape[2:])
     odd_x, odd_y = parity()
     far, back = pl.ds((1 - odd_x) * (cx - REACH), REACH), pl.ds(odd_x * (cx - REACH), REACH)
     for f in range(0, fields, 128):
@@ -362,18 +394,17 @@
     rows = up(len(SPOTS), 4) * LAYERS
     halves = fields // 128
 
-    pairs_x = [swap(across, first, True) for first in (0, 1)]
-    pairs_y = [swap(along, first, False) for first in (0, 1)]
+    def send(block, turn_x, turn_y):
+        return lax.ppermute(block, ("gx", "gy"), routes(across, along, turn_x, turn_y))
 
     def send_x(block, turn):
-        return lax.ppermute(block, "gx", pairs_x[turn])
+        return send(block, turn, None)
 
     def send_y(block, turn):
-        return lax.ppermute(block, "gy", pairs_y[turn])
+        return send(block, None, turn)
 
     def send_across(block, turn):
-        both = [(a * along + c, b * along + d) for a, b in pairs_x[1] for c, d in pairs_y[turn]]
-        return lax.ppermute(block, ("gx", "gy"), both)
+        return send(block, 1, turn)
 
     line = lambda *sides: shape(sides + (subregion, fields), kind)
     plain = (
@@ -403,36 +434,34 @@
     window = NEAR * NEAR * subregion
     padded = up(slots, 16)
     far = pltpu.with_memory_space_constraint(fit_ops[0, 0].transpose(2, 0, 1), pltpu.HBM)
-    design, wide, hot, fit = pl.pallas_call(
+    design, hot, fit = pl.pallas_call(
         lambda *refs: prepare_kernel((sx, sy), subregion, (cx, cy), *refs),
         out_shape=(
             shape((patches, rows, lanes), kind),
-            shape((cx, cy, depth, 128), full),
             shape((patches, padded, window), kind),
             shape((patches, unknowns, padded), kind),
         ),
-        in_specs=[SMEM, VMEM, VMEM, SMEM, SMEM, VMEM, pl.BlockSpec(memory_space=pl.ANY)],
-        out_specs=(VMEM,) * 4,
+        in_specs=[SMEM, VMEM, SMEM, SMEM, VMEM, pl.BlockSpec(memory_space=pl.ANY)],
+        out_specs=(VMEM,) * 3,
         scratch_shapes=[
             pltpu.VMEM(far.shape, kind),
             pltpu.VMEM((lanes // 128, slots * patches, 128), full),
             pltpu.VMEM((2, patches, up(padded, 128)), full),
             pltpu.SemaphoreType.DMA,
             pltpu.VMEM((3, patches, lanes), full),
-            pltpu.VMEM((16, lanes), full),
-            pltpu.VMEM((16, lanes), full),
-            pltpu.VMEM((SPAN // 2 + 1, 2 * LAYERS, lanes), full),
-            pltpu.VMEM((SPAN // 2 + 1, 2 * LAYERS, lanes), full),
-            pltpu.VMEM((SPAN // 2 + 1, 2 * LAYERS, 128), full),
+            pltpu.VMEM((LOOKS, 16, lanes), full),
+            pltpu.VMEM((LOOKS, 16, lanes), full),
+            pltpu.VMEM((LOOKS, SPAN // 2 + 1, 2 * LAYERS, lanes), full),
+            pltpu.VMEM((LOOKS, SPAN // 2 + 1, 2 * LAYERS, lanes), full),
+            pltpu.VMEM((LOOKS, SPAN // 2 + 1, 2 * LAYERS, 128), full),
+            pltpu.VMEM((LOOKS, len(DISTANCES), 2 * LAYERS, 128), full),
             pltpu.VMEM((len(DISTANCES), 2 * LAYERS, 128), full),
         ],
         compiler_params=params(24),
         cost_estimate=SMALL,
         name="prepare",
-    )(radius, xyz, scale, cells, valid, indices, far)
-    from_yb, from_ya, from_xb, from_db, from_da, hot = lax.optimization_barrier(
-        (from_yb, from_ya, from_xb, from_db, from_da, hot)
-    )
+    )(radius, xyz, cells, valid, indices, far)
+    from_xb, from_yb, from_ya, hot = lax.optimization_barrier((from_xb, from_yb, from_ya, hot))
     to_xa = pl.pallas_call(
         extend_kernel,
         out_shape=line(sy + 2),
@@ -445,14 +474,14 @@
     from_xa = send_x(to_xa, 0)
     samples = pl.pallas_call(
         lambda *refs: sample_kernel((cx, cy), *refs),
-        out_shape=shape((patches, padded, fields), full),
-        in_specs=[SMEM] + [VMEM] * 7,
+        out_shape=shape((patches, padded, fields), kind),
+        in_specs=[SMEM] + [VMEM] * 5,
         out_specs=VMEM,
         scratch_shapes=[pltpu.VMEM((sx + 2, sy + 2, subregion, fields), kind)],
         compiler_params=params(16),
         cost_estimate=LARGE,
         name="sample",
-    )(cells, node_values, from_xb, from_ya, from_yb, from_da, from_db, hot)
+    )(cells, node_values, from_xb, from_ya, from_yb, hot)
 
     block = lambda *dims, kind=kind: shape(dims + (depth, fields), kind)
     inner, xa, xb, da, db, za, zb = pl.pallas_call(
@@ -466,9 +495,10 @@
             block(cx, REACH, kind=full),
             block(cx, REACH, kind=full),
         ),
-        in_specs=[SMEM] + [VMEM] * 5,
+        in_specs=[SMEM] + [VMEM] * 7,
         out_specs=(VMEM,) * 7,
         scratch_shapes=[
+            pltpu.VMEM((2, sy + 2, subregion, fields), kind),
             pltpu.VMEM((patches, padded, fields), kind),
             pltpu.VMEM((patches, unknowns, fields), kind),
             pltpu.VMEM((patches, len(SPOTS) * LAYERS, fields), full),
@@ -477,7 +507,7 @@
         compiler_params=params(32),
         cost_estimate=SMALL,
         name="blend",
-    )(cells, from_xa, samples, hot, fit, design)
+    )(cells, from_xa, from_da, from_db, samples, hot, fit, design)
 
     got_xa = send_x(xa, 0)
     got_xb = send_x(xb, 1)
@@ -494,15 +524,15 @@
     )(za, zb, got_xa)
     got_za = send_y(za, 0)
     got_zb = send_y(zb, 1)
-    base = pl.pallas_call(
+    base, wide = pl.pallas_call(
         gather_kernel,
-        out_shape=block(cx, cy, kind=full),
+        out_shape=(block(cx, cy, kind=full), shape((cx, cy, depth, 128), full)),
         in_specs=[VMEM] * 6,
-        out_specs=VMEM,
+        out_specs=(VMEM, VMEM),
         compiler_params=params(12),
         cost_estimate=LARGE,
         name="gather",
-    )(inner, wide, got_xa, got_xb, got_za, got_zb)
+    )(inner, scale, got_xa, got_xb, got_za, got_zb)
     return pl.pallas_call(
         finish_kernel,
         out_shape=block(cx, cy),

time: 38 us -> 33.3 us (0.88)
  starting transfers between devices: 17.1 us -> 13.6 us
  waiting for transfers between devices: 6.65 us -> 5.48 us
    ppermute x12, starting transfers between devices: 17.1 us -> 13.6 us  [send(): lax.ppermute(block, ('gx', 'gy'), routes(across, along, turn_x, turn_y))]
    ppermute x12, waiting for transfers between devices: 6.65 us -> 5.48 us  [send(): lax.ppermute(block, ('gx', 'gy'), routes(across, along, turn_x, turn_y))]
  transfers between devices with their start and end apart: 12 -> 12, of which waited for: 5 -> 6; matrix products, arithmetic and copies ran while one was open for 0% -> 0% of each run, Pallas kernels for 20% -> 23%
where the time goes in v2:
time: 33.3 us; the launch traced here: 33.1 us
  Pallas kernels  13.9 us (42%)
  starting transfers between devices  13.6 us (41%)
  waiting for transfers between devices  5.48 us (16%)
    ppermute x12, starting transfers between devices, send(): lax.ppermute(block, ('gx', 'gy'), routes(across, along, turn_x, turn_y))  13.6 us
    ppermute x12, waiting for transfers between devices, send(): lax.ppermute(block, ('gx', 'gy'), routes(across, along, turn_x, turn_y))  5.48 us
    pallas_call x1, Pallas kernels, local(): pl.pallas_call(lambda *refs: prepare_kernel((sx, sy), subregion, (cx, cy)...  4.49 us
    pallas_call x1, Pallas kernels, local(): pl.pallas_call(lambda *refs: blend_kernel((sx, sy), (cx, cy), *refs), out...  3.86 us
    pallas_call x1, Pallas kernels, local(): pl.pallas_call(lambda *refs: sample_kernel((cx, cy), *refs), out_shape=sh...  2.46 us
    pallas_call x1, Pallas kernels, local(): pl.pallas_call(lambda *refs: pack_kernel(len(plain), *refs), out_shape=(l...  1.41 us
    pallas_call x1, Pallas kernels, local(): pl.pallas_call(finish_kernel, out_shape=block(cx, cy), in_specs=[VMEM] *...  0.93 us
  transfers between devices with their start and end apart: 12, of which 6 were waited for; matrix products, arithmetic and copies ran while one was open for 0% of the time, Pallas kernels for 23%

profile of v2, /device:TPU:8, one launch (start us, length us, event | category | flops | bytes accessed | tf_op | source)
XLA Modules:
  0.0 33.1 jit_solution(15212028151052113752)
XLA Ops:
  0.0 1.4 %pack.1 = (bf16[3,128,256]{2,1,0:T(8,128)(2,1)S(1)}, bf16[3,128,256]{2,1,0:T(8,128)(2,1)S(1)}, bf16[3,128,256]{2,1,0:T(8,128)(2,1)S(1)}, bf16[3,128,256]{2,1,0:T...) custom-call(bf16[3,3,128,256]{3,2,1,0:T(8,128)(2,1)} %refs_1_.1, ...), custom_call_target="tpu_custom_call" | custom-call | flops 1000 | bytes 1000 | tf_op jit(solution)/shard_map/pack/pallas_call | solution.py:418
  1.4 2.0 %collective-permute-start = (bf16[3,128,256]{2,1,0:T(8,128)(2,1)S(1)}, bf16[3,128,256]{2,1,0:T(8,128)(2,1)S(1)}, u32[]{:S(2)}, u32[]{:S(2)}) collective-permute-start(bf16[3,128,256]{2,1,0:T(8,128)(2,1)S(1)} %get-tuple-element.36), channel_id=1, source_target_pairs={{0,28},{1,29},{2,30},{3,31},{4,8},{5,9},{6,10},{7,11},{8,4},{9,5},... | collective-permute-start | bytes 589832 | tf_op jit(solution)/shard_map/ppermute | solution.py:398
  3.4 1.6 %collective-permute-start.1 = (bf16[3,128,256]{2,1,0:T(8,128)(2,1)S(1)}, bf16[3,128,256]{2,1,0:T(8,128)(2,1)S(1)}, u32[]{:S(2)}, u32[]{:S(2)}) collective-permute-start(bf16[3,128,256]{2,1,0:T(8,128)(2,1)S(1)} %get-tuple-element.37), channel_id=1, source_target_pairs={{0,4},{1,2},{2,1},{3,7},{4,0},{5,6},{6,5},{7,3},{8,12},{9,10},{10,... | collective-permute-start | bytes 589832 | tf_op jit(solution)/shard_map/ppermute | solution.py:398
  5.0 1.7 %collective-permute-start.4 = (bf16[128,256]{1,0:T(8,128)(2,1)S(1)}, bf16[128,256]{1,0:T(8,128)(2,1)S(1)}, u32[]{:S(2)}, u32[]{:S(2)}) collective-permute-start(bf16[128,256]{1,0:T(8,128)(2,1)S(1)} %get-tuple-element.47), channel_id=1, source_target_pairs={{0,29},{1,28},{2,31},{3,30},{4,9},{5,8},{6,11},{7,10},{8,5},{9,4},... | collective-permute-start | bytes 196616 | tf_op jit(solution)/shard_map/ppermute | solution.py:398
  6.6 2.3 %collective-permute-start.5 = (bf16[128,256]{1,0:T(8,128)(2,1)S(1)}, bf16[128,256]{1,0:T(8,128)(2,1)S(1)}, u32[]{:S(2)}, u32[]{:S(2)}) collective-permute-start(bf16[128,256]{1,0:T(8,128)(2,1)S(1)} %get-tuple-element.48), channel_id=1, source_target_pairs={{0,4},{1,30},{2,29},{3,7},{4,0},{5,10},{6,9},{7,3},{8,12},{9,6},{1... | collective-permute-start | bytes 196616 | tf_op jit(solution)/shard_map/ppermute | solution.py:398
  8.9 4.5 %prepare.1 = (bf16[8,336,384]{2,1,0:T(8,128)(2,1)S(1)}, bf16[8,304,1152]{2,1,0:T(8,128)(2,1)S(1)}, bf16[8,320,304]{2,1,0:T(8,128)(2,1)S(1)}) custom-call(f32[1,8]{1,0:T(1,128)S(1)} %get-tuple-element.39.refs_0_, f32[3,8,300]{2,1,0:T(8,128)S(1)} %get-tuple-element.40.refs_1_, s32[3,1,8]{2,1,0:T(1,128)S(1)} %get-tuple-element.35.refs_2_.refs_0_, ...), custom_call_target="tpu_custom_call" | custom-call | flops 1000 | bytes 1000 | tf_op jit(solution)/shard_map/prepare/pallas_call | solution.py:437
  13.5 0.1 collective-permute-start.3
  13.6 2.5 %sample.1.refs_4_ = bf16[8,304,256]{2,1,0:T(8,128)(2,1)S(1)} custom-call(s32[3,1,8]{2,1,0:T(1,128)S(1)} %get-tuple-element.35.refs_2_.refs_0_, bf16[3,3,128,256]{3,2,1,0:T(8,128)(2,1)S(1)} %copy-done, bf16[3,128,256]{2,1,0:T(8,128)(2,1)S(1)} %collective-permute-done.refs_2_, bf16[3,128,256]{2,1,0:T(8,128)(2,1)S(1)} %collective-permute-done.2.ya_ref.refs_3_, ...), custom_call_target="tpu_custom_call" | custom-call | flops 4000000000 | bytes 40000000 | tf_op jit(solution)/shard_map/sample/pallas_call | solution.py:475
  16.1 3.9 %blend.1 = (f32[12,12,8,256]{3,2,1,0:T(8,128)S(1)}, bf16[4,20,8,256]{3,2,1,0:T(8,128)(2,1)S(1)}, bf16[4,12,8,256]{3,2,1,0:T(8,128)(2,1)S(1)}, bf16[4,4,8,256]{3,...) custom-call(s32[3,1,8]{2,1,0:T(1,128)S(1)} %get-tuple-element.35.ref, ...), custom_call_target="tpu_custom_call" | custom-call | flops 1000 | bytes 1000 | tf_op jit(solution)/shard_map/blend/pallas_call | solution.py:487
  20.0 0.6 %collective-permute-start.6 = (bf16[4,20,8,256]{3,2,1,0:T(8,128)(2,1)S(1)}, bf16[4,20,8,256]{3,2,1,0:T(8,128)(2,1)S(1)}, u32[]{:S(2)}, u32[]{:S(2)}) collective-permute-start(bf16[4,20,8,256]{3,2,1,0:T(8,128)(2,1)S(1)} %get-tuple-element.55), channel_id=1, source_target_pairs={{0,4},{1,5},{2,6},{3,7},{4,0},{5,1},{6,2},{7,3},{8,12},{9,13},{10,... | collective-permute-start | bytes 983048 | tf_op jit(solution)/shard_map/ppermute | solution.py:398
  20.5 0.2 collective-permute-start.7
  20.7 1.1 %collective-permute-done.6.xa_ref = bf16[4,20,8,256]{3,2,1,0:T(8,128)(2,1)S(1)} collective-permute-done((bf16[4,20,8,256]{3,2,1,0:T(8,128)(2,1)S(1)}, bf16[4,20,8,256]{3,2,1,0:T(8,128)(2,1)S(1)}, u32[]{:S(2)}, u32[]{:S(2)}) %collective-permute-start.6) | collective-permute-done | bytes 327712 | tf_op jit(solution)/shard_map/ppermute | solution.py:398
  21.8 0.1 relay.1
  21.9 0.1 collective-permute-start.8
  22.0 1.7 %collective-permute-start.9 = (bf16[12,4,8,256]{3,2,1,0:T(8,128)(2,1)S(1)}, bf16[12,4,8,256]{3,2,1,0:T(8,128)(2,1)S(1)}, u32[]{:S(2)}, u32[]{:S(2)}) collective-permute-start(bf16[12,4,8,256]{3,2,1,0:T(8,128)(2,1)S(1)} %get-tuple-element.60), channel_id=1, source_target_pairs={{0,4},{1,2},{2,1},{3,7},{4,0},{5,6},{6,5},{7,3},{8,12},{9,10},{10,... | collective-permute-start | bytes 589832 | tf_op jit(solution)/shard_map/ppermute | solution.py:398
  23.7 0.9 %collective-permute-start.10 = (bf16[4,4,8,256]{3,2,1,0:T(8,128)(2,1)S(1)}, bf16[4,4,8,256]{3,2,1,0:T(8,128)(2,1)S(1)}, u32[]{:S(2)}, u32[]{:S(2)}) collective-permute-start(bf16[4,4,8,256]{3,2,1,0:T(8,128)(2,1)S(1)} %get-tuple-element.63), channel_id=1, source_target_pairs={{0,29},{1,28},{2,31},{3,30},{4,9},{5,8},{6,11},{7,10},{8,5},{9,4},... | collective-permute-start | bytes 196616 | tf_op jit(solution)/shard_map/ppermute | solution.py:398
  24.5 2.7 %collective-permute-start.11 = (bf16[4,4,8,256]{3,2,1,0:T(8,128)(2,1)S(1)}, bf16[4,4,8,256]{3,2,1,0:T(8,128)(2,1)S(1)}, u32[]{:S(2)}, u32[]{:S(2)}) collective-permute-start(bf16[4,4,8,256]{3,2,1,0:T(8,128)(2,1)S(1)} %get-tuple-element.64), channel_id=1, source_target_pairs={{0,4},{1,30},{2,29},{3,7},{4,0},{5,10},{6,9},{7,3},{8,12},{9,6},{1... | collective-permute-start | bytes 196616 | tf_op jit(solution)/shard_map/ppermute | solution.py:398
  27.2 0.7 %collective-permute-done.7.xb_ref = bf16[4,12,8,256]{3,2,1,0:T(8,128)(2,1)S(1)} collective-permute-done((bf16[4,12,8,256]{3,2,1,0:T(8,128)(2,1)S(1)}, bf16[4,12,8,256]{3,2,1,0:T(8,128)(2,1)S(1)}, u32[]{:S(2)}, u32[]{:S(2)}) %collective-permute-start.7) | collective-permute-done | bytes 196640 | tf_op jit(solution)/shard_map/ppermute | solution.py:398
  27.9 1.8 %collective-permute-done.8.za_ref = bf16[12,4,8,256]{3,2,1,0:T(8,128)(2,1)S(1)} collective-permute-done((bf16[12,4,8,256]{3,2,1,0:T(8,128)(2,1)S(1)}, bf16[12,4,8,256]{3,2,1,0:T(8,128)(2,1)S(1)}, u32[]{:S(2)}, u32[]{:S(2)}) %collective-permute-start.8) | collective-permute-done | bytes 196640 | tf_op jit(solution)/shard_map/ppermute | solution.py:398
  29.7 0.1 collective-permute-done.9.zb_ref
  29.8 0.6 %gather.1 = (f32[12,12,8,256]{3,2,1,0:T(8,128)S(1)}, f32[12,12,8,128]{3,2,1,0:T(8,128)S(1)}) custom-call(f32[12,12,8,256]{3,2,1,0:T(8,128)S(1)} %get-tuple-element.53.inner_ref, f32[12,8,12]{2,1,0:T(8,128)S(1)} %get-tuple-element.54.scale_ref, bf16[4,20,8,256]{3,2,1,0:T(8,128)(2,1)S(1)} %collective-permute-done.6.xa_ref, ...), custom_call_target="tpu_custom_call" | custom-call | flops 4000000000 | bytes 40000000 | tf_op jit(solution)/shard_map/gather/pallas_call | solution.py:527
  30.4 1.7 %collective-permute-done.10.da_ref = bf16[4,4,8,256]{3,2,1,0:T(8,128)(2,1)S(1)} collective-permute-done((bf16[4,4,8,256]{3,2,1,0:T(8,128)(2,1)S(1)}, bf16[4,4,8,256]{3,2,1,0:T(8,128)(2,1)S(1)}, u32[]{:S(2)}, u32[]{:S(2)}) %collective-permute-start.10) | collective-permute-done | bytes 65568 | tf_op jit(solution)/shard_map/ppermute | solution.py:398
  32.1 0.1 collective-permute-done.11.db_ref
  32.2 0.9 %finish.1 = bf16[12,12,8,256]{3,2,1,0:T(8,128)(2,1)} custom-call(f32[12,12,8,256]{3,2,1,0:T(8,128)S(1)} %get-tuple-element.61.base_ref, f32[12,12,8,128]{3,2,1,0:T(8,128)S(1)} %get-tuple-element.62.wide_ref, bf16[4,4,8,256]{3,2,1,0:T(8,128)(2,1)S(1)} %collective-permute-done.10.da_ref, bf16[4,4,8,256]{3,2,1,0:T(8,128)(2,1)S(1)} %collective-permute-done.11.db_ref), custom_call_target="tpu_custom_call" | custom-call | flops 1000 | bytes 1000 | tf_op jit(solution)/shard_map/finish/pallas_call | solution.py:536
  (10 shorter events, 0.0 us)
Async XLA Ops:
  0.0 13.6 %copy-start = (bf16[3,3,128,256]{3,2,1,0:T(8,128)(2,1)S(1)}, bf16[3,3,128,256]{3,2,1,0:T(8,128)(2,1)}, u32[]{:S(2)}) copy-start(bf16[3,3,128,256]{3,2,1,0:T(8,128)(2,1)} %refs_1_.1) | copy-start | bytes 1769476
  1.4 12.0 %collective-permute-start = (bf16[3,128,256]{2,1,0:T(8,128)(2,1)S(1)}, bf16[3,128,256]{2,1,0:T(8,128)(2,1)S(1)}, u32[]{:S(2)}, u32[]{:S(2)}) collective-permute-start(bf16[3,128,256]{2,1,0:T(8,128)(2,1)S(1)} %get-tuple-element.36), channel_id=1, source_target_pairs={{0,28},{1,29},{2,30},{3,31},{4,8},{5,9},{6,10},{7,11},{8,4},{9,5},... | collective-permute-start | bytes 589832 | tf_op jit(solution)/shard_map/ppermute | solution.py:398
  3.4 10.1 %collective-permute-start.1 = (bf16[3,128,256]{2,1,0:T(8,128)(2,1)S(1)}, bf16[3,128,256]{2,1,0:T(8,128)(2,1)S(1)}, u32[]{:S(2)}, u32[]{:S(2)}) collective-permute-start(bf16[3,128,256]{2,1,0:T(8,128)(2,1)S(1)} %get-tuple-element.37), channel_id=1, source_target_pairs={{0,4},{1,2},{2,1},{3,7},{4,0},{5,6},{6,5},{7,3},{8,12},{9,10},{10,... | collective-permute-start | bytes 589832 | tf_op jit(solution)/shard_map/ppermute | solution.py:398
  5.0 8.5 %collective-permute-start.2 = (bf16[3,128,256]{2,1,0:T(8,128)(2,1)S(1)}, bf16[3,128,256]{2,1,0:T(8,128)(2,1)S(1)}, u32[]{:S(2)}, u32[]{:S(2)}) collective-permute-start(bf16[3,128,256]{2,1,0:T(8,128)(2,1)S(1)} %get-tuple-element.38), channel_id=1, source_target_pairs={{0,1},{1,0},{2,3},{3,2},{4,5},{5,4},{6,7},{7,6},{8,9},{9,8},{10,11... | collective-permute-start | bytes 589832 | tf_op jit(solution)/shard_map/ppermute | solution.py:398
  5.0 11.1 %collective-permute-start.4 = (bf16[128,256]{1,0:T(8,128)(2,1)S(1)}, bf16[128,256]{1,0:T(8,128)(2,1)S(1)}, u32[]{:S(2)}, u32[]{:S(2)}) collective-permute-start(bf16[128,256]{1,0:T(8,128)(2,1)S(1)} %get-tuple-element.47), channel_id=1, source_target_pairs={{0,29},{1,28},{2,31},{3,30},{4,9},{5,8},{6,11},{7,10},{8,5},{9,4},... | collective-permute-start | bytes 196616 | tf_op jit(solution)/shard_map/ppermute | solution.py:398
  6.6 9.5 %collective-permute-start.5 = (bf16[128,256]{1,0:T(8,128)(2,1)S(1)}, bf16[128,256]{1,0:T(8,128)(2,1)S(1)}, u32[]{:S(2)}, u32[]{:S(2)}) collective-permute-start(bf16[128,256]{1,0:T(8,128)(2,1)S(1)} %get-tuple-element.48), channel_id=1, source_target_pairs={{0,4},{1,30},{2,29},{3,7},{4,0},{5,10},{6,9},{7,3},{8,12},{9,6},{1... | collective-permute-start | bytes 196616 | tf_op jit(solution)/shard_map/ppermute | solution.py:398
  13.5 2.6 %collective-permute-start.3 = (bf16[5,128,256]{2,1,0:T(8,128)(2,1)S(1)}, bf16[5,128,256]{2,1,0:T(8,128)(2,1)S(1)}, u32[]{:S(2)}, u32[]{:S(2)}) collective-permute-start(bf16[5,128,256]{2,1,0:T(8,128)(2,1)S(1)} %extend.1), channel_id=1, source_target_pairs={{0,4},{1,5},{2,6},{3,7},{4,0},{5,1},{6,2},{7,3},{8,12},{9,13},{10,... | collective-permute-start | bytes 983048 | tf_op jit(solution)/shard_map/ppermute | solution.py:398
  20.0 1.8 %collective-permute-start.6 = (bf16[4,20,8,256]{3,2,1,0:T(8,128)(2,1)S(1)}, bf16[4,20,8,256]{3,2,1,0:T(8,128)(2,1)S(1)}, u32[]{:S(2)}, u32[]{:S(2)}) collective-permute-start(bf16[4,20,8,256]{3,2,1,0:T(8,128)(2,1)S(1)} %get-tuple-element.55), channel_id=1, source_target_pairs={{0,4},{1,5},{2,6},{3,7},{4,0},{5,1},{6,2},{7,3},{8,12},{9,13},{10,... | collective-permute-start | bytes 983048 | tf_op jit(solution)/shard_map/ppermute | solution.py:398
  20.5 7.4 %collective-permute-start.7 = (bf16[4,12,8,256]{3,2,1,0:T(8,128)(2,1)S(1)}, bf16[4,12,8,256]{3,2,1,0:T(8,128)(2,1)S(1)}, u32[]{:S(2)}, u32[]{:S(2)}) collective-permute-start(bf16[4,12,8,256]{3,2,1,0:T(8,128)(2,1)S(1)} %get-tuple-element.56), channel_id=1, source_target_pairs={{0,28},{1,29},{2,30},{3,31},{4,8},{5,9},{6,10},{7,11},{8,4},{9,5},... | collective-permute-start | bytes 589832 | tf_op jit(solution)/shard_map/ppermute | solution.py:398
  21.9 7.8 %collective-permute-start.8 = (bf16[12,4,8,256]{3,2,1,0:T(8,128)(2,1)S(1)}, bf16[12,4,8,256]{3,2,1,0:T(8,128)(2,1)S(1)}, u32[]{:S(2)}, u32[]{:S(2)}) collective-permute-start(bf16[12,4,8,256]{3,2,1,0:T(8,128)(2,1)S(1)} %get-tuple-element.59), channel_id=1, source_target_pairs={{0,1},{1,0},{2,3},{3,2},{4,5},{5,4},{6,7},{7,6},{8,9},{9,8},{10,11... | collective-permute-start | bytes 589832 | tf_op jit(solution)/shard_map/ppermute | solution.py:398
  22.0 7.8 %collective-permute-start.9 = (bf16[12,4,8,256]{3,2,1,0:T(8,128)(2,1)S(1)}, bf16[12,4,8,256]{3,2,1,0:T(8,128)(2,1)S(1)}, u32[]{:S(2)}, u32[]{:S(2)}) collective-permute-start(bf16[12,4,8,256]{3,2,1,0:T(8,128)(2,1)S(1)} %get-tuple-element.60), channel_id=1, source_target_pairs={{0,4},{1,2},{2,1},{3,7},{4,0},{5,6},{6,5},{7,3},{8,12},{9,10},{10,... | collective-permute-start | bytes 589832 | tf_op jit(solution)/shard_map/ppermute | solution.py:398
  23.7 8.4 %collective-permute-start.10 = (bf16[4,4,8,256]{3,2,1,0:T(8,128)(2,1)S(1)}, bf16[4,4,8,256]{3,2,1,0:T(8,128)(2,1)S(1)}, u32[]{:S(2)}, u32[]{:S(2)}) collective-permute-start(bf16[4,4,8,256]{3,2,1,0:T(8,128)(2,1)S(1)} %get-tuple-element.63), channel_id=1, source_target_pairs={{0,29},{1,28},{2,31},{3,30},{4,9},{5,8},{6,11},{7,10},{8,5},{9,4},... | collective-permute-start | bytes 196616 | tf_op jit(solution)/shard_map/ppermute | solution.py:398
  24.5 7.7 %collective-permute-start.11 = (bf16[4,4,8,256]{3,2,1,0:T(8,128)(2,1)S(1)}, bf16[4,4,8,256]{3,2,1,0:T(8,128)(2,1)S(1)}, u32[]{:S(2)}, u32[]{:S(2)}) collective-permute-start(bf16[4,4,8,256]{3,2,1,0:T(8,128)(2,1)S(1)} %get-tuple-element.64), channel_id=1, source_target_pairs={{0,4},{1,30},{2,29},{3,7},{4,0},{5,10},{6,9},{7,3},{8,12},{9,6},{1... | collective-permute-start | bytes 196616 | tf_op jit(solution)/shard_map/ppermute | solution.py:398

commit v3 on v2

--- a/solution.py
+++ b/solution.py
@@ -276,7 +276,7 @@
 
 def blend_kernel(
     sides, tile, cells_ref, side_ref, ea_ref, eb_ref, sample_ref, hot_ref, fit_ref, design_ref,
-    inner_ref, xa_ref, xb_ref, da_ref, db_ref, za_ref, zb_ref, edges, chosen, coeffs, values, acc,
+    acc, xa_ref, xb_ref, da_ref, db_ref, edges, chosen, coeffs, values,
 ):
     sx, sy = sides
     subregion, fields = side_ref.shape[1:]
@@ -320,32 +320,33 @@
     rb = odd_x * (cx + REACH)
     sa = (1 - odd_y) * (cy + REACH)
     sb = odd_y * (cy + REACH)
-    rim, in_x, in_y = REACH, pl.ds(REACH, cx), pl.ds(REACH, cy)
+    rim, in_y = REACH, pl.ds(REACH, cy)
     for l in range(acc.shape[0]):
         f = pl.ds(l * 128, 128)
         xa_ref[:, :, :, f] = acc[l, pl.ds(ra, rim)].astype(xa_ref.dtype)
         xb_ref[:, :, :, f] = acc[l, pl.ds(rb, rim), in_y].astype(xb_ref.dtype)
         for ref, s, turn in ((da_ref, sa, 0), (db_ref, sb, 1)):
             ref[:, :, :, f] = (acc[l, pl.ds(rb, rim), pl.ds(s, rim)] * paired(turn)).astype(ref.dtype)
-        for ref, s in ((za_ref, sa), (zb_ref, sb)):
-            ref[:, :, :, f] = acc[l, in_x, pl.ds(s, rim)]
-        inner_ref[:, :, :, f] = acc[l, in_x, in_y]
-
-
-def relay_kernel(za_ref, zb_ref, xa_ref, outa_ref, outb_ref):
-    odd_x, odd_y = parity()
-    cx = za_ref.shape[0]
+
+
+def relay_kernel(acc_ref, xa_ref, outa_ref, outb_ref):
+    odd_x, odd_y = parity()
+    cx = outa_ref.shape[0]
     rows = pl.ds((1 - odd_x) * (cx - REACH), REACH)
     last = xa_ref.shape[1] - REACH
-    for z_ref, out_ref, s, turn in ((za_ref, outa_ref, (1 - odd_y) * last, 0), (zb_ref, outb_ref, odd_y * last, 1)):
+    for out_ref, s, turn in ((outa_ref, (1 - odd_y) * last, 0), (outb_ref, odd_y * last, 1)):
         keep = paired(turn)
-        out_ref[...] = (z_ref[...] * keep).astype(out_ref.dtype)
-        got = xa_ref[:, pl.ds(s, REACH)].astype(jnp.float32)
-        out_ref[rows] = ((z_ref[rows] + got) * keep).astype(out_ref.dtype)
-
-
-def gather_kernel(inner_ref, scale_ref, xa_ref, xb_ref, za_ref, zb_ref, out_ref, wide_ref):
-    cx, cy, depth, fields = inner_ref.shape
+        columns = pl.ds(s, REACH)
+        for l in range(acc_ref.shape[0]):
+            f = slice(l * 128, (l + 1) * 128)
+            out_ref[:, :, :, f] = (acc_ref[l, pl.ds(REACH, cx), columns] * keep).astype(out_ref.dtype)
+            mine = acc_ref[l, pl.ds((1 - odd_x) * (cx - REACH) + REACH, REACH), columns]
+            got = xa_ref[:, columns, :, f].astype(jnp.float32)
+            out_ref[rows, :, :, f] = ((mine + got) * keep).astype(out_ref.dtype)
+
+
+def gather_kernel(acc_ref, scale_ref, xa_ref, xb_ref, za_ref, zb_ref, out_ref, wide_ref):
+    cx, cy, depth, fields = out_ref.shape
     for i in range(cx):
         columns = scale_ref[i]
         for j in range(cy):
@@ -354,7 +355,7 @@
     far, back = pl.ds((1 - odd_x) * (cx - REACH), REACH), pl.ds(odd_x * (cx - REACH), REACH)
     for f in range(0, fields, 128):
         part = slice(f, f + 128)
-        out_ref[:, :, :, part] = inner_ref[:, :, :, part] * wide_ref[...]
+        out_ref[:, :, :, part] = acc_ref[f // 128, REACH : REACH + cx, REACH : REACH + cy] * wide_ref[...]
         got = xa_ref[:, REACH : REACH + cy, :, part].astype(jnp.float32)
         out_ref[far, :, :, part] = out_ref[far, :, :, part] + got * wide_ref[far]
         got = xb_ref[:, :, :, part].astype(jnp.float32)
@@ -484,25 +485,22 @@
     )(cells, node_values, from_xb, from_ya, from_yb, hot)
 
     block = lambda *dims, kind=kind: shape(dims + (depth, fields), kind)
-    inner, xa, xb, da, db, za, zb = pl.pallas_call(
+    total, xa, xb, da, db = pl.pallas_call(
         lambda *refs: blend_kernel((sx, sy), (cx, cy), *refs),
         out_shape=(
-            block(cx, cy, kind=full),
+            shape((halves, cx + 2 * REACH, cy + 2 * REACH, depth, 128), full),
             block(REACH, cy + 2 * REACH),
             block(REACH, cy),
             block(REACH, REACH),
             block(REACH, REACH),
-            block(cx, REACH, kind=full),
-            block(cx, REACH, kind=full),
         ),
         in_specs=[SMEM] + [VMEM] * 7,
-        out_specs=(VMEM,) * 7,
+        out_specs=(VMEM,) * 5,
         scratch_shapes=[
             pltpu.VMEM((2, sy + 2, subregion, fields), kind),
             pltpu.VMEM((patches, padded, fields), kind),
             pltpu.VMEM((patches, unknowns, fields), kind),
             pltpu.VMEM((patches, len(SPOTS) * LAYERS, fields), full),
-            pltpu.VMEM((halves, cx + 2 * REACH, cy + 2 * REACH, depth, 128), full),
         ],
         compiler_params=params(32),
         cost_estimate=SMALL,
@@ -516,12 +514,12 @@
     za, zb = pl.pallas_call(
         relay_kernel,
         out_shape=(block(cx, REACH), block(cx, REACH)),
-        in_specs=[VMEM] * 3,
+        in_specs=[VMEM] * 2,
         out_specs=(VMEM, VMEM),
         compiler_params=params(8),
         cost_estimate=SMALL,
         name="relay",
-    )(za, zb, got_xa)
+    )(total, got_xa)
     got_za = send_y(za, 0)
     got_zb = send_y(zb, 1)
     base, wide = pl.pallas_call(
@@ -532,7 +530,7 @@
         compiler_params=params(12),
         cost_estimate=LARGE,
         name="gather",
-    )(inner, scale, got_xa, got_xb, got_za, got_zb)
+    )(total, scale, got_xa, got_xb, got_za, got_zb)
     return pl.pallas_call(
         finish_kernel,
         out_shape=block(cx, cy),

time: 33.3 us -> 33.1 us (level)
  no operation moved by 1% of the time
where the time goes in v3:
time: 33.1 us; the launch traced here: 32.9 us
  Pallas kernels  13.8 us (42%)
  starting transfers between devices  13.6 us (41%)
  waiting for transfers between devices  5.46 us (16%)
    ppermute x12, starting transfers between devices, send(): lax.ppermute(block, ('gx', 'gy'), routes(across, along, turn_x, turn_y))  13.6 us
    ppermute x12, waiting for transfers between devices, send(): lax.ppermute(block, ('gx', 'gy'), routes(across, along, turn_x, turn_y))  5.46 us
    pallas_call x1, Pallas kernels, local(): pl.pallas_call(lambda *refs: prepare_kernel((sx, sy), subregion, (cx, cy)...  4.49 us
    pallas_call x1, Pallas kernels, local(): pl.pallas_call(lambda *refs: blend_kernel((sx, sy), (cx, cy), *refs), out...  3.75 us
    pallas_call x1, Pallas kernels, local(): pl.pallas_call(lambda *refs: sample_kernel((cx, cy), *refs), out_shape=sh...  2.46 us
    pallas_call x1, Pallas kernels, local(): pl.pallas_call(lambda *refs: pack_kernel(len(plain), *refs), out_shape=(l...  1.41 us
    pallas_call x1, Pallas kernels, local(): pl.pallas_call(finish_kernel, out_shape=block(cx, cy), in_specs=[VMEM] *...  0.93 us
  transfers between devices with their start and end apart: 12, of which 6 were waited for; matrix products, arithmetic and copies ran while one was open for 0% of the time, Pallas kernels for 23%

profile of v3, /device:TPU:8, one launch (start us, length us, event | category | flops | bytes accessed | tf_op | source)
XLA Modules:
  0.0 32.9 jit_solution(6227717756525004158)
XLA Ops:
  0.0 1.4 %pack.1 = (bf16[3,128,256]{2,1,0:T(8,128)(2,1)S(1)}, bf16[3,128,256]{2,1,0:T(8,128)(2,1)S(1)}, bf16[3,128,256]{2,1,0:T(8,128)(2,1)S(1)}, bf16[3,128,256]{2,1,0:T...) custom-call(bf16[3,3,128,256]{3,2,1,0:T(8,128)(2,1)} %refs_1_.1, ...), custom_call_target="tpu_custom_call" | custom-call | flops 1000 | bytes 1000 | tf_op jit(solution)/shard_map/pack/pallas_call | solution.py:419
  1.4 2.0 %collective-permute-start = (bf16[3,128,256]{2,1,0:T(8,128)(2,1)S(1)}, bf16[3,128,256]{2,1,0:T(8,128)(2,1)S(1)}, u32[]{:S(2)}, u32[]{:S(2)}) collective-permute-start(bf16[3,128,256]{2,1,0:T(8,128)(2,1)S(1)} %get-tuple-element.34), channel_id=1, source_target_pairs={{0,28},{1,29},{2,30},{3,31},{4,8},{5,9},{6,10},{7,11},{8,4},{9,5},... | collective-permute-start | bytes 589832 | tf_op jit(solution)/shard_map/ppermute | solution.py:399
  3.4 1.6 %collective-permute-start.1 = (bf16[3,128,256]{2,1,0:T(8,128)(2,1)S(1)}, bf16[3,128,256]{2,1,0:T(8,128)(2,1)S(1)}, u32[]{:S(2)}, u32[]{:S(2)}) collective-permute-start(bf16[3,128,256]{2,1,0:T(8,128)(2,1)S(1)} %get-tuple-element.35), channel_id=1, source_target_pairs={{0,4},{1,2},{2,1},{3,7},{4,0},{5,6},{6,5},{7,3},{8,12},{9,10},{10,... | collective-permute-start | bytes 589832 | tf_op jit(solution)/shard_map/ppermute | solution.py:399
  5.0 1.7 %collective-permute-start.4 = (bf16[128,256]{1,0:T(8,128)(2,1)S(1)}, bf16[128,256]{1,0:T(8,128)(2,1)S(1)}, u32[]{:S(2)}, u32[]{:S(2)}) collective-permute-start(bf16[128,256]{1,0:T(8,128)(2,1)S(1)} %get-tuple-element.45), channel_id=1, source_target_pairs={{0,29},{1,28},{2,31},{3,30},{4,9},{5,8},{6,11},{7,10},{8,5},{9,4},... | collective-permute-start | bytes 196616 | tf_op jit(solution)/shard_map/ppermute | solution.py:399
  6.6 2.3 %collective-permute-start.5 = (bf16[128,256]{1,0:T(8,128)(2,1)S(1)}, bf16[128,256]{1,0:T(8,128)(2,1)S(1)}, u32[]{:S(2)}, u32[]{:S(2)}) collective-permute-start(bf16[128,256]{1,0:T(8,128)(2,1)S(1)} %get-tuple-element.46), channel_id=1, source_target_pairs={{0,4},{1,30},{2,29},{3,7},{4,0},{5,10},{6,9},{7,3},{8,12},{9,6},{1... | collective-permute-start | bytes 196616 | tf_op jit(solution)/shard_map/ppermute | solution.py:399
  8.9 4.5 %prepare.1 = (bf16[8,336,384]{2,1,0:T(8,128)(2,1)S(1)}, bf16[8,304,1152]{2,1,0:T(8,128)(2,1)S(1)}, bf16[8,320,304]{2,1,0:T(8,128)(2,1)S(1)}) custom-call(f32[1,8]{1,0:T(1,128)S(1)} %get-tuple-element.37.refs_0_, f32[3,8,300]{2,1,0:T(8,128)S(1)} %get-tuple-element.38.refs_1_, s32[3,1,8]{2,1,0:T(1,128)S(1)} %get-tuple-element.33.refs_2_.refs_0_, ...), custom_call_target="tpu_custom_call" | custom-call | flops 1000 | bytes 1000 | tf_op jit(solution)/shard_map/prepare/pallas_call | solution.py:438
  13.5 0.1 collective-permute-start.3
  13.6 2.5 %sample.1.refs_4_ = bf16[8,304,256]{2,1,0:T(8,128)(2,1)S(1)} custom-call(s32[3,1,8]{2,1,0:T(1,128)S(1)} %get-tuple-element.33.refs_2_.refs_0_, bf16[3,3,128,256]{3,2,1,0:T(8,128)(2,1)S(1)} %copy-done, bf16[3,128,256]{2,1,0:T(8,128)(2,1)S(1)} %collective-permute-done.refs_2_, bf16[3,128,256]{2,1,0:T(8,128)(2,1)S(1)} %collective-permute-done.2.ya_ref.refs_3_, ...), custom_call_target="tpu_custom_call" | custom-call | flops 4000000000 | bytes 40000000 | tf_op jit(solution)/shard_map/sample/pallas_call | solution.py:476
  16.1 3.8 %blend.1 = (f32[2,20,20,8,128]{4,3,2,1,0:T(8,128)S(1)}, bf16[4,20,8,256]{3,2,1,0:T(8,128)(2,1)S(1)}, bf16[4,12,8,256]{3,2,1,0:T(8,128)(2,1)S(1)}, bf16[4,4,8,256...) custom-call(s32[3,1,8]{2,1,0:T(1,128)S(1)} %get-tuple-element.33.refs_2_.refs_0_, ...), custom_call_target="tpu_custom_call" | custom-call | flops 1000 | bytes 1000 | tf_op jit(solution)/shard_map/blend/pallas_call | solution.py:488
  19.9 0.5 %collective-permute-start.6 = (bf16[4,20,8,256]{3,2,1,0:T(8,128)(2,1)S(1)}, bf16[4,20,8,256]{3,2,1,0:T(8,128)(2,1)S(1)}, u32[]{:S(2)}, u32[]{:S(2)}) collective-permute-start(bf16[4,20,8,256]{3,2,1,0:T(8,128)(2,1)S(1)} %get-tuple-element.53), channel_id=1, source_target_pairs={{0,4},{1,5},{2,6},{3,7},{4,0},{5,1},{6,2},{7,3},{8,12},{9,13},{10,... | collective-permute-start | bytes 983048 | tf_op jit(solution)/shard_map/ppermute | solution.py:399
  20.4 0.2 collective-permute-start.7
  20.5 1.1 %collective-permute-done.6.xa_ref = bf16[4,20,8,256]{3,2,1,0:T(8,128)(2,1)S(1)} collective-permute-done((bf16[4,20,8,256]{3,2,1,0:T(8,128)(2,1)S(1)}, bf16[4,20,8,256]{3,2,1,0:T(8,128)(2,1)S(1)}, u32[]{:S(2)}, u32[]{:S(2)}) %collective-permute-start.6) | collective-permute-done | bytes 327712 | tf_op jit(solution)/shard_map/ppermute | solution.py:399
  21.6 0.1 relay.1
  21.7 0.1 collective-permute-start.8
  21.8 1.7 %collective-permute-start.9 = (bf16[12,4,8,256]{3,2,1,0:T(8,128)(2,1)S(1)}, bf16[12,4,8,256]{3,2,1,0:T(8,128)(2,1)S(1)}, u32[]{:S(2)}, u32[]{:S(2)}) collective-permute-start(bf16[12,4,8,256]{3,2,1,0:T(8,128)(2,1)S(1)} %get-tuple-element.56), channel_id=1, source_target_pairs={{0,4},{1,2},{2,1},{3,7},{4,0},{5,6},{6,5},{7,3},{8,12},{9,10},{10,... | collective-permute-start | bytes 589832 | tf_op jit(solution)/shard_map/ppermute | solution.py:399
  23.5 0.9 %collective-permute-start.10 = (bf16[4,4,8,256]{3,2,1,0:T(8,128)(2,1)S(1)}, bf16[4,4,8,256]{3,2,1,0:T(8,128)(2,1)S(1)}, u32[]{:S(2)}, u32[]{:S(2)}) collective-permute-start(bf16[4,4,8,256]{3,2,1,0:T(8,128)(2,1)S(1)} %get-tuple-element.59), channel_id=1, source_target_pairs={{0,29},{1,28},{2,31},{3,30},{4,9},{5,8},{6,11},{7,10},{8,5},{9,4},... | collective-permute-start | bytes 196616 | tf_op jit(solution)/shard_map/ppermute | solution.py:399
  24.4 2.6 %collective-permute-start.11 = (bf16[4,4,8,256]{3,2,1,0:T(8,128)(2,1)S(1)}, bf16[4,4,8,256]{3,2,1,0:T(8,128)(2,1)S(1)}, u32[]{:S(2)}, u32[]{:S(2)}) collective-permute-start(bf16[4,4,8,256]{3,2,1,0:T(8,128)(2,1)S(1)} %get-tuple-element.60), channel_id=1, source_target_pairs={{0,4},{1,30},{2,29},{3,7},{4,0},{5,10},{6,9},{7,3},{8,12},{9,6},{1... | collective-permute-start | bytes 196616 | tf_op jit(solution)/shard_map/ppermute | solution.py:399
  27.0 0.7 %collective-permute-done.7.xb_ref = bf16[4,12,8,256]{3,2,1,0:T(8,128)(2,1)S(1)} collective-permute-done((bf16[4,12,8,256]{3,2,1,0:T(8,128)(2,1)S(1)}, bf16[4,12,8,256]{3,2,1,0:T(8,128)(2,1)S(1)}, u32[]{:S(2)}, u32[]{:S(2)}) %collective-permute-start.7) | collective-permute-done | bytes 196640 | tf_op jit(solution)/shard_map/ppermute | solution.py:399
  27.7 1.8 %collective-permute-done.8.za_ref = bf16[12,4,8,256]{3,2,1,0:T(8,128)(2,1)S(1)} collective-permute-done((bf16[12,4,8,256]{3,2,1,0:T(8,128)(2,1)S(1)}, bf16[12,4,8,256]{3,2,1,0:T(8,128)(2,1)S(1)}, u32[]{:S(2)}, u32[]{:S(2)}) %collective-permute-start.8) | collective-permute-done | bytes 196640 | tf_op jit(solution)/shard_map/ppermute | solution.py:399
  29.5 0.1 collective-permute-done.9.zb_ref
  29.6 0.6 %gather.1 = (f32[12,12,8,256]{3,2,1,0:T(8,128)S(1)}, f32[12,12,8,128]{3,2,1,0:T(8,128)S(1)}) custom-call(f32[2,20,20,8,128]{4,3,2,1,0:T(8,128)S(1)} %get-tuple-element.51.acc_ref, f32[12,8,12]{2,1,0:T(8,128)S(1)} %get-tuple-element.52.scale_ref, bf16[4,20,8,256]{3,2,1,0:T(8,128)(2,1)S(1)} %collective-permute-done.6.xa_ref, ...), custom_call_target="tpu_custom_call" | custom-call | flops 4000000000 | bytes 40000000 | tf_op jit(solution)/shard_map/gather/pallas_call | solution.py:525
  30.2 1.7 %collective-permute-done.10.da_ref = bf16[4,4,8,256]{3,2,1,0:T(8,128)(2,1)S(1)} collective-permute-done((bf16[4,4,8,256]{3,2,1,0:T(8,128)(2,1)S(1)}, bf16[4,4,8,256]{3,2,1,0:T(8,128)(2,1)S(1)}, u32[]{:S(2)}, u32[]{:S(2)}) %collective-permute-start.10) | collective-permute-done | bytes 65568 | tf_op jit(solution)/shard_map/ppermute | solution.py:399
  31.9 0.1 collective-permute-done.11.db_ref
  32.0 0.9 %finish.1 = bf16[12,12,8,256]{3,2,1,0:T(8,128)(2,1)} custom-call(f32[12,12,8,256]{3,2,1,0:T(8,128)S(1)} %get-tuple-element.57.base_ref, f32[12,12,8,128]{3,2,1,0:T(8,128)S(1)} %get-tuple-element.58.wide_ref, bf16[4,4,8,256]{3,2,1,0:T(8,128)(2,1)S(1)} %collective-permute-done.10.da_ref, bf16[4,4,8,256]{3,2,1,0:T(8,128)(2,1)S(1)} %collective-permute-done.11.db_ref), custom_call_target="tpu_custom_call" | custom-call | flops 1000 | bytes 1000 | tf_op jit(solution)/shard_map/finish/pallas_call | solution.py:534
  (10 shorter events, 0.0 us)
Async XLA Ops:
  0.0 13.6 %copy-start = (bf16[3,3,128,256]{3,2,1,0:T(8,128)(2,1)S(1)}, bf16[3,3,128,256]{3,2,1,0:T(8,128)(2,1)}, u32[]{:S(2)}) copy-start(bf16[3,3,128,256]{3,2,1,0:T(8,128)(2,1)} %refs_1_.1) | copy-start | bytes 1769476
  1.4 12.0 %collective-permute-start = (bf16[3,128,256]{2,1,0:T(8,128)(2,1)S(1)}, bf16[3,128,256]{2,1,0:T(8,128)(2,1)S(1)}, u32[]{:S(2)}, u32[]{:S(2)}) collective-permute-start(bf16[3,128,256]{2,1,0:T(8,128)(2,1)S(1)} %get-tuple-element.34), channel_id=1, source_target_pairs={{0,28},{1,29},{2,30},{3,31},{4,8},{5,9},{6,10},{7,11},{8,4},{9,5},... | collective-permute-start | bytes 589832 | tf_op jit(solution)/shard_map/ppermute | solution.py:399
  3.4 10.1 %collective-permute-start.1 = (bf16[3,128,256]{2,1,0:T(8,128)(2,1)S(1)}, bf16[3,128,256]{2,1,0:T(8,128)(2,1)S(1)}, u32[]{:S(2)}, u32[]{:S(2)}) collective-permute-start(bf16[3,128,256]{2,1,0:T(8,128)(2,1)S(1)} %get-tuple-element.35), channel_id=1, source_target_pairs={{0,4},{1,2},{2,1},{3,7},{4,0},{5,6},{6,5},{7,3},{8,12},{9,10},{10,... | collective-permute-start | bytes 589832 | tf_op jit(solution)/shard_map/ppermute | solution.py:399
  5.0 8.5 %collective-permute-start.2 = (bf16[3,128,256]{2,1,0:T(8,128)(2,1)S(1)}, bf16[3,128,256]{2,1,0:T(8,128)(2,1)S(1)}, u32[]{:S(2)}, u32[]{:S(2)}) collective-permute-start(bf16[3,128,256]{2,1,0:T(8,128)(2,1)S(1)} %get-tuple-element.36), channel_id=1, source_target_pairs={{0,1},{1,0},{2,3},{3,2},{4,5},{5,4},{6,7},{7,6},{8,9},{9,8},{10,11... | collective-permute-start | bytes 589832 | tf_op jit(solution)/shard_map/ppermute | solution.py:399
  5.0 11.1 %collective-permute-start.4 = (bf16[128,256]{1,0:T(8,128)(2,1)S(1)}, bf16[128,256]{1,0:T(8,128)(2,1)S(1)}, u32[]{:S(2)}, u32[]{:S(2)}) collective-permute-start(bf16[128,256]{1,0:T(8,128)(2,1)S(1)} %get-tuple-element.45), channel_id=1, source_target_pairs={{0,29},{1,28},{2,31},{3,30},{4,9},{5,8},{6,11},{7,10},{8,5},{9,4},... | collective-permute-start | bytes 196616 | tf_op jit(solution)/shard_map/ppermute | solution.py:399
  6.6 9.5 %collective-permute-start.5 = (bf16[128,256]{1,0:T(8,128)(2,1)S(1)}, bf16[128,256]{1,0:T(8,128)(2,1)S(1)}, u32[]{:S(2)}, u32[]{:S(2)}) collective-permute-start(bf16[128,256]{1,0:T(8,128)(2,1)S(1)} %get-tuple-element.46), channel_id=1, source_target_pairs={{0,4},{1,30},{2,29},{3,7},{4,0},{5,10},{6,9},{7,3},{8,12},{9,6},{1... | collective-permute-start | bytes 196616 | tf_op jit(solution)/shard_map/ppermute | solution.py:399
  13.5 2.6 %collective-permute-start.3 = (bf16[5,128,256]{2,1,0:T(8,128)(2,1)S(1)}, bf16[5,128,256]{2,1,0:T(8,128)(2,1)S(1)}, u32[]{:S(2)}, u32[]{:S(2)}) collective-permute-start(bf16[5,128,256]{2,1,0:T(8,128)(2,1)S(1)} %extend.1), channel_id=1, source_target_pairs={{0,4},{1,5},{2,6},{3,7},{4,0},{5,1},{6,2},{7,3},{8,12},{9,13},{10,... | collective-permute-start | bytes 983048 | tf_op jit(solution)/shard_map/ppermute | solution.py:399
  19.9 1.8 %collective-permute-start.6 = (bf16[4,20,8,256]{3,2,1,0:T(8,128)(2,1)S(1)}, bf16[4,20,8,256]{3,2,1,0:T(8,128)(2,1)S(1)}, u32[]{:S(2)}, u32[]{:S(2)}) collective-permute-start(bf16[4,20,8,256]{3,2,1,0:T(8,128)(2,1)S(1)} %get-tuple-element.53), channel_id=1, source_target_pairs={{0,4},{1,5},{2,6},{3,7},{4,0},{5,1},{6,2},{7,3},{8,12},{9,13},{10,... | collective-permute-start | bytes 983048 | tf_op jit(solution)/shard_map/ppermute | solution.py:399
  20.4 7.4 %collective-permute-start.7 = (bf16[4,12,8,256]{3,2,1,0:T(8,128)(2,1)S(1)}, bf16[4,12,8,256]{3,2,1,0:T(8,128)(2,1)S(1)}, u32[]{:S(2)}, u32[]{:S(2)}) collective-permute-start(bf16[4,12,8,256]{3,2,1,0:T(8,128)(2,1)S(1)} %get-tuple-element.54), channel_id=1, source_target_pairs={{0,28},{1,29},{2,30},{3,31},{4,8},{5,9},{6,10},{7,11},{8,4},{9,5},... | collective-permute-start | bytes 589832 | tf_op jit(solution)/shard_map/ppermute | solution.py:399
  21.7 7.8 %collective-permute-start.8 = (bf16[12,4,8,256]{3,2,1,0:T(8,128)(2,1)S(1)}, bf16[12,4,8,256]{3,2,1,0:T(8,128)(2,1)S(1)}, u32[]{:S(2)}, u32[]{:S(2)}) collective-permute-start(bf16[12,4,8,256]{3,2,1,0:T(8,128)(2,1)S(1)} %get-tuple-element.55), channel_id=1, source_target_pairs={{0,1},{1,0},{2,3},{3,2},{4,5},{5,4},{6,7},{7,6},{8,9},{9,8},{10,11... | collective-permute-start | bytes 589832 | tf_op jit(solution)/shard_map/ppermute | solution.py:399
  21.8 7.8 %collective-permute-start.9 = (bf16[12,4,8,256]{3,2,1,0:T(8,128)(2,1)S(1)}, bf16[12,4,8,256]{3,2,1,0:T(8,128)(2,1)S(1)}, u32[]{:S(2)}, u32[]{:S(2)}) collective-permute-start(bf16[12,4,8,256]{3,2,1,0:T(8,128)(2,1)S(1)} %get-tuple-element.56), channel_id=1, source_target_pairs={{0,4},{1,2},{2,1},{3,7},{4,0},{5,6},{6,5},{7,3},{8,12},{9,10},{10,... | collective-permute-start | bytes 589832 | tf_op jit(solution)/shard_map/ppermute | solution.py:399
  23.5 8.4 %collective-permute-start.10 = (bf16[4,4,8,256]{3,2,1,0:T(8,128)(2,1)S(1)}, bf16[4,4,8,256]{3,2,1,0:T(8,128)(2,1)S(1)}, u32[]{:S(2)}, u32[]{:S(2)}) collective-permute-start(bf16[4,4,8,256]{3,2,1,0:T(8,128)(2,1)S(1)} %get-tuple-element.59), channel_id=1, source_target_pairs={{0,29},{1,28},{2,31},{3,30},{4,9},{5,8},{6,11},{7,10},{8,5},{9,4},... | collective-permute-start | bytes 196616 | tf_op jit(solution)/shard_map/ppermute | solution.py:399
  24.4 7.6 %collective-permute-start.11 = (bf16[4,4,8,256]{3,2,1,0:T(8,128)(2,1)S(1)}, bf16[4,4,8,256]{3,2,1,0:T(8,128)(2,1)S(1)}, u32[]{:S(2)}, u32[]{:S(2)}) collective-permute-start(bf16[4,4,8,256]{3,2,1,0:T(8,128)(2,1)S(1)} %get-tuple-element.60), channel_id=1, source_target_pairs={{0,4},{1,30},{2,29},{3,7},{4,0},{5,10},{6,9},{7,3},{8,12},{9,6},{1... | collective-permute-start | bytes 196616 | tf_op jit(solution)/shard_map/ppermute | solution.py:399

commit v4 on v3

--- a/solution.py
+++ b/solution.py
@@ -113,14 +113,17 @@
     copy = pltpu.make_async_copy(far_ref, near_ref, sem)
     copy.start()
     choose(sides, subregion, tile, cells_ref, valid_ref, nodes_ref, hot_ref, places)
-    design_kernel(slots, unknowns, radius_ref, xyz_ref, design_ref, *scratch)
-    copy.wait()
-    spread(near_ref, split)
-    for p in range(patches):
+
+    def also(p):
+        if p == 0:
+            copy.wait()
+            spread(near_ref, split)
         turn(p, split, fit_ref, slots)
 
-
-def design_kernel(nodes, unknowns, radius_ref, xyz_ref, design_ref, pos, ax, by, ax2, bc, bm, bl, far):
+    design_kernel(slots, unknowns, radius_ref, xyz_ref, design_ref, also, *scratch)
+
+
+def design_kernel(nodes, unknowns, radius_ref, xyz_ref, design_ref, also, pos, ax, by, ax2, bc, bm, bl, far):
     patches = design_ref.shape[0]
     lanes = design_ref.shape[2]
     tile = (2 * LAYERS, lanes)
@@ -199,13 +202,14 @@
 
     for p in range(patches):
         patch(p, p % LOOKS)
+        also(p)
 
 
 def spread(fit_ref, wide):
     slots, patches, unknowns = fit_ref.shape
     for c in range(0, unknowns, 128):
         width = min(128, unknowns - c)
-        wide[c // 128, :, :width] = fit_ref[:, :, c : c + width].astype(jnp.float32).reshape(slots * patches, width)
+        wide[c // 128, 0 : slots * patches, :width] = fit_ref[:, :, c : c + width].astype(jnp.float32).reshape(slots * patches, width)
 
 
 def turn(p, wide, fit, slots):
@@ -446,7 +450,7 @@
         out_specs=(VMEM,) * 3,
         scratch_shapes=[
             pltpu.VMEM(far.shape, kind),
-            pltpu.VMEM((lanes // 128, slots * patches, 128), full),
+            pltpu.VMEM((lanes // 128, padded * patches, 128), full),
             pltpu.VMEM((2, patches, up(padded, 128)), full),
             pltpu.SemaphoreType.DMA,
             pltpu.VMEM((3, patches, lanes), full),
@@ -488,7 +492,7 @@
     total, xa, xb, da, db = pl.pallas_call(
         lambda *refs: blend_kernel((sx, sy), (cx, cy), *refs),
         out_shape=(
-            shape((halves, cx + 2 * REACH, cy + 2 * REACH, depth, 128), full),
+            shape((halves, cx + 2 * REACH + 1, cy + 2 * REACH, depth, 128), full),
             block(REACH, cy + 2 * REACH),
             block(REACH, cy),
             block(REACH, REACH),

time: 33.1 us -> 33.1 us (level)
  no operation moved by 1% of the time
where the time goes in v4:
time: 33.1 us; the launch traced here: 32.9 us
  Pallas kernels  13.7 us (41%)
  starting transfers between devices  13.6 us (41%)
  waiting for transfers between devices  5.51 us (17%)
    ppermute x12, starting transfers between devices, send(): lax.ppermute(block, ('gx', 'gy'), routes(across, along, turn_x, turn_y))  13.6 us
    ppermute x12, waiting for transfers between devices, send(): lax.ppermute(block, ('gx', 'gy'), routes(across, along, turn_x, turn_y))  5.51 us
    pallas_call x1, Pallas kernels, local(): pl.pallas_call(lambda *refs: prepare_kernel((sx, sy), subregion, (cx, cy)...  4.44 us
    pallas_call x1, Pallas kernels, local(): pl.pallas_call(lambda *refs: blend_kernel((sx, sy), (cx, cy), *refs), out...  3.75 us
    pallas_call x1, Pallas kernels, local(): pl.pallas_call(lambda *refs: sample_kernel((cx, cy), *refs), out_shape=sh...  2.46 us
    pallas_call x1, Pallas kernels, local(): pl.pallas_call(lambda *refs: pack_kernel(len(plain), *refs), out_shape=(l...  1.41 us
    pallas_call x1, Pallas kernels, local(): pl.pallas_call(finish_kernel, out_shape=block(cx, cy), in_specs=[VMEM] *...  0.93 us
  transfers between devices with their start and end apart: 12, of which 6 were waited for; matrix products, arithmetic and copies ran while one was open for 0% of the time, Pallas kernels for 23%

profile of v4, /device:TPU:8, one launch (start us, length us, event | category | flops | bytes accessed | tf_op | source)
XLA Modules:
  0.0 32.9 jit_solution(5000447709526755488)
XLA Ops:
  0.0 1.4 %pack.1 = (bf16[3,128,256]{2,1,0:T(8,128)(2,1)S(1)}, bf16[3,128,256]{2,1,0:T(8,128)(2,1)S(1)}, bf16[3,128,256]{2,1,0:T(8,128)(2,1)S(1)}, bf16[3,128,256]{2,1,0:T...) custom-call(bf16[3,3,128,256]{3,2,1,0:T(8,128)(2,1)} %refs_1_.1, ...), custom_call_target="tpu_custom_call" | custom-call | flops 1000 | bytes 1000 | tf_op jit(solution)/shard_map/pack/pallas_call | solution.py:423
  1.4 2.0 %collective-permute-start = (bf16[3,128,256]{2,1,0:T(8,128)(2,1)S(1)}, bf16[3,128,256]{2,1,0:T(8,128)(2,1)S(1)}, u32[]{:S(2)}, u32[]{:S(2)}) collective-permute-start(bf16[3,128,256]{2,1,0:T(8,128)(2,1)S(1)} %get-tuple-element.34), channel_id=1, source_target_pairs={{0,28},{1,29},{2,30},{3,31},{4,8},{5,9},{6,10},{7,11},{8,4},{9,5},... | collective-permute-start | bytes 589832 | tf_op jit(solution)/shard_map/ppermute | solution.py:403
  3.4 1.6 %collective-permute-start.1 = (bf16[3,128,256]{2,1,0:T(8,128)(2,1)S(1)}, bf16[3,128,256]{2,1,0:T(8,128)(2,1)S(1)}, u32[]{:S(2)}, u32[]{:S(2)}) collective-permute-start(bf16[3,128,256]{2,1,0:T(8,128)(2,1)S(1)} %get-tuple-element.35), channel_id=1, source_target_pairs={{0,4},{1,2},{2,1},{3,7},{4,0},{5,6},{6,5},{7,3},{8,12},{9,10},{10,... | collective-permute-start | bytes 589832 | tf_op jit(solution)/shard_map/ppermute | solution.py:403
  5.0 1.7 %collective-permute-start.4 = (bf16[128,256]{1,0:T(8,128)(2,1)S(1)}, bf16[128,256]{1,0:T(8,128)(2,1)S(1)}, u32[]{:S(2)}, u32[]{:S(2)}) collective-permute-start(bf16[128,256]{1,0:T(8,128)(2,1)S(1)} %get-tuple-element.45), channel_id=1, source_target_pairs={{0,29},{1,28},{2,31},{3,30},{4,9},{5,8},{6,11},{7,10},{8,5},{9,4},... | collective-permute-start | bytes 196616 | tf_op jit(solution)/shard_map/ppermute | solution.py:403
  6.6 2.3 %collective-permute-start.5 = (bf16[128,256]{1,0:T(8,128)(2,1)S(1)}, bf16[128,256]{1,0:T(8,128)(2,1)S(1)}, u32[]{:S(2)}, u32[]{:S(2)}) collective-permute-start(bf16[128,256]{1,0:T(8,128)(2,1)S(1)} %get-tuple-element.46), channel_id=1, source_target_pairs={{0,4},{1,30},{2,29},{3,7},{4,0},{5,10},{6,9},{7,3},{8,12},{9,6},{1... | collective-permute-start | bytes 196616 | tf_op jit(solution)/shard_map/ppermute | solution.py:403
  8.9 4.4 %prepare.1 = (bf16[8,336,384]{2,1,0:T(8,128)(2,1)S(1)}, bf16[8,304,1152]{2,1,0:T(8,128)(2,1)S(1)}, bf16[8,320,304]{2,1,0:T(8,128)(2,1)S(1)}) custom-call(f32[1,8]{1,0:T(1,128)S(1)} %get-tuple-element.37.refs_0_, f32[3,8,300]{2,1,0:T(8,128)S(1)} %get-tuple-element.38.refs_1_, s32[3,1,8]{2,1,0:T(1,128)S(1)} %get-tuple-element.33.refs_2_.refs_0_, ...), custom_call_target="tpu_custom_call" | custom-call | flops 1000 | bytes 1000 | tf_op jit(solution)/shard_map/prepare/pallas_call | solution.py:442
  13.5 0.1 collective-permute-start.3
  13.6 2.5 %sample.1.refs_4_ = bf16[8,304,256]{2,1,0:T(8,128)(2,1)S(1)} custom-call(s32[3,1,8]{2,1,0:T(1,128)S(1)} %get-tuple-element.33.refs_2_.refs_0_, bf16[3,3,128,256]{3,2,1,0:T(8,128)(2,1)S(1)} %copy-done, bf16[3,128,256]{2,1,0:T(8,128)(2,1)S(1)} %collective-permute-done.refs_2_, bf16[3,128,256]{2,1,0:T(8,128)(2,1)S(1)} %collective-permute-done.2.ya_ref.refs_3_, ...), custom_call_target="tpu_custom_call" | custom-call | flops 4000000000 | bytes 40000000 | tf_op jit(solution)/shard_map/sample/pallas_call | solution.py:480
  16.0 3.7 %blend.1 = (f32[2,21,20,8,128]{4,3,2,1,0:T(8,128)S(1)}, bf16[4,20,8,256]{3,2,1,0:T(8,128)(2,1)S(1)}, bf16[4,12,8,256]{3,2,1,0:T(8,128)(2,1)S(1)}, bf16[4,4,8,256...) custom-call(s32[3,1,8]{2,1,0:T(1,128)S(1)} %get-tuple-element.33.refs_2_.refs_0_, ...), custom_call_target="tpu_custom_call" | custom-call | flops 1000 | bytes 1000 | tf_op jit(solution)/shard_map/blend/pallas_call | solution.py:492
  19.8 0.5 %collective-permute-start.6 = (bf16[4,20,8,256]{3,2,1,0:T(8,128)(2,1)S(1)}, bf16[4,20,8,256]{3,2,1,0:T(8,128)(2,1)S(1)}, u32[]{:S(2)}, u32[]{:S(2)}) collective-permute-start(bf16[4,20,8,256]{3,2,1,0:T(8,128)(2,1)S(1)} %get-tuple-element.53), channel_id=1, source_target_pairs={{0,4},{1,5},{2,6},{3,7},{4,0},{5,1},{6,2},{7,3},{8,12},{9,13},{10,... | collective-permute-start | bytes 983048 | tf_op jit(solution)/shard_map/ppermute | solution.py:403
  20.3 0.2 collective-permute-start.7
  20.5 1.1 %collective-permute-done.6.xa_ref = bf16[4,20,8,256]{3,2,1,0:T(8,128)(2,1)S(1)} collective-permute-done((bf16[4,20,8,256]{3,2,1,0:T(8,128)(2,1)S(1)}, bf16[4,20,8,256]{3,2,1,0:T(8,128)(2,1)S(1)}, u32[]{:S(2)}, u32[]{:S(2)}) %collective-permute-start.6) | collective-permute-done | bytes 327712 | tf_op jit(solution)/shard_map/ppermute | solution.py:403
  21.6 0.1 relay.1
  21.7 0.1 collective-permute-start.8
  21.8 1.6 %collective-permute-start.9 = (bf16[12,4,8,256]{3,2,1,0:T(8,128)(2,1)S(1)}, bf16[12,4,8,256]{3,2,1,0:T(8,128)(2,1)S(1)}, u32[]{:S(2)}, u32[]{:S(2)}) collective-permute-start(bf16[12,4,8,256]{3,2,1,0:T(8,128)(2,1)S(1)} %get-tuple-element.56), channel_id=1, source_target_pairs={{0,4},{1,2},{2,1},{3,7},{4,0},{5,6},{6,5},{7,3},{8,12},{9,10},{10,... | collective-permute-start | bytes 589832 | tf_op jit(solution)/shard_map/ppermute | solution.py:403
  23.4 0.9 %collective-permute-start.10 = (bf16[4,4,8,256]{3,2,1,0:T(8,128)(2,1)S(1)}, bf16[4,4,8,256]{3,2,1,0:T(8,128)(2,1)S(1)}, u32[]{:S(2)}, u32[]{:S(2)}) collective-permute-start(bf16[4,4,8,256]{3,2,1,0:T(8,128)(2,1)S(1)} %get-tuple-element.59), channel_id=1, source_target_pairs={{0,29},{1,28},{2,31},{3,30},{4,9},{5,8},{6,11},{7,10},{8,5},{9,4},... | collective-permute-start | bytes 196616 | tf_op jit(solution)/shard_map/ppermute | solution.py:403
  24.3 2.6 %collective-permute-start.11 = (bf16[4,4,8,256]{3,2,1,0:T(8,128)(2,1)S(1)}, bf16[4,4,8,256]{3,2,1,0:T(8,128)(2,1)S(1)}, u32[]{:S(2)}, u32[]{:S(2)}) collective-permute-start(bf16[4,4,8,256]{3,2,1,0:T(8,128)(2,1)S(1)} %get-tuple-element.60), channel_id=1, source_target_pairs={{0,4},{1,30},{2,29},{3,7},{4,0},{5,10},{6,9},{7,3},{8,12},{9,6},{1... | collective-permute-start | bytes 196616 | tf_op jit(solution)/shard_map/ppermute | solution.py:403
  27.0 0.8 %collective-permute-done.7.xb_ref = bf16[4,12,8,256]{3,2,1,0:T(8,128)(2,1)S(1)} collective-permute-done((bf16[4,12,8,256]{3,2,1,0:T(8,128)(2,1)S(1)}, bf16[4,12,8,256]{3,2,1,0:T(8,128)(2,1)S(1)}, u32[]{:S(2)}, u32[]{:S(2)}) %collective-permute-start.7) | collective-permute-done | bytes 196640 | tf_op jit(solution)/shard_map/ppermute | solution.py:403
  27.8 1.7 %collective-permute-done.8.za_ref = bf16[12,4,8,256]{3,2,1,0:T(8,128)(2,1)S(1)} collective-permute-done((bf16[12,4,8,256]{3,2,1,0:T(8,128)(2,1)S(1)}, bf16[12,4,8,256]{3,2,1,0:T(8,128)(2,1)S(1)}, u32[]{:S(2)}, u32[]{:S(2)}) %collective-permute-start.8) | collective-permute-done | bytes 196640 | tf_op jit(solution)/shard_map/ppermute | solution.py:403
  29.5 0.1 collective-permute-done.9.zb_ref
  29.6 0.6 %gather.1 = (f32[12,12,8,256]{3,2,1,0:T(8,128)S(1)}, f32[12,12,8,128]{3,2,1,0:T(8,128)S(1)}) custom-call(f32[2,21,20,8,128]{4,3,2,1,0:T(8,128)S(1)} %get-tuple-element.51.acc_ref, f32[12,8,12]{2,1,0:T(8,128)S(1)} %get-tuple-element.52.scale_ref, bf16[4,20,8,256]{3,2,1,0:T(8,128)(2,1)S(1)} %collective-permute-done.6.xa_ref, ...), custom_call_target="tpu_custom_call" | custom-call | flops 4000000000 | bytes 40000000 | tf_op jit(solution)/shard_map/gather/pallas_call | solution.py:529
  30.2 1.7 %collective-permute-done.10.da_ref = bf16[4,4,8,256]{3,2,1,0:T(8,128)(2,1)S(1)} collective-permute-done((bf16[4,4,8,256]{3,2,1,0:T(8,128)(2,1)S(1)}, bf16[4,4,8,256]{3,2,1,0:T(8,128)(2,1)S(1)}, u32[]{:S(2)}, u32[]{:S(2)}) %collective-permute-start.10) | collective-permute-done | bytes 65568 | tf_op jit(solution)/shard_map/ppermute | solution.py:403
  31.9 0.1 collective-permute-done.11.db_ref
  32.0 0.9 %finish.1 = bf16[12,12,8,256]{3,2,1,0:T(8,128)(2,1)} custom-call(f32[12,12,8,256]{3,2,1,0:T(8,128)S(1)} %get-tuple-element.57.base_ref, f32[12,12,8,128]{3,2,1,0:T(8,128)S(1)} %get-tuple-element.58.wide_ref, bf16[4,4,8,256]{3,2,1,0:T(8,128)(2,1)S(1)} %collective-permute-done.10.da_ref, bf16[4,4,8,256]{3,2,1,0:T(8,128)(2,1)S(1)} %collective-permute-done.11.db_ref), custom_call_target="tpu_custom_call" | custom-call | flops 1000 | bytes 1000 | tf_op jit(solution)/shard_map/finish/pallas_call | solution.py:538
  (10 shorter events, 0.0 us)
Async XLA Ops:
  0.0 13.5 %copy-start = (bf16[3,3,128,256]{3,2,1,0:T(8,128)(2,1)S(1)}, bf16[3,3,128,256]{3,2,1,0:T(8,128)(2,1)}, u32[]{:S(2)}) copy-start(bf16[3,3,128,256]{3,2,1,0:T(8,128)(2,1)} %refs_1_.1) | copy-start | bytes 1769476
  1.4 12.0 %collective-permute-start = (bf16[3,128,256]{2,1,0:T(8,128)(2,1)S(1)}, bf16[3,128,256]{2,1,0:T(8,128)(2,1)S(1)}, u32[]{:S(2)}, u32[]{:S(2)}) collective-permute-start(bf16[3,128,256]{2,1,0:T(8,128)(2,1)S(1)} %get-tuple-element.34), channel_id=1, source_target_pairs={{0,28},{1,29},{2,30},{3,31},{4,8},{5,9},{6,10},{7,11},{8,4},{9,5},... | collective-permute-start | bytes 589832 | tf_op jit(solution)/shard_map/ppermute | solution.py:403
  3.4 10.0 %collective-permute-start.1 = (bf16[3,128,256]{2,1,0:T(8,128)(2,1)S(1)}, bf16[3,128,256]{2,1,0:T(8,128)(2,1)S(1)}, u32[]{:S(2)}, u32[]{:S(2)}) collective-permute-start(bf16[3,128,256]{2,1,0:T(8,128)(2,1)S(1)} %get-tuple-element.35), channel_id=1, source_target_pairs={{0,4},{1,2},{2,1},{3,7},{4,0},{5,6},{6,5},{7,3},{8,12},{9,10},{10,... | collective-permute-start | bytes 589832 | tf_op jit(solution)/shard_map/ppermute | solution.py:403
  5.0 8.5 %collective-permute-start.2 = (bf16[3,128,256]{2,1,0:T(8,128)(2,1)S(1)}, bf16[3,128,256]{2,1,0:T(8,128)(2,1)S(1)}, u32[]{:S(2)}, u32[]{:S(2)}) collective-permute-start(bf16[3,128,256]{2,1,0:T(8,128)(2,1)S(1)} %get-tuple-element.36), channel_id=1, source_target_pairs={{0,1},{1,0},{2,3},{3,2},{4,5},{5,4},{6,7},{7,6},{8,9},{9,8},{10,11... | collective-permute-start | bytes 589832 | tf_op jit(solution)/shard_map/ppermute | solution.py:403
  5.0 11.1 %collective-permute-start.4 = (bf16[128,256]{1,0:T(8,128)(2,1)S(1)}, bf16[128,256]{1,0:T(8,128)(2,1)S(1)}, u32[]{:S(2)}, u32[]{:S(2)}) collective-permute-start(bf16[128,256]{1,0:T(8,128)(2,1)S(1)} %get-tuple-element.45), channel_id=1, source_target_pairs={{0,29},{1,28},{2,31},{3,30},{4,9},{5,8},{6,11},{7,10},{8,5},{9,4},... | collective-permute-start | bytes 196616 | tf_op jit(solution)/shard_map/ppermute | solution.py:403
  6.6 9.4 %collective-permute-start.5 = (bf16[128,256]{1,0:T(8,128)(2,1)S(1)}, bf16[128,256]{1,0:T(8,128)(2,1)S(1)}, u32[]{:S(2)}, u32[]{:S(2)}) collective-permute-start(bf16[128,256]{1,0:T(8,128)(2,1)S(1)} %get-tuple-element.46), channel_id=1, source_target_pairs={{0,4},{1,30},{2,29},{3,7},{4,0},{5,10},{6,9},{7,3},{8,12},{9,6},{1... | collective-permute-start | bytes 196616 | tf_op jit(solution)/shard_map/ppermute | solution.py:403
  13.5 2.6 %collective-permute-start.3 = (bf16[5,128,256]{2,1,0:T(8,128)(2,1)S(1)}, bf16[5,128,256]{2,1,0:T(8,128)(2,1)S(1)}, u32[]{:S(2)}, u32[]{:S(2)}) collective-permute-start(bf16[5,128,256]{2,1,0:T(8,128)(2,1)S(1)} %extend.1), channel_id=1, source_target_pairs={{0,4},{1,5},{2,6},{3,7},{4,0},{5,1},{6,2},{7,3},{8,12},{9,13},{10,... | collective-permute-start | bytes 983048 | tf_op jit(solution)/shard_map/ppermute | solution.py:403
  19.8 1.8 %collective-permute-start.6 = (bf16[4,20,8,256]{3,2,1,0:T(8,128)(2,1)S(1)}, bf16[4,20,8,256]{3,2,1,0:T(8,128)(2,1)S(1)}, u32[]{:S(2)}, u32[]{:S(2)}) collective-permute-start(bf16[4,20,8,256]{3,2,1,0:T(8,128)(2,1)S(1)} %get-tuple-element.53), channel_id=1, source_target_pairs={{0,4},{1,5},{2,6},{3,7},{4,0},{5,1},{6,2},{7,3},{8,12},{9,13},{10,... | collective-permute-start | bytes 983048 | tf_op jit(solution)/shard_map/ppermute | solution.py:403
  20.3 7.4 %collective-permute-start.7 = (bf16[4,12,8,256]{3,2,1,0:T(8,128)(2,1)S(1)}, bf16[4,12,8,256]{3,2,1,0:T(8,128)(2,1)S(1)}, u32[]{:S(2)}, u32[]{:S(2)}) collective-permute-start(bf16[4,12,8,256]{3,2,1,0:T(8,128)(2,1)S(1)} %get-tuple-element.54), channel_id=1, source_target_pairs={{0,28},{1,29},{2,30},{3,31},{4,8},{5,9},{6,10},{7,11},{8,4},{9,5},... | collective-permute-start | bytes 589832 | tf_op jit(solution)/shard_map/ppermute | solution.py:403
  21.7 7.8 %collective-permute-start.8 = (bf16[12,4,8,256]{3,2,1,0:T(8,128)(2,1)S(1)}, bf16[12,4,8,256]{3,2,1,0:T(8,128)(2,1)S(1)}, u32[]{:S(2)}, u32[]{:S(2)}) collective-permute-start(bf16[12,4,8,256]{3,2,1,0:T(8,128)(2,1)S(1)} %get-tuple-element.55), channel_id=1, source_target_pairs={{0,1},{1,0},{2,3},{3,2},{4,5},{5,4},{6,7},{7,6},{8,9},{9,8},{10,11... | collective-permute-start | bytes 589832 | tf_op jit(solution)/shard_map/ppermute | solution.py:403
  21.8 7.8 %collective-permute-start.9 = (bf16[12,4,8,256]{3,2,1,0:T(8,128)(2,1)S(1)}, bf16[12,4,8,256]{3,2,1,0:T(8,128)(2,1)S(1)}, u32[]{:S(2)}, u32[]{:S(2)}) collective-permute-start(bf16[12,4,8,256]{3,2,1,0:T(8,128)(2,1)S(1)} %get-tuple-element.56), channel_id=1, source_target_pairs={{0,4},{1,2},{2,1},{3,7},{4,0},{5,6},{6,5},{7,3},{8,12},{9,10},{10,... | collective-permute-start | bytes 589832 | tf_op jit(solution)/shard_map/ppermute | solution.py:403
  23.4 8.5 %collective-permute-start.10 = (bf16[4,4,8,256]{3,2,1,0:T(8,128)(2,1)S(1)}, bf16[4,4,8,256]{3,2,1,0:T(8,128)(2,1)S(1)}, u32[]{:S(2)}, u32[]{:S(2)}) collective-permute-start(bf16[4,4,8,256]{3,2,1,0:T(8,128)(2,1)S(1)} %get-tuple-element.59), channel_id=1, source_target_pairs={{0,29},{1,28},{2,31},{3,30},{4,9},{5,8},{6,11},{7,10},{8,5},{9,4},... | collective-permute-start | bytes 196616 | tf_op jit(solution)/shard_map/ppermute | solution.py:403
  24.3 7.7 %collective-permute-start.11 = (bf16[4,4,8,256]{3,2,1,0:T(8,128)(2,1)S(1)}, bf16[4,4,8,256]{3,2,1,0:T(8,128)(2,1)S(1)}, u32[]{:S(2)}, u32[]{:S(2)}) collective-permute-start(bf16[4,4,8,256]{3,2,1,0:T(8,128)(2,1)S(1)} %get-tuple-element.60), channel_id=1, source_target_pairs={{0,4},{1,30},{2,29},{3,7},{4,0},{5,10},{6,9},{7,3},{8,12},{9,6},{1... | collective-permute-start | bytes 196616 | tf_op jit(solution)/shard_map/ppermute | solution.py:403

commit v5 on v4

--- a/solution.py
+++ b/solution.py
@@ -370,17 +370,25 @@
             out_ref[spot + (slice(None), part)] = out_ref[spot + (slice(None), part)] + got * wide_ref[spot]
 
 
-def finish_kernel(base_ref, wide_ref, da_ref, db_ref, out_ref):
+def finish_kernel(base_ref, wide_ref, da_ref, db_ref, out_ref, done, sems):
     cx, cy, depth, fields = base_ref.shape
     odd_x, odd_y = parity()
-    back = pl.ds(odd_x * (cx - REACH), REACH)
-    for f in range(0, fields, 128):
-        part = slice(f, f + 128)
-        out_ref[:, :, :, part] = base_ref[:, :, :, part].astype(out_ref.dtype)
-        for d_ref, s in ((da_ref, (1 - odd_y) * (cy - REACH)), (db_ref, odd_y * (cy - REACH))):
-            spot = (back, pl.ds(s, REACH))
-            got = d_ref[:, :, :, part].astype(jnp.float32) * wide_ref[spot]
-            out_ref[spot + (slice(None), part)] = (base_ref[spot + (slice(None), part)] + got).astype(out_ref.dtype)
+    far, back = pl.ds((1 - odd_x) * (cx - REACH), REACH), pl.ds(odd_x * (cx - REACH), REACH)
+    copies = []
+    for index, rows in enumerate((pl.ds(REACH, cx - 2 * REACH), far, back)):
+        done[rows] = base_ref[rows].astype(done.dtype)
+        if index == 2:
+            for f in range(0, fields, 128):
+                part = slice(f, f + 128)
+                for d_ref, s in ((da_ref, (1 - odd_y) * (cy - REACH)), (db_ref, odd_y * (cy - REACH))):
+                    spot = (back, pl.ds(s, REACH))
+                    got = d_ref[:, :, :, part].astype(jnp.float32) * wide_ref[spot]
+                    done[spot + (slice(None), part)] = (base_ref[spot + (slice(None), part)] + got).astype(done.dtype)
+        copy = pltpu.make_async_copy(done.at[rows], out_ref.at[rows], sems.at[index])
+        copy.start()
+        copies.append(copy)
+    for copy in copies:
+        copy.wait()
 
 
 def params(megabytes):
@@ -539,7 +547,8 @@
         finish_kernel,
         out_shape=block(cx, cy),
         in_specs=[VMEM] * 4,
-        out_specs=VMEM,
+        out_specs=pl.BlockSpec(memory_space=pl.ANY),
+        scratch_shapes=[pltpu.VMEM((cx, cy, depth, fields), kind), pltpu.SemaphoreType.DMA((3,))],
         compiler_params=params(12),
         cost_estimate=SMALL,
         name="finish",

time: 33.1 us -> 33.1 us (level)
  no operation moved by 1% of the time
where the time goes in v5:
time: 33.1 us; the launch traced here: 32.9 us
  Pallas kernels  13.6 us (41%)
  starting transfers between devices  13.6 us (41%)
  waiting for transfers between devices  5.55 us (17%)
    ppermute x12, starting transfers between devices, send(): lax.ppermute(block, ('gx', 'gy'), routes(across, along, turn_x, turn_y))  13.6 us
    ppermute x12, waiting for transfers between devices, send(): lax.ppermute(block, ('gx', 'gy'), routes(across, along, turn_x, turn_y))  5.55 us
    pallas_call x1, Pallas kernels, local(): pl.pallas_call(lambda *refs: prepare_kernel((sx, sy), subregion, (cx, cy)...  4.44 us
    pallas_call x1, Pallas kernels, local(): pl.pallas_call(lambda *refs: blend_kernel((sx, sy), (cx, cy), *refs), out...  3.73 us
    pallas_call x1, Pallas kernels, local(): pl.pallas_call(lambda *refs: sample_kernel((cx, cy), *refs), out_shape=sh...  2.46 us
    pallas_call x1, Pallas kernels, local(): pl.pallas_call(lambda *refs: pack_kernel(len(plain), *refs), out_shape=(l...  1.41 us
    pallas_call x1, Pallas kernels, local(): pl.pallas_call(finish_kernel, out_shape=block(cx, cy), in_specs=[VMEM] *...  0.85 us
  transfers between devices with their start and end apart: 12, of which 6 were waited for; matrix products, arithmetic and copies ran while one was open for 0% of the time, Pallas kernels for 23%

profile of v5, /device:TPU:8, one launch (start us, length us, event | category | flops | bytes accessed | tf_op | source)
XLA Modules:
  0.0 32.9 jit_solution(17568486229397924820)
XLA Ops:
  0.0 1.4 %pack.1 = (bf16[3,128,256]{2,1,0:T(8,128)(2,1)S(1)}, bf16[3,128,256]{2,1,0:T(8,128)(2,1)S(1)}, bf16[3,128,256]{2,1,0:T(8,128)(2,1)S(1)}, bf16[3,128,256]{2,1,0:T...) custom-call(bf16[3,3,128,256]{3,2,1,0:T(8,128)(2,1)} %refs_1_.1, ...), custom_call_target="tpu_custom_call" | custom-call | flops 1000 | bytes 1000 | tf_op jit(solution)/shard_map/pack/pallas_call | solution.py:431
  1.4 2.0 %collective-permute-start = (bf16[3,128,256]{2,1,0:T(8,128)(2,1)S(1)}, bf16[3,128,256]{2,1,0:T(8,128)(2,1)S(1)}, u32[]{:S(2)}, u32[]{:S(2)}) collective-permute-start(bf16[3,128,256]{2,1,0:T(8,128)(2,1)S(1)} %get-tuple-element.34), channel_id=1, source_target_pairs={{0,28},{1,29},{2,30},{3,31},{4,8},{5,9},{6,10},{7,11},{8,4},{9,5},... | collective-permute-start | bytes 589832 | tf_op jit(solution)/shard_map/ppermute | solution.py:411
  3.4 1.6 %collective-permute-start.1 = (bf16[3,128,256]{2,1,0:T(8,128)(2,1)S(1)}, bf16[3,128,256]{2,1,0:T(8,128)(2,1)S(1)}, u32[]{:S(2)}, u32[]{:S(2)}) collective-permute-start(bf16[3,128,256]{2,1,0:T(8,128)(2,1)S(1)} %get-tuple-element.35), channel_id=1, source_target_pairs={{0,4},{1,2},{2,1},{3,7},{4,0},{5,6},{6,5},{7,3},{8,12},{9,10},{10,... | collective-permute-start | bytes 589832 | tf_op jit(solution)/shard_map/ppermute | solution.py:411
  5.0 1.7 %collective-permute-start.4 = (bf16[128,256]{1,0:T(8,128)(2,1)S(1)}, bf16[128,256]{1,0:T(8,128)(2,1)S(1)}, u32[]{:S(2)}, u32[]{:S(2)}) collective-permute-start(bf16[128,256]{1,0:T(8,128)(2,1)S(1)} %get-tuple-element.45), channel_id=1, source_target_pairs={{0,29},{1,28},{2,31},{3,30},{4,9},{5,8},{6,11},{7,10},{8,5},{9,4},... | collective-permute-start | bytes 196616 | tf_op jit(solution)/shard_map/ppermute | solution.py:411
  6.6 2.3 %collective-permute-start.5 = (bf16[128,256]{1,0:T(8,128)(2,1)S(1)}, bf16[128,256]{1,0:T(8,128)(2,1)S(1)}, u32[]{:S(2)}, u32[]{:S(2)}) collective-permute-start(bf16[128,256]{1,0:T(8,128)(2,1)S(1)} %get-tuple-element.46), channel_id=1, source_target_pairs={{0,4},{1,30},{2,29},{3,7},{4,0},{5,10},{6,9},{7,3},{8,12},{9,6},{1... | collective-permute-start | bytes 196616 | tf_op jit(solution)/shard_map/ppermute | solution.py:411
  8.9 4.4 %prepare.1 = (bf16[8,336,384]{2,1,0:T(8,128)(2,1)S(1)}, bf16[8,304,1152]{2,1,0:T(8,128)(2,1)S(1)}, bf16[8,320,304]{2,1,0:T(8,128)(2,1)S(1)}) custom-call(f32[1,8]{1,0:T(1,128)S(1)} %get-tuple-element.37.refs_0_, f32[3,8,300]{2,1,0:T(8,128)S(1)} %get-tuple-element.38.refs_1_, s32[3,1,8]{2,1,0:T(1,128)S(1)} %get-tuple-element.33.refs_2_.refs_0_, ...), custom_call_target="tpu_custom_call" | custom-call | flops 1000 | bytes 1000 | tf_op jit(solution)/shard_map/prepare/pallas_call | solution.py:450
  13.5 0.1 collective-permute-start.3
  13.6 2.5 %sample.1.refs_4_ = bf16[8,304,256]{2,1,0:T(8,128)(2,1)S(1)} custom-call(s32[3,1,8]{2,1,0:T(1,128)S(1)} %get-tuple-element.33.refs_2_.refs_0_, bf16[3,3,128,256]{3,2,1,0:T(8,128)(2,1)S(1)} %copy-done, bf16[3,128,256]{2,1,0:T(8,128)(2,1)S(1)} %collective-permute-done.refs_2_, bf16[3,128,256]{2,1,0:T(8,128)(2,1)S(1)} %collective-permute-done.2.ya_ref.refs_3_, ...), custom_call_target="tpu_custom_call" | custom-call | flops 4000000000 | bytes 40000000 | tf_op jit(solution)/shard_map/sample/pallas_call | solution.py:488
  16.0 3.7 %blend.1 = (f32[2,21,20,8,128]{4,3,2,1,0:T(8,128)S(1)}, bf16[4,20,8,256]{3,2,1,0:T(8,128)(2,1)S(1)}, bf16[4,12,8,256]{3,2,1,0:T(8,128)(2,1)S(1)}, bf16[4,4,8,256...) custom-call(s32[3,1,8]{2,1,0:T(1,128)S(1)} %get-tuple-element.33.refs_2_.refs_0_, ...), custom_call_target="tpu_custom_call" | custom-call | flops 1000 | bytes 1000 | tf_op jit(solution)/shard_map/blend/pallas_call | solution.py:500
  19.8 0.6 %collective-permute-start.6 = (bf16[4,20,8,256]{3,2,1,0:T(8,128)(2,1)S(1)}, bf16[4,20,8,256]{3,2,1,0:T(8,128)(2,1)S(1)}, u32[]{:S(2)}, u32[]{:S(2)}) collective-permute-start(bf16[4,20,8,256]{3,2,1,0:T(8,128)(2,1)S(1)} %get-tuple-element.53), channel_id=1, source_target_pairs={{0,4},{1,5},{2,6},{3,7},{4,0},{5,1},{6,2},{7,3},{8,12},{9,13},{10,... | collective-permute-start | bytes 983048 | tf_op jit(solution)/shard_map/ppermute | solution.py:411
  20.4 0.2 collective-permute-start.7
  20.6 1.1 %collective-permute-done.6.xa_ref = bf16[4,20,8,256]{3,2,1,0:T(8,128)(2,1)S(1)} collective-permute-done((bf16[4,20,8,256]{3,2,1,0:T(8,128)(2,1)S(1)}, bf16[4,20,8,256]{3,2,1,0:T(8,128)(2,1)S(1)}, u32[]{:S(2)}, u32[]{:S(2)}) %collective-permute-start.6) | collective-permute-done | bytes 327712 | tf_op jit(solution)/shard_map/ppermute | solution.py:411
  21.6 0.1 relay.1
  21.7 0.1 collective-permute-start.8
  21.8 1.6 %collective-permute-start.9 = (bf16[12,4,8,256]{3,2,1,0:T(8,128)(2,1)S(1)}, bf16[12,4,8,256]{3,2,1,0:T(8,128)(2,1)S(1)}, u32[]{:S(2)}, u32[]{:S(2)}) collective-permute-start(bf16[12,4,8,256]{3,2,1,0:T(8,128)(2,1)S(1)} %get-tuple-element.56), channel_id=1, source_target_pairs={{0,4},{1,2},{2,1},{3,7},{4,0},{5,6},{6,5},{7,3},{8,12},{9,10},{10,... | collective-permute-start | bytes 589832 | tf_op jit(solution)/shard_map/ppermute | solution.py:411
  23.4 1.0 %collective-permute-start.10 = (bf16[4,4,8,256]{3,2,1,0:T(8,128)(2,1)S(1)}, bf16[4,4,8,256]{3,2,1,0:T(8,128)(2,1)S(1)}, u32[]{:S(2)}, u32[]{:S(2)}) collective-permute-start(bf16[4,4,8,256]{3,2,1,0:T(8,128)(2,1)S(1)} %get-tuple-element.59), channel_id=1, source_target_pairs={{0,29},{1,28},{2,31},{3,30},{4,9},{5,8},{6,11},{7,10},{8,5},{9,4},... | collective-permute-start | bytes 196616 | tf_op jit(solution)/shard_map/ppermute | solution.py:411
  24.4 2.6 %collective-permute-start.11 = (bf16[4,4,8,256]{3,2,1,0:T(8,128)(2,1)S(1)}, bf16[4,4,8,256]{3,2,1,0:T(8,128)(2,1)S(1)}, u32[]{:S(2)}, u32[]{:S(2)}) collective-permute-start(bf16[4,4,8,256]{3,2,1,0:T(8,128)(2,1)S(1)} %get-tuple-element.60), channel_id=1, source_target_pairs={{0,4},{1,30},{2,29},{3,7},{4,0},{5,10},{6,9},{7,3},{8,12},{9,6},{1... | collective-permute-start | bytes 196616 | tf_op jit(solution)/shard_map/ppermute | solution.py:411
  26.9 0.8 %collective-permute-done.7.xb_ref = bf16[4,12,8,256]{3,2,1,0:T(8,128)(2,1)S(1)} collective-permute-done((bf16[4,12,8,256]{3,2,1,0:T(8,128)(2,1)S(1)}, bf16[4,12,8,256]{3,2,1,0:T(8,128)(2,1)S(1)}, u32[]{:S(2)}, u32[]{:S(2)}) %collective-permute-start.7) | collective-permute-done | bytes 196640 | tf_op jit(solution)/shard_map/ppermute | solution.py:411
  27.8 1.8 %collective-permute-done.8.za_ref = bf16[12,4,8,256]{3,2,1,0:T(8,128)(2,1)S(1)} collective-permute-done((bf16[12,4,8,256]{3,2,1,0:T(8,128)(2,1)S(1)}, bf16[12,4,8,256]{3,2,1,0:T(8,128)(2,1)S(1)}, u32[]{:S(2)}, u32[]{:S(2)}) %collective-permute-start.8) | collective-permute-done | bytes 196640 | tf_op jit(solution)/shard_map/ppermute | solution.py:411
  29.5 0.1 collective-permute-done.9.zb_ref
  29.6 0.6 %gather.1 = (f32[12,12,8,256]{3,2,1,0:T(8,128)S(1)}, f32[12,12,8,128]{3,2,1,0:T(8,128)S(1)}) custom-call(f32[2,21,20,8,128]{4,3,2,1,0:T(8,128)S(1)} %get-tuple-element.51.acc_ref, f32[12,8,12]{2,1,0:T(8,128)S(1)} %get-tuple-element.52.scale_ref, bf16[4,20,8,256]{3,2,1,0:T(8,128)(2,1)S(1)} %collective-permute-done.6.xa_ref, ...), custom_call_target="tpu_custom_call" | custom-call | flops 4000000000 | bytes 40000000 | tf_op jit(solution)/shard_map/gather/pallas_call | solution.py:537
  30.2 1.8 %collective-permute-done.10.da_ref = bf16[4,4,8,256]{3,2,1,0:T(8,128)(2,1)S(1)} collective-permute-done((bf16[4,4,8,256]{3,2,1,0:T(8,128)(2,1)S(1)}, bf16[4,4,8,256]{3,2,1,0:T(8,128)(2,1)S(1)}, u32[]{:S(2)}, u32[]{:S(2)}) %collective-permute-start.10) | collective-permute-done | bytes 65568 | tf_op jit(solution)/shard_map/ppermute | solution.py:411
  32.0 0.1 collective-permute-done.11.db_ref
  32.0 0.9 %finish.1 = bf16[12,12,8,256]{3,2,1,0:T(8,128)(2,1)} custom-call(f32[12,12,8,256]{3,2,1,0:T(8,128)S(1)} %get-tuple-element.57.base_ref, f32[12,12,8,128]{3,2,1,0:T(8,128)S(1)} %get-tuple-element.58.wide_ref, bf16[4,4,8,256]{3,2,1,0:T(8,128)(2,1)S(1)} %collective-permute-done.10.da_ref, bf16[4,4,8,256]{3,2,1,0:T(8,128)(2,1)S(1)} %collective-permute-done.11.db_ref), custom_call_target="tpu_custom_call" | custom-call | flops 1000 | bytes 1000 | tf_op jit(solution)/shard_map/finish/pallas_call | solution.py:546
  (10 shorter events, 0.0 us)
Async XLA Ops:
  0.0 13.5 %copy-start = (bf16[3,3,128,256]{3,2,1,0:T(8,128)(2,1)S(1)}, bf16[3,3,128,256]{3,2,1,0:T(8,128)(2,1)}, u32[]{:S(2)}) copy-start(bf16[3,3,128,256]{3,2,1,0:T(8,128)(2,1)} %refs_1_.1) | copy-start | bytes 1769476
  1.4 12.0 %collective-permute-start = (bf16[3,128,256]{2,1,0:T(8,128)(2,1)S(1)}, bf16[3,128,256]{2,1,0:T(8,128)(2,1)S(1)}, u32[]{:S(2)}, u32[]{:S(2)}) collective-permute-start(bf16[3,128,256]{2,1,0:T(8,128)(2,1)S(1)} %get-tuple-element.34), channel_id=1, source_target_pairs={{0,28},{1,29},{2,30},{3,31},{4,8},{5,9},{6,10},{7,11},{8,4},{9,5},... | collective-permute-start | bytes 589832 | tf_op jit(solution)/shard_map/ppermute | solution.py:411
  3.4 10.0 %collective-permute-start.1 = (bf16[3,128,256]{2,1,0:T(8,128)(2,1)S(1)}, bf16[3,128,256]{2,1,0:T(8,128)(2,1)S(1)}, u32[]{:S(2)}, u32[]{:S(2)}) collective-permute-start(bf16[3,128,256]{2,1,0:T(8,128)(2,1)S(1)} %get-tuple-element.35), channel_id=1, source_target_pairs={{0,4},{1,2},{2,1},{3,7},{4,0},{5,6},{6,5},{7,3},{8,12},{9,10},{10,... | collective-permute-start | bytes 589832 | tf_op jit(solution)/shard_map/ppermute | solution.py:411
  5.0 8.5 %collective-permute-start.2 = (bf16[3,128,256]{2,1,0:T(8,128)(2,1)S(1)}, bf16[3,128,256]{2,1,0:T(8,128)(2,1)S(1)}, u32[]{:S(2)}, u32[]{:S(2)}) collective-permute-start(bf16[3,128,256]{2,1,0:T(8,128)(2,1)S(1)} %get-tuple-element.36), channel_id=1, source_target_pairs={{0,1},{1,0},{2,3},{3,2},{4,5},{5,4},{6,7},{7,6},{8,9},{9,8},{10,11... | collective-permute-start | bytes 589832 | tf_op jit(solution)/shard_map/ppermute | solution.py:411
  5.0 11.1 %collective-permute-start.4 = (bf16[128,256]{1,0:T(8,128)(2,1)S(1)}, bf16[128,256]{1,0:T(8,128)(2,1)S(1)}, u32[]{:S(2)}, u32[]{:S(2)}) collective-permute-start(bf16[128,256]{1,0:T(8,128)(2,1)S(1)} %get-tuple-element.45), channel_id=1, source_target_pairs={{0,29},{1,28},{2,31},{3,30},{4,9},{5,8},{6,11},{7,10},{8,5},{9,4},... | collective-permute-start | bytes 196616 | tf_op jit(solution)/shard_map/ppermute | solution.py:411
  6.6 9.4 %collective-permute-start.5 = (bf16[128,256]{1,0:T(8,128)(2,1)S(1)}, bf16[128,256]{1,0:T(8,128)(2,1)S(1)}, u32[]{:S(2)}, u32[]{:S(2)}) collective-permute-start(bf16[128,256]{1,0:T(8,128)(2,1)S(1)} %get-tuple-element.46), channel_id=1, source_target_pairs={{0,4},{1,30},{2,29},{3,7},{4,0},{5,10},{6,9},{7,3},{8,12},{9,6},{1... | collective-permute-start | bytes 196616 | tf_op jit(solution)/shard_map/ppermute | solution.py:411
  13.5 2.6 %collective-permute-start.3 = (bf16[5,128,256]{2,1,0:T(8,128)(2,1)S(1)}, bf16[5,128,256]{2,1,0:T(8,128)(2,1)S(1)}, u32[]{:S(2)}, u32[]{:S(2)}) collective-permute-start(bf16[5,128,256]{2,1,0:T(8,128)(2,1)S(1)} %extend.1), channel_id=1, source_target_pairs={{0,4},{1,5},{2,6},{3,7},{4,0},{5,1},{6,2},{7,3},{8,12},{9,13},{10,... | collective-permute-start | bytes 983048 | tf_op jit(solution)/shard_map/ppermute | solution.py:411
  19.8 1.8 %collective-permute-start.6 = (bf16[4,20,8,256]{3,2,1,0:T(8,128)(2,1)S(1)}, bf16[4,20,8,256]{3,2,1,0:T(8,128)(2,1)S(1)}, u32[]{:S(2)}, u32[]{:S(2)}) collective-permute-start(bf16[4,20,8,256]{3,2,1,0:T(8,128)(2,1)S(1)} %get-tuple-element.53), channel_id=1, source_target_pairs={{0,4},{1,5},{2,6},{3,7},{4,0},{5,1},{6,2},{7,3},{8,12},{9,13},{10,... | collective-permute-start | bytes 983048 | tf_op jit(solution)/shard_map/ppermute | solution.py:411
  20.4 7.4 %collective-permute-start.7 = (bf16[4,12,8,256]{3,2,1,0:T(8,128)(2,1)S(1)}, bf16[4,12,8,256]{3,2,1,0:T(8,128)(2,1)S(1)}, u32[]{:S(2)}, u32[]{:S(2)}) collective-permute-start(bf16[4,12,8,256]{3,2,1,0:T(8,128)(2,1)S(1)} %get-tuple-element.54), channel_id=1, source_target_pairs={{0,28},{1,29},{2,30},{3,31},{4,8},{5,9},{6,10},{7,11},{8,4},{9,5},... | collective-permute-start | bytes 589832 | tf_op jit(solution)/shard_map/ppermute | solution.py:411
  21.7 7.8 %collective-permute-start.8 = (bf16[12,4,8,256]{3,2,1,0:T(8,128)(2,1)S(1)}, bf16[12,4,8,256]{3,2,1,0:T(8,128)(2,1)S(1)}, u32[]{:S(2)}, u32[]{:S(2)}) collective-permute-start(bf16[12,4,8,256]{3,2,1,0:T(8,128)(2,1)S(1)} %get-tuple-element.55), channel_id=1, source_target_pairs={{0,1},{1,0},{2,3},{3,2},{4,5},{5,4},{6,7},{7,6},{8,9},{9,8},{10,11... | collective-permute-start | bytes 589832 | tf_op jit(solution)/shard_map/ppermute | solution.py:411
  21.8 7.8 %collective-permute-start.9 = (bf16[12,4,8,256]{3,2,1,0:T(8,128)(2,1)S(1)}, bf16[12,4,8,256]{3,2,1,0:T(8,128)(2,1)S(1)}, u32[]{:S(2)}, u32[]{:S(2)}) collective-permute-start(bf16[12,4,8,256]{3,2,1,0:T(8,128)(2,1)S(1)} %get-tuple-element.56), channel_id=1, source_target_pairs={{0,4},{1,2},{2,1},{3,7},{4,0},{5,6},{6,5},{7,3},{8,12},{9,10},{10,... | collective-permute-start | bytes 589832 | tf_op jit(solution)/shard_map/ppermute | solution.py:411
  23.4 8.6 %collective-permute-start.10 = (bf16[4,4,8,256]{3,2,1,0:T(8,128)(2,1)S(1)}, bf16[4,4,8,256]{3,2,1,0:T(8,128)(2,1)S(1)}, u32[]{:S(2)}, u32[]{:S(2)}) collective-permute-start(bf16[4,4,8,256]{3,2,1,0:T(8,128)(2,1)S(1)} %get-tuple-element.59), channel_id=1, source_target_pairs={{0,29},{1,28},{2,31},{3,30},{4,9},{5,8},{6,11},{7,10},{8,5},{9,4},... | collective-permute-start | bytes 196616 | tf_op jit(solution)/shard_map/ppermute | solution.py:411
  24.4 7.7 %collective-permute-start.11 = (bf16[4,4,8,256]{3,2,1,0:T(8,128)(2,1)S(1)}, bf16[4,4,8,256]{3,2,1,0:T(8,128)(2,1)S(1)}, u32[]{:S(2)}, u32[]{:S(2)}) collective-permute-start(bf16[4,4,8,256]{3,2,1,0:T(8,128)(2,1)S(1)} %get-tuple-element.60), channel_id=1, source_target_pairs={{0,4},{1,30},{2,29},{3,7},{4,0},{5,10},{6,9},{7,3},{8,12},{9,6},{1... | collective-permute-start | bytes 196616 | tf_op jit(solution)/shard_map/ppermute | solution.py:411
